TPU v7x, 512 devices: a whole 4x4x16 slice. The times are simulated.
512 devices in a mesh: src: 16 (over x, z_hi, core), rcv: 32 (over z_lo, y).
Axes of the slice: x: 4, y: 4, z: 16 (z_hi: 2, z_lo: 8; z = z_hi * 8 + z_lo), core: 2. Of those that a mesh axis runs over, the one named last changes fastest.
Arguments:
- source_spectra: bfloat16 [32, 8, 23, 2, 8, 4096], P('rcv', None, None, None, None, 'src'), may hold values from -6 to 6
- receiver_spectra: bfloat16 [16, 8, 23, 2, 8, 8192], P('src', None, None, None, None, 'rcv'), may hold values from -6 to 6
Outputs:
- cross_stack: bfloat16 [2, 8, 4096, 8192], P(None, None, 'src', 'rcv')
All inputs are finite; a program needn't handle non-finite values.
Results may differ from a plain program's by a relative error of at most 0.0058.
Values may be sent and summed in bfloat16 or wider, within the bound.
No kernel may reach another device: no remote copies, remote signals or barrier semaphores. Data moves between devices by JAX's collectives and lax.ppermute only.
A program may use at most 64 MiB of HBM per device.

v0:
```python
import jax
import jax.numpy as jnp
from jax import lax
from jax.sharding import PartitionSpec as P


def from_behind(block, axis, distance):
    devices = range(lax.axis_size(axis))
    route = [((i - distance) % len(devices), i) for i in devices]
    return lax.ppermute(block, axis, route)


def whiten(spectra):
    values = spectra.astype(jnp.float32)
    power_sum = jnp.sum(values * values, axis=3, keepdims=True)
    mean_level = jnp.mean(power_sum, axis=4, keepdims=True)
    return (values / jnp.sqrt(0.5 * power_sum + 0.5 * mean_level + 0.25)).astype(jnp.bfloat16)[0]


def cross_terms(source_slot, receiver_slot):
    bins_count = source_slot.shape[2]
    width = source_slot.shape[3]
    left_side = source_slot.reshape(-1, bins_count, width)
    swapped = jnp.concatenate([source_slot[:, 1:2], -source_slot[:, 0:1]], axis=1).reshape(
        -1, bins_count, width
    )
    right_side = receiver_slot.reshape(-1, bins_count, width)
    real_part = jnp.einsum(
        "kbp,kbq->bpq", left_side, right_side, preferred_element_type=jnp.float32
    )
    imag_part = jnp.einsum("kbp,kbq->bpq", swapped, right_side, preferred_element_type=jnp.float32)
    return jnp.stack([real_part, imag_part])


def body(source_spectra, receiver_spectra):
    source_white = whiten(source_spectra)
    receiver_white = whiten(receiver_spectra)
    groups = source_white.shape[0]
    windows = source_white.shape[1]
    running = cross_terms(source_white[0], receiver_white[0])
    carried = source_white
    for step_index in range(1, groups):
        carried = from_behind(carried[1:], "rcv", -1)
        source_slot = carried[0]
        receiver_slot = from_behind(receiver_white[step_index], "src", -step_index)
        running = running + cross_terms(source_slot, receiver_slot)
    return (running * (groups * windows) ** (-0.5)).astype(jnp.bfloat16)


def solution(mesh):
    return jax.shard_map(
        body,
        mesh=mesh,
        in_specs=(P("rcv", None, None, None, None, "src"), P("src", None, None, None, None, "rcv")),
        out_specs=P(None, None, "src", "rcv"),
        check_vma=False,
    )
```

profile of v0, /device:TPU:4, one launch (start us, length us, event | category | flops | bytes accessed | tf_op | source)
XLA Modules:
  0.0 251.9 jit_solution(8739288080236362648)
XLA Ops:
  0.0 2.3 fusion.8
  2.4 0.5 add_sqrt_fusion.1
  2.9 0.9 copy-done
  3.7 0.5 fusion.12
  4.3 0.1 slice_bitcast_fusion
  4.4 15.7 %collective-permute-start = (bf16[7,23,2,8,256]{4,3,2,1,0:T(8,128)(2,1)S(1)}, bf16[7,23,2,8,256]{4,3,2,1,0:T(8,128)(2,1)S(1)}, u32[]{:S(2)}, u32[]{:S(2)}) collective-permute-start(bf16[7,23,2,8,256]{4,3,2,1,0:T(8,128)(2,1)S(1)} %slice_bitcast_fusion), channel_id=1, source_target_pairs={{1,0},{2,1},{3,2},{4,3},{5,4},{6,5},{7,6},{8,7},{9,8},{10,9},{11,1... | collective-permute-start | bytes 3956744 | tf_op jit(solution)/shard_map/ppermute | solution.py:10
  20.1 0.7 fusion.10
  20.9 0.5 add_sqrt_fusion
  21.4 0.5 fusion.13
  21.9 0.1 slice_bitcast_fusion.1
  22.0 1.9 collective-permute-start.13
  24.0 10.3 %collective-permute-start.11 = (bf16[23,2,8,256]{3,2,1,0:T(8,128)(2,1)S(1)}, bf16[23,2,8,256]{3,2,1,0:T(8,128)(2,1)S(1)}, u32[]{:S(2)}, u32[]{:S(2)}) collective-permute-start(bf16[23,2,8,256]{3,2,1,0:T(8,128)(2,1)S(1)} %get-tuple-element.10), channel_id=1, source_target_pairs={{192,0},{224,32},{256,64},{288,96},{320,128},{352,160},{384,192},{... | collective-permute-start | bytes 565256 | tf_op jit(solution)/shard_map/ppermute | solution.py:10
  34.3 12.9 %collective-permute-start.9 = (bf16[23,2,8,256]{3,2,1,0:T(8,128)(2,1)S(1)}, bf16[23,2,8,256]{3,2,1,0:T(8,128)(2,1)S(1)}, u32[]{:S(2)}, u32[]{:S(2)}) collective-permute-start(bf16[23,2,8,256]{3,2,1,0:T(8,128)(2,1)S(1)} %get-tuple-element.11), channel_id=1, source_target_pairs={{160,0},{192,32},{224,64},{256,96},{288,128},{320,160},{352,192},{... | collective-permute-start | bytes 565256 | tf_op jit(solution)/shard_map/ppermute | solution.py:10
  47.3 1.9 collective-permute-start.1
  49.2 2.6 %collective-permute-done = bf16[7,23,2,8,256]{4,3,2,1,0:T(8,128)(2,1)S(1)} collective-permute-done((bf16[7,23,2,8,256]{4,3,2,1,0:T(8,128)(2,1)S(1)}, bf16[7,23,2,8,256]{4,3,2,1,0:T(8,128)(2,1)S(1)}, u32[]{:S(2)}, u32[]{:S(2)}) %collective-permute-start) | collective-permute-done | bytes 1318944 | tf_op jit(solution)/shard_map/ppermute | solution.py:10
  51.9 0.1 slice.174
  52.0 13.2 %collective-permute-start.2 = (bf16[6,23,2,8,256]{4,3,2,1,0:T(8,128)(2,1)S(1)}, bf16[6,23,2,8,256]{4,3,2,1,0:T(8,128)(2,1)S(1)}, u32[]{:S(2)}, u32[]{:S(2)}) collective-permute-start(bf16[6,23,2,8,256]{4,3,2,1,0:T(8,128)(2,1)S(1)} %slice.174), channel_id=1, source_target_pairs={{1,0},{2,1},{3,2},{4,3},{5,4},{6,5},{7,6},{8,7},{9,8},{10,9},{11,1... | collective-permute-start | bytes 3391496 | tf_op jit(solution)/shard_map/ppermute | solution.py:10
  65.3 0.5 convolution_bitcast_fusion.14
  65.8 0.5 convolution_bitcast_fusion.15
  66.4 7.4 %collective-permute-start.3 = (bf16[23,2,8,256]{3,2,1,0:T(8,128)(2,1)S(1)}, bf16[23,2,8,256]{3,2,1,0:T(8,128)(2,1)S(1)}, u32[]{:S(2)}, u32[]{:S(2)}) collective-permute-start(bf16[23,2,8,256]{3,2,1,0:T(8,128)(2,1)S(1)} %get-tuple-element.14), channel_id=1, source_target_pairs={{64,0},{96,32},{128,64},{160,96},{192,128},{224,160},{256,192},{28... | collective-permute-start | bytes 565256 | tf_op jit(solution)/shard_map/ppermute | solution.py:10
  73.7 0.5 convolution_bitcast_fusion.12
  74.2 26.7 %collective-permute-done.2 = bf16[6,23,2,8,256]{4,3,2,1,0:T(8,128)(2,1)S(1)} collective-permute-done((bf16[6,23,2,8,256]{4,3,2,1,0:T(8,128)(2,1)S(1)}, bf16[6,23,2,8,256]{4,3,2,1,0:T(8,128)(2,1)S(1)}, u32[]{:S(2)}, u32[]{:S(2)}) %collective-permute-start.2) | collective-permute-done | bytes 1130528 | tf_op jit(solution)/shard_map/ppermute | solution.py:10
  100.9 0.1 slice.179
  101.0 13.5 %collective-permute-start.4 = (bf16[5,23,2,8,256]{4,3,2,1,0:T(8,128)(2,1)S(1)}, bf16[5,23,2,8,256]{4,3,2,1,0:T(8,128)(2,1)S(1)}, u32[]{:S(2)}, u32[]{:S(2)}) collective-permute-start(bf16[5,23,2,8,256]{4,3,2,1,0:T(8,128)(2,1)S(1)} %slice.179), channel_id=1, source_target_pairs={{1,0},{2,1},{3,2},{4,3},{5,4},{6,5},{7,6},{8,7},{9,8},{10,9},{11,1... | collective-permute-start | bytes 2826248 | tf_op jit(solution)/shard_map/ppermute | solution.py:10
  114.5 0.5 convolution_bitcast_fusion.13
  115.1 1.9 collective-permute-start.5
  117.0 0.5 convolution_bitcast_fusion.10
  117.5 0.5 convolution_bitcast_fusion.11
  118.0 28.1 %collective-permute-done.4 = bf16[5,23,2,8,256]{4,3,2,1,0:T(8,128)(2,1)S(1)} collective-permute-done((bf16[5,23,2,8,256]{4,3,2,1,0:T(8,128)(2,1)S(1)}, bf16[5,23,2,8,256]{4,3,2,1,0:T(8,128)(2,1)S(1)}, u32[]{:S(2)}, u32[]{:S(2)}) %collective-permute-start.4) | collective-permute-done | bytes 942112 | tf_op jit(solution)/shard_map/ppermute | solution.py:10
  146.2 13.3 %collective-permute-start.6 = (bf16[4,23,2,8,256]{4,3,2,1,0:T(8,128)(2,1)S(1)}, bf16[4,23,2,8,256]{4,3,2,1,0:T(8,128)(2,1)S(1)}, u32[]{:S(2)}, u32[]{:S(2)}) collective-permute-start(bf16[4,23,2,8,256]{4,3,2,1,0:T(8,128)(2,1)S(1)} %slice.184), channel_id=1, source_target_pairs={{1,0},{2,1},{3,2},{4,3},{5,4},{6,5},{7,6},{8,7},{9,8},{10,9},{11,1... | collective-permute-start | bytes 2261000 | tf_op jit(solution)/shard_map/ppermute | solution.py:10
  159.7 1.9 collective-permute-start.7
  161.6 0.5 convolution_bitcast_fusion.8
  162.1 0.5 convolution_bitcast_fusion.9
  162.6 15.1 %collective-permute-done.6 = bf16[4,23,2,8,256]{4,3,2,1,0:T(8,128)(2,1)S(1)} collective-permute-done((bf16[4,23,2,8,256]{4,3,2,1,0:T(8,128)(2,1)S(1)}, bf16[4,23,2,8,256]{4,3,2,1,0:T(8,128)(2,1)S(1)}, u32[]{:S(2)}, u32[]{:S(2)}) %collective-permute-start.6) | collective-permute-done | bytes 753696 | tf_op jit(solution)/shard_map/ppermute | solution.py:10
  177.7 13.2 %collective-permute-start.8 = (bf16[3,23,2,8,256]{4,3,2,1,0:T(8,128)(2,1)S(1)}, bf16[3,23,2,8,256]{4,3,2,1,0:T(8,128)(2,1)S(1)}, u32[]{:S(2)}, u32[]{:S(2)}) collective-permute-start(bf16[3,23,2,8,256]{4,3,2,1,0:T(8,128)(2,1)S(1)} %slice.189), channel_id=1, source_target_pairs={{1,0},{2,1},{3,2},{4,3},{5,4},{6,5},{7,6},{8,7},{9,8},{10,9},{11,1... | collective-permute-start | bytes 1695752 | tf_op jit(solution)/shard_map/ppermute | solution.py:10
  191.0 0.5 convolution_bitcast_fusion.6
  191.5 1.8 convolution_bitcast_fusion.7
  193.3 9.7 %collective-permute-done.8 = bf16[3,23,2,8,256]{4,3,2,1,0:T(8,128)(2,1)S(1)} collective-permute-done((bf16[3,23,2,8,256]{4,3,2,1,0:T(8,128)(2,1)S(1)}, bf16[3,23,2,8,256]{4,3,2,1,0:T(8,128)(2,1)S(1)}, u32[]{:S(2)}, u32[]{:S(2)}) %collective-permute-start.8) | collective-permute-done | bytes 565280 | tf_op jit(solution)/shard_map/ppermute | solution.py:10
  203.1 13.1 %collective-permute-start.10 = (bf16[2,23,2,8,256]{4,3,2,1,0:T(8,128)(2,1)S(1)}, bf16[2,23,2,8,256]{4,3,2,1,0:T(8,128)(2,1)S(1)}, u32[]{:S(2)}, u32[]{:S(2)}) collective-permute-start(bf16[2,23,2,8,256]{4,3,2,1,0:T(8,128)(2,1)S(1)} %slice.194), channel_id=1, source_target_pairs={{1,0},{2,1},{3,2},{4,3},{5,4},{6,5},{7,6},{8,7},{9,8},{10,9},{11,1... | collective-permute-start | bytes 1130504 | tf_op jit(solution)/shard_map/ppermute | solution.py:10
  216.3 1.8 convolution_bitcast_fusion.4
  218.1 1.8 convolution_bitcast_fusion.5
  219.9 3.5 %collective-permute-done.10 = bf16[2,23,2,8,256]{4,3,2,1,0:T(8,128)(2,1)S(1)} collective-permute-done((bf16[2,23,2,8,256]{4,3,2,1,0:T(8,128)(2,1)S(1)}, bf16[2,23,2,8,256]{4,3,2,1,0:T(8,128)(2,1)S(1)}, u32[]{:S(2)}, u32[]{:S(2)}) %collective-permute-start.10) | collective-permute-done | bytes 376864 | tf_op jit(solution)/shard_map/ppermute | solution.py:10
  223.5 13.3 %collective-permute-start.12 = (bf16[1,23,2,8,256]{4,3,2,1,0:T(8,128)(2,1)S(1)}, bf16[1,23,2,8,256]{4,3,2,1,0:T(8,128)(2,1)S(1)}, u32[]{:S(2)}, u32[]{:S(2)}) collective-permute-start(bf16[1,23,2,8,256]{4,3,2,1,0:T(8,128)(2,1)S(1)} %get-tuple-element.29), channel_id=1, source_target_pairs={{1,0},{2,1},{3,2},{4,3},{5,4},{6,5},{7,6},{8,7},{9,8},{10,9},{11,1... | collective-permute-start | bytes 565256 | tf_op jit(solution)/shard_map/ppermute | solution.py:10
  236.8 1.9 convolution_bitcast_fusion.2
  238.7 1.9 convolution_bitcast_fusion.3
  240.7 1.8 convolution_bitcast_fusion
  242.5 1.8 convolution_bitcast_fusion.1
  244.3 7.6 %fusion.7 = bf16[2,8,256,256]{3,2,1,0:T(8,128)(2,1)} fusion(f32[1,8,256,256]{3,2,1,0:T(8,128)S(1)} %convolution_bitcast_fusion.14, f32[1,8,256,256]{3,2,1,0:T(8,128)S(1)} %convolution_bitcast_fusion.15, f32[1,8,256,256]{3,2,1,0:T(8,128)S(1)} %convolution_bitcast_fusion.12, f32[1,8,256,256]{3,2,1,0:T(8,128)S(1)} %convolution_bitcast_fusion.13, ...), kind=kLoop, calls=%fused_computation.8 | loop fusion | flops 17825792 | bytes 35651584 | tf_op jit(solution)/shard_map/convert_element_type | solution.py:47
  (39 shorter events, 0.7 us)
Async XLA Ops:
  2.3 1.4 copy-start
  4.3 15.9 %copy-start.1 = (bf16[1,8,23,2,8,256]{5,4,3,2,1,0:T(8,128)(2,1)S(1)}, bf16[1,8,23,2,8,256]{5,4,3,2,1,0:T(8,128)(2,1)}, u32[]{:S(2)}) copy-start(bf16[1,8,23,2,8,256]{5,4,3,2,1,0:T(8,128)(2,1)} %param.3) | copy-start | bytes 4521988
  4.4 47.5 %collective-permute-start = (bf16[7,23,2,8,256]{4,3,2,1,0:T(8,128)(2,1)S(1)}, bf16[7,23,2,8,256]{4,3,2,1,0:T(8,128)(2,1)S(1)}, u32[]{:S(2)}, u32[]{:S(2)}) collective-permute-start(bf16[7,23,2,8,256]{4,3,2,1,0:T(8,128)(2,1)S(1)} %slice_bitcast_fusion), channel_id=1, source_target_pairs={{1,0},{2,1},{3,2},{4,3},{5,4},{6,5},{7,6},{8,7},{9,8},{10,9},{11,1... | collective-permute-start | bytes 3956744 | tf_op jit(solution)/shard_map/ppermute | solution.py:10
  22.0 218.6 %collective-permute-start.13 = (bf16[23,2,8,256]{3,2,1,0:T(8,128)(2,1)S(1)}, bf16[23,2,8,256]{3,2,1,0:T(8,128)(2,1)S(1)}, u32[]{:S(2)}, u32[]{:S(2)}) collective-permute-start(bf16[23,2,8,256]{3,2,1,0:T(8,128)(2,1)S(1)} %get-tuple-element.9), channel_id=1, source_target_pairs={{224,0},{256,32},{288,64},{320,96},{352,128},{384,160},{416,192},{... | collective-permute-start | bytes 565256 | tf_op jit(solution)/shard_map/ppermute | solution.py:10
  24.0 212.9 %collective-permute-start.11 = (bf16[23,2,8,256]{3,2,1,0:T(8,128)(2,1)S(1)}, bf16[23,2,8,256]{3,2,1,0:T(8,128)(2,1)S(1)}, u32[]{:S(2)}, u32[]{:S(2)}) collective-permute-start(bf16[23,2,8,256]{3,2,1,0:T(8,128)(2,1)S(1)} %get-tuple-element.10), channel_id=1, source_target_pairs={{192,0},{224,32},{256,64},{288,96},{320,128},{352,160},{384,192},{... | collective-permute-start | bytes 565256 | tf_op jit(solution)/shard_map/ppermute | solution.py:10
  34.3 182.0 %collective-permute-start.9 = (bf16[23,2,8,256]{3,2,1,0:T(8,128)(2,1)S(1)}, bf16[23,2,8,256]{3,2,1,0:T(8,128)(2,1)S(1)}, u32[]{:S(2)}, u32[]{:S(2)}) collective-permute-start(bf16[23,2,8,256]{3,2,1,0:T(8,128)(2,1)S(1)} %get-tuple-element.11), channel_id=1, source_target_pairs={{160,0},{192,32},{224,64},{256,96},{288,128},{320,160},{352,192},{... | collective-permute-start | bytes 565256 | tf_op jit(solution)/shard_map/ppermute | solution.py:10
  47.3 19.1 %collective-permute-start.1 = (bf16[23,2,8,256]{3,2,1,0:T(8,128)(2,1)S(1)}, bf16[23,2,8,256]{3,2,1,0:T(8,128)(2,1)S(1)}, u32[]{:S(2)}, u32[]{:S(2)}) collective-permute-start(bf16[23,2,8,256]{3,2,1,0:T(8,128)(2,1)S(1)} %get-tuple-element.15), channel_id=1, source_target_pairs={{32,0},{64,32},{96,64},{128,96},{160,128},{192,160},{224,192},{256... | collective-permute-start | bytes 565256 | tf_op jit(solution)/shard_map/ppermute | solution.py:10
  52.0 49.0 %collective-permute-start.2 = (bf16[6,23,2,8,256]{4,3,2,1,0:T(8,128)(2,1)S(1)}, bf16[6,23,2,8,256]{4,3,2,1,0:T(8,128)(2,1)S(1)}, u32[]{:S(2)}, u32[]{:S(2)}) collective-permute-start(bf16[6,23,2,8,256]{4,3,2,1,0:T(8,128)(2,1)S(1)} %slice.174), channel_id=1, source_target_pairs={{1,0},{2,1},{3,2},{4,3},{5,4},{6,5},{7,6},{8,7},{9,8},{10,9},{11,1... | collective-permute-start | bytes 3391496 | tf_op jit(solution)/shard_map/ppermute | solution.py:10
  66.4 48.7 %collective-permute-start.3 = (bf16[23,2,8,256]{3,2,1,0:T(8,128)(2,1)S(1)}, bf16[23,2,8,256]{3,2,1,0:T(8,128)(2,1)S(1)}, u32[]{:S(2)}, u32[]{:S(2)}) collective-permute-start(bf16[23,2,8,256]{3,2,1,0:T(8,128)(2,1)S(1)} %get-tuple-element.14), channel_id=1, source_target_pairs={{64,0},{96,32},{128,64},{160,96},{192,128},{224,160},{256,192},{28... | collective-permute-start | bytes 565256 | tf_op jit(solution)/shard_map/ppermute | solution.py:10
  101.0 45.2 %collective-permute-start.4 = (bf16[5,23,2,8,256]{4,3,2,1,0:T(8,128)(2,1)S(1)}, bf16[5,23,2,8,256]{4,3,2,1,0:T(8,128)(2,1)S(1)}, u32[]{:S(2)}, u32[]{:S(2)}) collective-permute-start(bf16[5,23,2,8,256]{4,3,2,1,0:T(8,128)(2,1)S(1)} %slice.179), channel_id=1, source_target_pairs={{1,0},{2,1},{3,2},{4,3},{5,4},{6,5},{7,6},{8,7},{9,8},{10,9},{11,1... | collective-permute-start | bytes 2826248 | tf_op jit(solution)/shard_map/ppermute | solution.py:10
  115.1 44.6 %collective-permute-start.5 = (bf16[23,2,8,256]{3,2,1,0:T(8,128)(2,1)S(1)}, bf16[23,2,8,256]{3,2,1,0:T(8,128)(2,1)S(1)}, u32[]{:S(2)}, u32[]{:S(2)}) collective-permute-start(bf16[23,2,8,256]{3,2,1,0:T(8,128)(2,1)S(1)} %get-tuple-element.13), channel_id=1, source_target_pairs={{96,0},{128,32},{160,64},{192,96},{224,128},{256,160},{288,192},{3... | collective-permute-start | bytes 565256 | tf_op jit(solution)/shard_map/ppermute | solution.py:10
  146.2 31.4 %collective-permute-start.6 = (bf16[4,23,2,8,256]{4,3,2,1,0:T(8,128)(2,1)S(1)}, bf16[4,23,2,8,256]{4,3,2,1,0:T(8,128)(2,1)S(1)}, u32[]{:S(2)}, u32[]{:S(2)}) collective-permute-start(bf16[4,23,2,8,256]{4,3,2,1,0:T(8,128)(2,1)S(1)} %slice.184), channel_id=1, source_target_pairs={{1,0},{2,1},{3,2},{4,3},{5,4},{6,5},{7,6},{8,7},{9,8},{10,9},{11,1... | collective-permute-start | bytes 2261000 | tf_op jit(solution)/shard_map/ppermute | solution.py:10
  159.7 31.3 %collective-permute-start.7 = (bf16[23,2,8,256]{3,2,1,0:T(8,128)(2,1)S(1)}, bf16[23,2,8,256]{3,2,1,0:T(8,128)(2,1)S(1)}, u32[]{:S(2)}, u32[]{:S(2)}) collective-permute-start(bf16[23,2,8,256]{3,2,1,0:T(8,128)(2,1)S(1)} %get-tuple-element.12), channel_id=1, source_target_pairs={{128,0},{160,32},{192,64},{224,96},{256,128},{288,160},{320,192},{... | collective-permute-start | bytes 565256 | tf_op jit(solution)/shard_map/ppermute | solution.py:10
  177.7 25.3 %collective-permute-start.8 = (bf16[3,23,2,8,256]{4,3,2,1,0:T(8,128)(2,1)S(1)}, bf16[3,23,2,8,256]{4,3,2,1,0:T(8,128)(2,1)S(1)}, u32[]{:S(2)}, u32[]{:S(2)}) collective-permute-start(bf16[3,23,2,8,256]{4,3,2,1,0:T(8,128)(2,1)S(1)} %slice.189), channel_id=1, source_target_pairs={{1,0},{2,1},{3,2},{4,3},{5,4},{6,5},{7,6},{8,7},{9,8},{10,9},{11,1... | collective-permute-start | bytes 1695752 | tf_op jit(solution)/shard_map/ppermute | solution.py:10
  203.1 20.3 %collective-permute-start.10 = (bf16[2,23,2,8,256]{4,3,2,1,0:T(8,128)(2,1)S(1)}, bf16[2,23,2,8,256]{4,3,2,1,0:T(8,128)(2,1)S(1)}, u32[]{:S(2)}, u32[]{:S(2)}) collective-permute-start(bf16[2,23,2,8,256]{4,3,2,1,0:T(8,128)(2,1)S(1)} %slice.194), channel_id=1, source_target_pairs={{1,0},{2,1},{3,2},{4,3},{5,4},{6,5},{7,6},{8,7},{9,8},{10,9},{11,1... | collective-permute-start | bytes 1130504 | tf_op jit(solution)/shard_map/ppermute | solution.py:10
  223.5 17.1 %collective-permute-start.12 = (bf16[1,23,2,8,256]{4,3,2,1,0:T(8,128)(2,1)S(1)}, bf16[1,23,2,8,256]{4,3,2,1,0:T(8,128)(2,1)S(1)}, u32[]{:S(2)}, u32[]{:S(2)}) collective-permute-start(bf16[1,23,2,8,256]{4,3,2,1,0:T(8,128)(2,1)S(1)} %get-tuple-element.29), channel_id=1, source_target_pairs={{1,0},{2,1},{3,2},{4,3},{5,4},{6,5},{7,6},{8,7},{9,8},{10,9},{11,1... | collective-permute-start | bytes 565256 | tf_op jit(solution)/shard_map/ppermute | solution.py:10
where the time goes:
time: 252 us
  starting transfers between devices  134 us (53%)
  waiting for transfers between devices  85.8 us (34%)
  matrix products  17.3 us (7%)
  other arithmetic  13 us (5%)
    ppermute x14, starting transfers between devices, from_behind(): return lax.ppermute(block, axis, route)  134 us
    ppermute x14, waiting for transfers between devices, from_behind(): return lax.ppermute(block, axis, route)  85.8 us
    dot_general x8, matrix products, cross_terms(): jnp.einsum('kbp,kbq->bpq', left_side, right_side, preferred_element_type=...  9.33 us
    dot_general x8, matrix products, cross_terms(): jnp.einsum('kbp,kbq->bpq', swapped, right_side, preferred_element_type=jn...  7.94 us
    convert_element_type x1, other arithmetic, body(): return (running * (groups * windows) ** (-0.5)).astype(jnp.bfloat16)  7.57 us
  transfers between devices with their start and end apart: 14, of which 6 were waited for; matrix products, arithmetic and copies ran while one was open for 6% of the time, Pallas kernels for 0%

commit v1 on v0

v1 whole, which is shorter than its diff:
```python
import jax
import jax.numpy as jnp
from jax import lax
from jax.sharding import PartitionSpec as P


def from_ahead(block, axis, distance):
    size = lax.axis_size(axis)
    return lax.ppermute(block, axis, [((i + distance) % size, i) for i in range(size)])


def whiten(spectra):
    values = spectra.astype(jnp.float32)
    power = jnp.sum(values * values, axis=-3, keepdims=True)
    level = jnp.mean(power, axis=-2, keepdims=True)
    return (values / jnp.sqrt(0.5 * power + 0.5 * level + 0.25)).astype(jnp.bfloat16)


def cross_terms(source_slots, receiver_slots):
    left = jnp.stack([whiten(s) for s in source_slots])
    right = jnp.stack([whiten(r) for r in receiver_slots])
    bins, width = left.shape[-2:]
    turned = jnp.concatenate([left[:, :, 1:2], -left[:, :, 0:1]], axis=2)
    both = jnp.concatenate([left, turned], axis=-1).reshape(-1, bins, 2 * width)
    right = right.reshape(-1, bins, width)
    return jnp.einsum("kbp,kbq->bpq", both, right, preferred_element_type=jnp.float32)


def body(source_spectra, receiver_spectra):
    source, receiver = source_spectra[0], receiver_spectra[0]
    groups, windows = source.shape[:2]
    width = source.shape[-1]
    source_slots = [source[0]]
    receiver_slots = [receiver[0]]
    source_slots += [from_ahead(source[t], "rcv", t) for t in range(1, groups)]
    receiver_slots += [from_ahead(receiver[t], "src", t) for t in range(1, groups)]
    total = cross_terms(source_slots, receiver_slots)
    stacked = jnp.stack([total[:, :width], total[:, width:]])
    return (stacked * (groups * windows) ** (-0.5)).astype(jnp.bfloat16)


def solution(mesh):
    return jax.shard_map(
        body,
        mesh=mesh,
        in_specs=(P("rcv", None, None, None, None, "src"), P("src", None, None, None, None, "rcv")),
        out_specs=P(None, None, "src", "rcv"),
        check_vma=False,
    )
```

time: 252 us -> 177 us (0.70)
  the two profiles are of different devices: /device:TPU:4 before, /device:TPU:73 now
where the time goes in v1:
time: 177 us; the launch traced here: 176 us
  starting transfers between devices  87.6 us (49%)
  waiting for transfers between devices  76.2 us (43%)
  other arithmetic  7.59 us (4%)
  matrix products  2.38 us (1%)
  local copies, waits for them, and re-layouts  1.95 us (1%)
    ppermute x14, starting transfers between devices, from_ahead(): lax.ppermute(block, axis, [((i + distance) % size, i) for i in range(size)])  87.6 us
    ppermute x14, waiting for transfers between devices, from_ahead(): lax.ppermute(block, axis, [((i + distance) % size, i) for i in range(size)])  76.2 us
  transfers between devices with their start and end apart: 14, of which 6 were waited for; matrix products, arithmetic and copies ran while one was open for 2% of the time, Pallas kernels for 0%

profile of v1, /device:TPU:73, one launch (start us, length us, event | category | flops | bytes accessed | tf_op | source)
XLA Modules:
  0.0 176.3 jit_solution(12356737759937438201)
XLA Ops:
  0.0 1.6 slice_bitcast_fusion.9
  1.6 2.3 %collective-permute-start.6 = (bf16[23,2,8,256]{3,2,1,0:T(8,128)(2,1)S(1)}, bf16[23,2,8,256]{3,2,1,0:T(8,128)(2,1)S(1)}, u32[]{:S(2)}, u32[]{:S(2)}) collective-permute-start(bf16[23,2,8,256]{3,2,1,0:T(8,128)(2,1)S(1)} %get-tuple-element.48), channel_id=1, source_target_pairs={{7,0},{8,1},{9,2},{10,3},{11,4},{12,5},{13,6},{14,7},{15,8},{16,9}... | collective-permute-start | bytes 565256 | tf_op jit(solution)/shard_map/ppermute | solution.py:9
  3.9 11.9 %collective-permute-start.4 = (bf16[23,2,8,256]{3,2,1,0:T(8,128)(2,1)S(1)}, bf16[23,2,8,256]{3,2,1,0:T(8,128)(2,1)S(1)}, u32[]{:S(2)}, u32[]{:S(2)}) collective-permute-start(bf16[23,2,8,256]{3,2,1,0:T(8,128)(2,1)S(1)} %get-tuple-element.49), channel_id=1, source_target_pairs={{5,0},{6,1},{7,2},{8,3},{9,4},{10,5},{11,6},{12,7},{13,8},{14,9},{... | collective-permute-start | bytes 565256 | tf_op jit(solution)/shard_map/ppermute | solution.py:9
  15.8 2.0 %collective-permute-start.3 = (bf16[23,2,8,256]{3,2,1,0:T(8,128)(2,1)S(1)}, bf16[23,2,8,256]{3,2,1,0:T(8,128)(2,1)S(1)}, u32[]{:S(2)}, u32[]{:S(2)}) collective-permute-start(bf16[23,2,8,256]{3,2,1,0:T(8,128)(2,1)S(1)} %get-tuple-element.50), channel_id=1, source_target_pairs={{4,0},{5,1},{6,2},{7,3},{8,4},{9,5},{10,6},{11,7},{12,8},{13,9},{1... | collective-permute-start | bytes 565256 | tf_op jit(solution)/shard_map/ppermute | solution.py:9
  17.8 3.4 %collective-permute-start.2 = (bf16[23,2,8,256]{3,2,1,0:T(8,128)(2,1)S(1)}, bf16[23,2,8,256]{3,2,1,0:T(8,128)(2,1)S(1)}, u32[]{:S(2)}, u32[]{:S(2)}) collective-permute-start(bf16[23,2,8,256]{3,2,1,0:T(8,128)(2,1)S(1)} %get-tuple-element.51), channel_id=1, source_target_pairs={{3,0},{4,1},{5,2},{6,3},{7,4},{8,5},{9,6},{10,7},{11,8},{12,9},{13... | collective-permute-start | bytes 565256 | tf_op jit(solution)/shard_map/ppermute | solution.py:9
  21.2 3.9 %collective-permute-start.5 = (bf16[23,2,8,256]{3,2,1,0:T(8,128)(2,1)S(1)}, bf16[23,2,8,256]{3,2,1,0:T(8,128)(2,1)S(1)}, u32[]{:S(2)}, u32[]{:S(2)}) collective-permute-start(bf16[23,2,8,256]{3,2,1,0:T(8,128)(2,1)S(1)} %get-tuple-element.54), channel_id=1, source_target_pairs={{6,0},{7,1},{8,2},{9,3},{10,4},{11,5},{12,6},{13,7},{14,8},{15,9},... | collective-permute-start | bytes 565256 | tf_op jit(solution)/shard_map/ppermute | solution.py:9
  25.0 1.0 fusion.32
  26.1 0.1 fusion.34
  26.1 0.1 slice_bitcast_fusion.2
  26.5 1.0 fusion.55
  27.5 7.5 %collective-permute-done.5 = bf16[23,2,8,256]{3,2,1,0:T(8,128)(2,1)S(1)} collective-permute-done((bf16[23,2,8,256]{3,2,1,0:T(8,128)(2,1)S(1)}, bf16[23,2,8,256]{3,2,1,0:T(8,128)(2,1)S(1)}, u32[]{:S(2)}, u32[]{:S(2)}) %collective-permute-start.5) | collective-permute-done | bytes 188448 | tf_op jit(solution)/shard_map/ppermute | solution.py:9
  35.0 1.9 %collective-permute-start = (bf16[23,2,8,256]{3,2,1,0:T(8,128)(2,1)S(1)}, bf16[23,2,8,256]{3,2,1,0:T(8,128)(2,1)S(1)}, u32[]{:S(2)}, u32[]{:S(2)}) collective-permute-start(bf16[23,2,8,256]{3,2,1,0:T(8,128)(2,1)S(1)} %get-tuple-element.53), channel_id=1, source_target_pairs={{1,0},{2,1},{3,2},{4,3},{5,4},{6,5},{7,6},{8,7},{9,8},{10,9},{11,1... | collective-permute-start | bytes 565256 | tf_op jit(solution)/shard_map/ppermute | solution.py:9
  36.9 0.1 fusion.14
  37.0 9.9 %collective-permute-done = bf16[23,2,8,256]{3,2,1,0:T(8,128)(2,1)S(1)} collective-permute-done((bf16[23,2,8,256]{3,2,1,0:T(8,128)(2,1)S(1)}, bf16[23,2,8,256]{3,2,1,0:T(8,128)(2,1)S(1)}, u32[]{:S(2)}, u32[]{:S(2)}) %collective-permute-start) | collective-permute-done | bytes 188448 | tf_op jit(solution)/shard_map/ppermute | solution.py:9
  46.9 2.6 %collective-permute-start.1 = (bf16[23,2,8,256]{3,2,1,0:T(8,128)(2,1)S(1)}, bf16[23,2,8,256]{3,2,1,0:T(8,128)(2,1)S(1)}, u32[]{:S(2)}, u32[]{:S(2)}) collective-permute-start(bf16[23,2,8,256]{3,2,1,0:T(8,128)(2,1)S(1)} %get-tuple-element.52), channel_id=1, source_target_pairs={{2,0},{3,1},{4,2},{5,3},{6,4},{7,5},{8,6},{9,7},{10,8},{11,9},{12,... | collective-permute-start | bytes 565256 | tf_op jit(solution)/shard_map/ppermute | solution.py:9
  49.6 0.1 fusion.4
  49.7 5.1 %collective-permute-done.1 = bf16[23,2,8,256]{3,2,1,0:T(8,128)(2,1)S(1)} collective-permute-done((bf16[23,2,8,256]{3,2,1,0:T(8,128)(2,1)S(1)}, bf16[23,2,8,256]{3,2,1,0:T(8,128)(2,1)S(1)}, u32[]{:S(2)}, u32[]{:S(2)}) %collective-permute-start.1) | collective-permute-done | bytes 188448 | tf_op jit(solution)/shard_map/ppermute | solution.py:9
  54.7 19.8 %collective-permute-start.13 = (bf16[23,2,8,256]{3,2,1,0:T(8,128)(2,1)S(1)}, bf16[23,2,8,256]{3,2,1,0:T(8,128)(2,1)S(1)}, u32[]{:S(2)}, u32[]{:S(2)}) collective-permute-start(bf16[23,2,8,256]{3,2,1,0:T(8,128)(2,1)S(1)} %get-tuple-element.39), channel_id=1, source_target_pairs={{224,0},{256,32},{288,64},{320,96},{352,128},{384,160},{416,192},{... | collective-permute-start | bytes 565256 | tf_op jit(solution)/shard_map/ppermute | solution.py:9
  74.5 0.1 fusion.6
  74.6 1.9 %collective-permute-start.11 = (bf16[23,2,8,256]{3,2,1,0:T(8,128)(2,1)S(1)}, bf16[23,2,8,256]{3,2,1,0:T(8,128)(2,1)S(1)}, u32[]{:S(2)}, u32[]{:S(2)}) collective-permute-start(bf16[23,2,8,256]{3,2,1,0:T(8,128)(2,1)S(1)} %get-tuple-element.40), channel_id=1, source_target_pairs={{160,0},{192,32},{224,64},{256,96},{288,128},{320,160},{352,192},{... | collective-permute-start | bytes 565256 | tf_op jit(solution)/shard_map/ppermute | solution.py:9
  76.5 0.1 fusion.8
  76.6 2.8 %collective-permute-start.10 = (bf16[23,2,8,256]{3,2,1,0:T(8,128)(2,1)S(1)}, bf16[23,2,8,256]{3,2,1,0:T(8,128)(2,1)S(1)}, u32[]{:S(2)}, u32[]{:S(2)}) collective-permute-start(bf16[23,2,8,256]{3,2,1,0:T(8,128)(2,1)S(1)} %get-tuple-element.41), channel_id=1, source_target_pairs={{128,0},{160,32},{192,64},{224,96},{256,128},{288,160},{320,192},{... | collective-permute-start | bytes 565256 | tf_op jit(solution)/shard_map/ppermute | solution.py:9
  79.4 0.1 fusion.10
  79.5 13.6 %collective-permute-start.9 = (bf16[23,2,8,256]{3,2,1,0:T(8,128)(2,1)S(1)}, bf16[23,2,8,256]{3,2,1,0:T(8,128)(2,1)S(1)}, u32[]{:S(2)}, u32[]{:S(2)}) collective-permute-start(bf16[23,2,8,256]{3,2,1,0:T(8,128)(2,1)S(1)} %get-tuple-element.42), channel_id=1, source_target_pairs={{96,0},{128,32},{160,64},{192,96},{224,128},{256,160},{288,192},{3... | collective-permute-start | bytes 565256 | tf_op jit(solution)/shard_map/ppermute | solution.py:9
  93.1 0.1 fusion.12
  93.2 1.9 %collective-permute-start.12 = (bf16[23,2,8,256]{3,2,1,0:T(8,128)(2,1)S(1)}, bf16[23,2,8,256]{3,2,1,0:T(8,128)(2,1)S(1)}, u32[]{:S(2)}, u32[]{:S(2)}) collective-permute-start(bf16[23,2,8,256]{3,2,1,0:T(8,128)(2,1)S(1)} %get-tuple-element.45), channel_id=1, source_target_pairs={{192,0},{224,32},{256,64},{288,96},{320,128},{352,160},{384,192},{... | collective-permute-start | bytes 565256 | tf_op jit(solution)/shard_map/ppermute | solution.py:9
  95.2 0.1 fusion.16
  95.3 31.0 %collective-permute-done.12 = bf16[23,2,8,256]{3,2,1,0:T(8,128)(2,1)S(1)} collective-permute-done((bf16[23,2,8,256]{3,2,1,0:T(8,128)(2,1)S(1)}, bf16[23,2,8,256]{3,2,1,0:T(8,128)(2,1)S(1)}, u32[]{:S(2)}, u32[]{:S(2)}) %collective-permute-start.12) | collective-permute-done | bytes 188448 | tf_op jit(solution)/shard_map/ppermute | solution.py:9
  126.3 1.9 %collective-permute-start.7 = (bf16[23,2,8,256]{3,2,1,0:T(8,128)(2,1)S(1)}, bf16[23,2,8,256]{3,2,1,0:T(8,128)(2,1)S(1)}, u32[]{:S(2)}, u32[]{:S(2)}) collective-permute-start(bf16[23,2,8,256]{3,2,1,0:T(8,128)(2,1)S(1)} %get-tuple-element.44), channel_id=1, source_target_pairs={{32,0},{64,32},{96,64},{128,96},{160,128},{192,160},{224,192},{256... | collective-permute-start | bytes 565256 | tf_op jit(solution)/shard_map/ppermute | solution.py:9
  128.2 0.1 fusion.28
  128.3 18.0 %collective-permute-done.7 = bf16[23,2,8,256]{3,2,1,0:T(8,128)(2,1)S(1)} collective-permute-done((bf16[23,2,8,256]{3,2,1,0:T(8,128)(2,1)S(1)}, bf16[23,2,8,256]{3,2,1,0:T(8,128)(2,1)S(1)}, u32[]{:S(2)}, u32[]{:S(2)}) %collective-permute-start.7) | collective-permute-done | bytes 188448 | tf_op jit(solution)/shard_map/ppermute | solution.py:9
  146.3 17.8 %collective-permute-start.8 = (bf16[23,2,8,256]{3,2,1,0:T(8,128)(2,1)S(1)}, bf16[23,2,8,256]{3,2,1,0:T(8,128)(2,1)S(1)}, u32[]{:S(2)}, u32[]{:S(2)}) collective-permute-start(bf16[23,2,8,256]{3,2,1,0:T(8,128)(2,1)S(1)} %get-tuple-element.43), channel_id=1, source_target_pairs={{64,0},{96,32},{128,64},{160,96},{192,128},{224,160},{256,192},{28... | collective-permute-start | bytes 565256 | tf_op jit(solution)/shard_map/ppermute | solution.py:9
  164.1 0.1 fusion.18
  164.2 4.7 %collective-permute-done.8 = bf16[23,2,8,256]{3,2,1,0:T(8,128)(2,1)S(1)} collective-permute-done((bf16[23,2,8,256]{3,2,1,0:T(8,128)(2,1)S(1)}, bf16[23,2,8,256]{3,2,1,0:T(8,128)(2,1)S(1)}, u32[]{:S(2)}, u32[]{:S(2)}) %collective-permute-start.8) | collective-permute-done | bytes 188448 | tf_op jit(solution)/shard_map/ppermute | solution.py:9
  168.9 0.1 fusion.20
  169.0 0.1 fusion.22
  169.1 0.1 fusion.24
  169.2 0.1 fusion.26
  169.3 0.1 fusion.30
  169.4 0.1 add_sqrt_fusion.9
  169.5 0.1 add_sqrt_fusion.14
  169.6 0.1 add_sqrt_fusion.13
  169.6 0.1 add_sqrt_fusion.12
  170.3 0.1 fusion.84
  171.0 0.4 maximum_maximum_fusion
  171.8 2.4 %fusion.1 = f32[8,512,256]{2,1,0:T(8,128)S(1)} fusion(bf16[368,8,512]{2,1,0:T(8,128)(2,1)S(1)} %bitcast.106, bf16[368,8,256]{2,1,0:T(8,128)(2,1)S(1)} %bitcast.107), kind=kOutput, calls=%fused_computation.3 | convolution fusion | flops 771751936 | bytes 8716288 | tf_op jit(solution)/shard_map/kbp,kbq->bpq/dot_general | solution.py:26
  174.2 0.3 slice_bitcast_fusion.1
  174.5 1.9 %fusion = bf16[2,8,256,256]{3,2,1,0:T(8,128)(2,1)} fusion(f32[1,8,256,256]{3,2,1,0:T(8,128)S(1)} %get-tuple-element.38, f32[1,8,256,256]{3,2,1,0:T(8,128)S(1)} %get-tuple-element.37), kind=kLoop, calls=%fused_computation.1 | loop fusion | flops 3145728 | bytes 6291456 | tf_op jit(solution)/shard_map/convert_element_type | solution.py:39
  (53 shorter events, 1.7 us)
Async XLA Ops:
  0.0 26.1 %copy-start = (bf16[1,8,23,2,8,256]{5,4,3,2,1,0:T(8,128)(2,1)S(1)}, bf16[1,8,23,2,8,256]{5,4,3,2,1,0:T(8,128)(2,1)}, u32[]{:S(2)}) copy-start(bf16[1,8,23,2,8,256]{5,4,3,2,1,0:T(8,128)(2,1)} %param.3) | copy-start | bytes 4521988
  1.6 91.6 %collective-permute-start.6 = (bf16[23,2,8,256]{3,2,1,0:T(8,128)(2,1)S(1)}, bf16[23,2,8,256]{3,2,1,0:T(8,128)(2,1)S(1)}, u32[]{:S(2)}, u32[]{:S(2)}) collective-permute-start(bf16[23,2,8,256]{3,2,1,0:T(8,128)(2,1)S(1)} %get-tuple-element.48), channel_id=1, source_target_pairs={{7,0},{8,1},{9,2},{10,3},{11,4},{12,5},{13,6},{14,7},{15,8},{16,9}... | collective-permute-start | bytes 565256 | tf_op jit(solution)/shard_map/ppermute | solution.py:9
  3.9 75.6 %collective-permute-start.4 = (bf16[23,2,8,256]{3,2,1,0:T(8,128)(2,1)S(1)}, bf16[23,2,8,256]{3,2,1,0:T(8,128)(2,1)S(1)}, u32[]{:S(2)}, u32[]{:S(2)}) collective-permute-start(bf16[23,2,8,256]{3,2,1,0:T(8,128)(2,1)S(1)} %get-tuple-element.49), channel_id=1, source_target_pairs={{5,0},{6,1},{7,2},{8,3},{9,4},{10,5},{11,6},{12,7},{13,8},{14,9},{... | collective-permute-start | bytes 565256 | tf_op jit(solution)/shard_map/ppermute | solution.py:9
  15.8 60.9 %collective-permute-start.3 = (bf16[23,2,8,256]{3,2,1,0:T(8,128)(2,1)S(1)}, bf16[23,2,8,256]{3,2,1,0:T(8,128)(2,1)S(1)}, u32[]{:S(2)}, u32[]{:S(2)}) collective-permute-start(bf16[23,2,8,256]{3,2,1,0:T(8,128)(2,1)S(1)} %get-tuple-element.50), channel_id=1, source_target_pairs={{4,0},{5,1},{6,2},{7,3},{8,4},{9,5},{10,6},{11,7},{12,8},{13,9},{1... | collective-permute-start | bytes 565256 | tf_op jit(solution)/shard_map/ppermute | solution.py:9
  17.8 56.8 %collective-permute-start.2 = (bf16[23,2,8,256]{3,2,1,0:T(8,128)(2,1)S(1)}, bf16[23,2,8,256]{3,2,1,0:T(8,128)(2,1)S(1)}, u32[]{:S(2)}, u32[]{:S(2)}) collective-permute-start(bf16[23,2,8,256]{3,2,1,0:T(8,128)(2,1)S(1)} %get-tuple-element.51), channel_id=1, source_target_pairs={{3,0},{4,1},{5,2},{6,3},{7,4},{8,5},{9,6},{10,7},{11,8},{12,9},{13... | collective-permute-start | bytes 565256 | tf_op jit(solution)/shard_map/ppermute | solution.py:9
  21.2 13.8 %collective-permute-start.5 = (bf16[23,2,8,256]{3,2,1,0:T(8,128)(2,1)S(1)}, bf16[23,2,8,256]{3,2,1,0:T(8,128)(2,1)S(1)}, u32[]{:S(2)}, u32[]{:S(2)}) collective-permute-start(bf16[23,2,8,256]{3,2,1,0:T(8,128)(2,1)S(1)} %get-tuple-element.54), channel_id=1, source_target_pairs={{6,0},{7,1},{8,2},{9,3},{10,4},{11,5},{12,6},{13,7},{14,8},{15,9},... | collective-permute-start | bytes 565256 | tf_op jit(solution)/shard_map/ppermute | solution.py:9
  35.0 11.9 %collective-permute-start = (bf16[23,2,8,256]{3,2,1,0:T(8,128)(2,1)S(1)}, bf16[23,2,8,256]{3,2,1,0:T(8,128)(2,1)S(1)}, u32[]{:S(2)}, u32[]{:S(2)}) collective-permute-start(bf16[23,2,8,256]{3,2,1,0:T(8,128)(2,1)S(1)} %get-tuple-element.53), channel_id=1, source_target_pairs={{1,0},{2,1},{3,2},{4,3},{5,4},{6,5},{7,6},{8,7},{9,8},{10,9},{11,1... | collective-permute-start | bytes 565256 | tf_op jit(solution)/shard_map/ppermute | solution.py:9
  46.9 7.8 %collective-permute-start.1 = (bf16[23,2,8,256]{3,2,1,0:T(8,128)(2,1)S(1)}, bf16[23,2,8,256]{3,2,1,0:T(8,128)(2,1)S(1)}, u32[]{:S(2)}, u32[]{:S(2)}) collective-permute-start(bf16[23,2,8,256]{3,2,1,0:T(8,128)(2,1)S(1)} %get-tuple-element.52), channel_id=1, source_target_pairs={{2,0},{3,1},{4,2},{5,3},{6,4},{7,5},{8,6},{9,7},{10,8},{11,9},{12,... | collective-permute-start | bytes 565256 | tf_op jit(solution)/shard_map/ppermute | solution.py:9
  54.7 114.6 %collective-permute-start.13 = (bf16[23,2,8,256]{3,2,1,0:T(8,128)(2,1)S(1)}, bf16[23,2,8,256]{3,2,1,0:T(8,128)(2,1)S(1)}, u32[]{:S(2)}, u32[]{:S(2)}) collective-permute-start(bf16[23,2,8,256]{3,2,1,0:T(8,128)(2,1)S(1)} %get-tuple-element.39), channel_id=1, source_target_pairs={{224,0},{256,32},{288,64},{320,96},{352,128},{384,160},{416,192},{... | collective-permute-start | bytes 565256 | tf_op jit(solution)/shard_map/ppermute | solution.py:9
  74.6 94.6 %collective-permute-start.11 = (bf16[23,2,8,256]{3,2,1,0:T(8,128)(2,1)S(1)}, bf16[23,2,8,256]{3,2,1,0:T(8,128)(2,1)S(1)}, u32[]{:S(2)}, u32[]{:S(2)}) collective-permute-start(bf16[23,2,8,256]{3,2,1,0:T(8,128)(2,1)S(1)} %get-tuple-element.40), channel_id=1, source_target_pairs={{160,0},{192,32},{224,64},{256,96},{288,128},{320,160},{352,192},{... | collective-permute-start | bytes 565256 | tf_op jit(solution)/shard_map/ppermute | solution.py:9
  76.6 92.4 %collective-permute-start.10 = (bf16[23,2,8,256]{3,2,1,0:T(8,128)(2,1)S(1)}, bf16[23,2,8,256]{3,2,1,0:T(8,128)(2,1)S(1)}, u32[]{:S(2)}, u32[]{:S(2)}) collective-permute-start(bf16[23,2,8,256]{3,2,1,0:T(8,128)(2,1)S(1)} %get-tuple-element.41), channel_id=1, source_target_pairs={{128,0},{160,32},{192,64},{224,96},{256,128},{288,160},{320,192},{... | collective-permute-start | bytes 565256 | tf_op jit(solution)/shard_map/ppermute | solution.py:9
  79.5 89.4 %collective-permute-start.9 = (bf16[23,2,8,256]{3,2,1,0:T(8,128)(2,1)S(1)}, bf16[23,2,8,256]{3,2,1,0:T(8,128)(2,1)S(1)}, u32[]{:S(2)}, u32[]{:S(2)}) collective-permute-start(bf16[23,2,8,256]{3,2,1,0:T(8,128)(2,1)S(1)} %get-tuple-element.42), channel_id=1, source_target_pairs={{96,0},{128,32},{160,64},{192,96},{224,128},{256,160},{288,192},{3... | collective-permute-start | bytes 565256 | tf_op jit(solution)/shard_map/ppermute | solution.py:9
  93.2 33.0 %collective-permute-start.12 = (bf16[23,2,8,256]{3,2,1,0:T(8,128)(2,1)S(1)}, bf16[23,2,8,256]{3,2,1,0:T(8,128)(2,1)S(1)}, u32[]{:S(2)}, u32[]{:S(2)}) collective-permute-start(bf16[23,2,8,256]{3,2,1,0:T(8,128)(2,1)S(1)} %get-tuple-element.45), channel_id=1, source_target_pairs={{192,0},{224,32},{256,64},{288,96},{320,128},{352,160},{384,192},{... | collective-permute-start | bytes 565256 | tf_op jit(solution)/shard_map/ppermute | solution.py:9
  126.3 20.0 %collective-permute-start.7 = (bf16[23,2,8,256]{3,2,1,0:T(8,128)(2,1)S(1)}, bf16[23,2,8,256]{3,2,1,0:T(8,128)(2,1)S(1)}, u32[]{:S(2)}, u32[]{:S(2)}) collective-permute-start(bf16[23,2,8,256]{3,2,1,0:T(8,128)(2,1)S(1)} %get-tuple-element.44), channel_id=1, source_target_pairs={{32,0},{64,32},{96,64},{128,96},{160,128},{192,160},{224,192},{256... | collective-permute-start | bytes 565256 | tf_op jit(solution)/shard_map/ppermute | solution.py:9
  146.3 22.6 %collective-permute-start.8 = (bf16[23,2,8,256]{3,2,1,0:T(8,128)(2,1)S(1)}, bf16[23,2,8,256]{3,2,1,0:T(8,128)(2,1)S(1)}, u32[]{:S(2)}, u32[]{:S(2)}) collective-permute-start(bf16[23,2,8,256]{3,2,1,0:T(8,128)(2,1)S(1)} %get-tuple-element.43), channel_id=1, source_target_pairs={{64,0},{96,32},{128,64},{160,96},{192,128},{224,160},{256,192},{28... | collective-permute-start | bytes 565256 | tf_op jit(solution)/shard_map/ppermute | solution.py:9

commit v2 on v1

v2 whole, which is shorter than its diff:
```python
import functools

import jax
import jax.numpy as jnp
from jax import lax
from jax.experimental import pallas as pl
from jax.experimental.pallas import tpu as pltpu
from jax.sharding import PartitionSpec as P


LANES = 128


def whiten_slot(slot_ref, first, out_ref, turned_ref=None):
    windows, parts, bins, width = slot_ref.shape

    def put(ref, row, values):
        for h in range(width // LANES):
            ref[h, pl.ds(row, bins), :] = values[:, h * LANES:(h + 1) * LANES]

    def one_window(w, carry):
        values = slot_ref[w].astype(jnp.float32)
        re, im = values[0], values[1]
        power = re * re + im * im
        level = jnp.mean(power, axis=0, keepdims=True)
        gain = lax.rsqrt(0.5 * power + 0.5 * level + 0.25)
        re, im = re * gain, im * gain
        row = pl.multiple_of(first + w * parts * bins, bins)
        put(out_ref, row, re)
        put(out_ref, row + bins, im)
        if turned_ref is not None:
            put(turned_ref, row, im)
            put(turned_ref, row + bins, -re)
        return carry

    lax.fori_loop(0, windows, one_window, 0, unroll=True)


def of_bin(ref, b, first, rows, bins):
    halves = [ref[h, pl.ds(first * bins + b, rows, stride=bins), :] for h in range(ref.shape[0])]
    return jnp.concatenate(halves, axis=-1)


def early_kernel(count, *refs):
    slots, (acc, left, u, t, v) = refs[:-5], refs[-5:]
    sources, receivers = slots[:count], slots[count:]
    windows, parts, bins, width = slots[0].shape
    slot_rows = windows * parts
    for k, ref in enumerate(sources):
        whiten_slot(ref, k * slot_rows * bins, u, t)
    for k, ref in enumerate(receivers):
        whiten_slot(ref, k * slot_rows * bins, v)
    met = len(receivers) * slot_rows
    rest = (len(sources) - len(receivers)) * slot_rows
    for b in range(bins):
        right = of_bin(v, b, 0, met, bins).astype(jnp.bfloat16)
        for part, ref in enumerate((u, t)):
            now = of_bin(ref, b, 0, met, bins).astype(jnp.bfloat16)
            acc[b, part * width:(part + 1) * width, :] = lax.dot_general(
                now, right, (((0,), (0,)), ((), ())), preferred_element_type=jnp.float32
            )
            later = of_bin(ref, b, met, rest, bins)
            left[b, part * width:(part + 1) * width, :] = later.T.astype(jnp.bfloat16)


def late_kernel(scale, count, *refs):
    slots = [ref.at[k] for ref in refs[:count] for k in range(ref.shape[0])]
    acc, left, out_hbm, v, block, out_sem = refs[count:]
    windows, parts, bins, width = slots[0].shape
    slot_rows = windows * parts
    for k, ref in enumerate(slots):
        whiten_slot(ref, k * slot_rows * bins, v)
    stores = []
    for b in range(bins):
        right = of_bin(v, b, 0, len(slots) * slot_rows, bins).astype(jnp.bfloat16)
        total = acc[b] + jnp.dot(left[b], right, preferred_element_type=jnp.float32)
        total = (total * scale).astype(jnp.bfloat16)
        block[0, b] = total[:width]
        block[1, b] = total[width:]
        for part in range(2):
            copy = pltpu.make_async_copy(block.at[part, b], out_hbm.at[part, b], out_sem.at[part, b])
            copy.start()
            stores.append(copy)
    for copy in stores:
        copy.wait()


def early(sources, receivers):
    windows, parts, bins, width = sources[0].shape
    slot_rows = windows * parts
    met = len(receivers) * slot_rows
    rest = (len(sources) - len(receivers)) * slot_rows
    vmem = pl.BlockSpec(memory_space=pltpu.VMEM)
    lanes = width // LANES
    return pl.pallas_call(
        functools.partial(early_kernel, len(sources)),
        out_shape=(
            jax.ShapeDtypeStruct((bins, 2 * width, width), jnp.float32),
            jax.ShapeDtypeStruct((bins, 2 * width, rest), jnp.bfloat16),
        ),
        in_specs=[vmem] * (len(sources) + len(receivers)),
        out_specs=(vmem, vmem),
        scratch_shapes=[
            pltpu.VMEM((lanes, (met + rest) * bins, LANES), jnp.float32),
            pltpu.VMEM((lanes, (met + rest) * bins, LANES), jnp.float32),
            pltpu.VMEM((lanes, met * bins, LANES), jnp.float32),
        ],
        compiler_params=pltpu.CompilerParams(vmem_limit_bytes=40 * 2**20),
        cost_estimate=pl.CostEstimate(flops=1_000_000, bytes_accessed=1_000_000, transcendentals=0),
    )(*sources, *receivers)


def late(receivers, acc, left, scale):
    windows, parts, bins, width = receivers[0].shape[1:]
    vmem = pl.BlockSpec(memory_space=pltpu.VMEM)
    hbm = pl.BlockSpec(memory_space=pl.ANY)
    return pl.pallas_call(
        functools.partial(late_kernel, scale, len(receivers)),
        out_shape=jax.ShapeDtypeStruct((2, bins, width, width), jnp.bfloat16),
        in_specs=[vmem] * (len(receivers) + 2),
        out_specs=hbm,
        scratch_shapes=[
            pltpu.VMEM((width // LANES, left.shape[-1] * bins, LANES), jnp.float32),
            pltpu.VMEM((2, bins, width, width), jnp.bfloat16),
            pltpu.SemaphoreType.DMA((2, bins)),
        ],
        compiler_params=pltpu.CompilerParams(vmem_limit_bytes=40 * 2**20),
        cost_estimate=pl.CostEstimate(flops=200_000_000, bytes_accessed=9_000_000, transcendentals=200_000),
    )(*receivers, acc, left)


def pack_kernel(place_ref, source, z, p, q, y1, y2, y3, y4):
    place = place_ref[0, 0]
    pairs = (None, y1, y2, y3)
    for t in range(1, 8):
        out = y4 if t == 4 else pairs[t % 4].at[t // 4]

        def put(cond, ref, index, out=out):
            @pl.when(cond)
            def _():
                out[...] = ref[index]

        if t <= 3:
            put(place >= t, source, t)
        put((place < t) & (place >= t - 4), z, jnp.clip(t - 1 - place, 0, 3))
        if t in (5, 6):
            put(place == 0, p, t - 5)
        if t in (6, 7):
            put(place == 1, p, t - 6)
        if t == 7:
            put((place == 0) | (place == 2), q, 0)


def pack(place, source, z, p, q):
    slot = jax.ShapeDtypeStruct(source.shape[1:], source.dtype)
    two = jax.ShapeDtypeStruct((2,) + source.shape[1:], source.dtype)
    vmem = pl.BlockSpec(memory_space=pltpu.VMEM)
    return pl.pallas_call(
        pack_kernel,
        out_shape=(two, two, two, slot),
        in_specs=[pl.BlockSpec(memory_space=pltpu.SMEM)] + [vmem] * 4,
        out_specs=(vmem,) * 4,
        compiler_params=pltpu.CompilerParams(vmem_limit_bytes=24 * 2**20),
        cost_estimate=pl.CostEstimate(flops=60_000_000_000, bytes_accessed=6_000_000, transcendentals=0),
    )(place.astype(jnp.int32).reshape(1, 1), source, z, p, q)


PLAN = (
    ("send", "Cl"),
    ("send", "D"),
    ("send", "X6"),
    ("send", "X2"),
    ("send", "Q"),
    ("send", "P"),
    ("send", "Z"),
    ("after", "X2"),
    ("send", "O"),
    ("after", "P"),
    ("after", "Q"),
    ("after", "Z"),
    ("send", "F"),
    ("send", "Y1"),
    ("send", "Y2"),
    ("send", "Y3"),
)


def body(source_spectra, receiver_spectra):
    source, receiver = source_spectra[0], receiver_spectra[0]
    groups, windows = source.shape[:2]
    core = lax.axis_index("src") % 2
    place = lax.axis_index("rcv") % 4
    got, held = {}, {}

    def of_core(zero, one):
        return jnp.where(core == 0, zero, one)

    def pair(b):
        if not held:
            held["y"] = pack(place, source, got["Z"], got["P"], got["Q"][None])
        return held["y"][b - 1]

    def low(far):
        return of_core(receiver[1], receiver[3]) if far else of_core(receiver[3], receiver[1])

    def high(far):
        return of_core(receiver[5], receiver[7]) if far else of_core(receiver[7], receiver[5])

    def back(steps):
        return [(i, (i - steps(i)) % 16) for i in range(16)]

    def back_z(steps, places=range(4)):
        return [(i, (i - 4 * steps) % 32) for i in range(32) if i % 4 in places]

    def back_y(steps):
        return [(i, i // 4 * 4 + (i % 4 - steps) % 4) for i in range(32)]

    moves = {
        "Cl": ("src", [(i, i ^ 1) for i in range(16)], lambda: low(True)),
        "D": ("src", [(i, (i - 4) % 16 ^ 1) for i in range(16)], lambda: high(True)),
        "X6": ("src", back(lambda i: 4), lambda: receiver[6]),
        "X2": ("src", back(lambda i: 4), lambda: jnp.stack([receiver[4], high(False)])),
        "O": ("src", back(lambda i: 3 - 2 * (i % 2)), lambda: jnp.stack([low(False), got["X2"][1]])),
        "F": ("src", back(lambda i: 2), lambda: jnp.stack([receiver[2], got["X6"], got["Cl"], got["D"]])),
        "Z": ("rcv", back_z(1), lambda: lax.dynamic_slice_in_dim(source, 1 + place, 4, 0)),
        "P": ("rcv", back_z(2, (0, 1)), lambda: lax.dynamic_slice_in_dim(source, jnp.minimum(5 + place, 6), 2, 0)),
        "Q": ("rcv", back_z(2, (0, 2)), lambda: source[7]),
        "Y1": ("rcv", back_y(1), lambda: pair(1)),
        "Y2": ("rcv", back_y(2), lambda: pair(2)),
        "Y3": ("rcv", back_y(3), lambda: pair(3)),
    }
    tied = []
    for act, name in PLAN:
        if act == "after":
            tied.append(name)
            continue
        axis, route, make = moves[name]
        block = make()
        if tied:
            block, *arrived = lax.optimization_barrier((block, *[got[n] for n in tied]))
            got.update(zip(tied, arrived))
        got[name] = lax.ppermute(block, axis, route)
    y1, y2, y3 = got["Y1"], got["Y2"], got["Y3"]
    sources = [source[0], held["y"][3], of_core(y1[0], y3[0]), of_core(y1[1], y3[1])]
    sources += [y2[0], y2[1], of_core(y3[0], y1[0]), of_core(y3[1], y1[1])]
    acc, left = early(sources, [receiver[0], got["X2"][0], got["O"][0], got["O"][1]])
    return late([got["F"]], acc, left, (groups * windows) ** (-0.5))


def solution(mesh):
    return jax.shard_map(
        body,
        mesh=mesh,
        in_specs=(P("rcv", None, None, None, None, "src"), P("src", None, None, None, None, "rcv")),
        out_specs=P(None, None, "src", "rcv"),
        check_vma=False,
    )
```

time: 177 us -> 129 us (0.73)
  the two profiles are of different devices: /device:TPU:73 before, /device:TPU:65 now
where the time goes in v2:
time: 129 us
  waiting for transfers between devices  62.2 us (48%)
  starting transfers between devices  52.7 us (41%)
  Pallas kernels  6.2 us (5%)
  other arithmetic  4.37 us (3%)
  local copies, waits for them, and re-layouts  3.17 us (2%)
    ppermute x12, waiting for transfers between devices, body(): got[name] = lax.ppermute(block, axis, route)  62.2 us
    ppermute x12, starting transfers between devices, body(): got[name] = lax.ppermute(block, axis, route)  52.7 us
    pallas_call x1, Pallas kernels, early(): pl.pallas_call(functools.partial(early_kernel, len(sources)), out_shape=(...  3.67 us
  transfers between devices with their start and end apart: 12, of which 6 were waited for; matrix products, arithmetic and copies ran while one was open for 5% of the time, Pallas kernels for 3%

profile of v2, /device:TPU:65, one launch (start us, length us, event | category | flops | bytes accessed | tf_op | source)
XLA Modules:
  0.0 128.8 jit_solution(16923947649542539986)
XLA Ops:
  0.0 1.2 dynamic-slice_bitcast_fusion
  1.2 1.9 %collective-permute-start.6 = (bf16[4,23,2,8,256]{4,3,2,1,0:T(8,128)(2,1)S(1)}, bf16[4,23,2,8,256]{4,3,2,1,0:T(8,128)(2,1)S(1)}, u32[]{:S(2)}, u32[]{:S(2)}) collective-permute-start(bf16[4,23,2,8,256]{4,3,2,1,0:T(8,128)(2,1)S(1)} %dynamic-slice_bitcast_fusion), channel_id=1, source_target_pairs={{0,28},{1,29},{2,30},{3,31},{4,0},{5,1},{6,2},{7,3},{8,4},{9,5},{1... | collective-permute-start | bytes 2261000 | tf_op jit(solution)/shard_map/ppermute | solution.py:242
  3.1 0.0 copy-start
  3.1 2.5 %slice_bitcast_fusion.5 = (bf16[23,2,8,256]{3,2,1,0:T(8,128)(2,1)S(1)}, bf16[23,2,8,256]{3,2,1,0:T(8,128)(2,1)}, bf16[1,23,2,8,256]{4,3,2,1,0:T(8,128)(2,1)S(1)}...) fusion(bf16[1,8,23,2,8,256]{5,4,3,2,1,0:T(8,128)(2,1)} %param.3, ...), kind=kLoop, calls=%fused_computation.10 | loop fusion | flops 376832 | bytes 3014657 | tf_op jit(solution)/shard_map/squeeze | solution.py:246
  5.6 5.0 %collective-permute-start.2 = (bf16[23,2,8,256]{3,2,1,0:T(8,128)(2,1)}, bf16[23,2,8,256]{3,2,1,0:T(8,128)(2,1)}, u32[]{:S(2)}, u32[]{:S(2)}) collective-permute-start(bf16[23,2,8,256]{3,2,1,0:T(8,128)(2,1)} %get-tuple-element.44), channel_id=1, source_target_pairs={{0,416},{32,384},{64,480},{96,448},{128,32},{160,0},{192,96},{224,... | collective-permute-start | bytes 565256 | tf_op jit(solution)/shard_map/ppermute | solution.py:242
  10.6 0.8 pad_maximum_fusion.1
  11.4 2.4 %collective-permute-start.3 = (bf16[2,23,2,8,256]{4,3,2,1,0:T(8,128)(2,1)}, bf16[2,23,2,8,256]{4,3,2,1,0:T(8,128)(2,1)}, u32[]{:S(2)}, u32[]{:S(2)}) collective-permute-start(bf16[2,23,2,8,256]{4,3,2,1,0:T(8,128)(2,1)} %pad_maximum_fusion.1), channel_id=1, source_target_pairs={{0,384},{32,416},{64,448},{96,480},{128,0},{160,32},{192,64},{224,... | collective-permute-start | bytes 1130504 | tf_op jit(solution)/shard_map/ppermute | solution.py:242
  13.9 0.0 copy-done
  13.9 0.0 copy-start.1
  13.9 12.6 %collective-permute-start.4 = (bf16[2,23,2,8,256]{4,3,2,1,0:T(8,128)(2,1)S(1)}, bf16[2,23,2,8,256]{4,3,2,1,0:T(8,128)(2,1)S(1)}, u32[]{:S(2)}, u32[]{:S(2)}) collective-permute-start(bf16[2,23,2,8,256]{4,3,2,1,0:T(8,128)(2,1)S(1)} %dynamic-slice_bitcast_fusion.1), channel_id=1, source_target_pairs={{0,24},{1,25},{4,28},{5,29},{8,0},{9,1},{12,4},{13,5},{16,8},{17,9... | collective-permute-start | bytes 1130504 | tf_op jit(solution)/shard_map/ppermute | solution.py:242
  26.5 2.0 %collective-permute-start.1 = (bf16[23,2,8,256]{3,2,1,0:T(8,128)(2,1)}, bf16[23,2,8,256]{3,2,1,0:T(8,128)(2,1)S(1)}, u32[]{:S(2)}, u32[]{:S(2)}) collective-permute-start(bf16[23,2,8,256]{3,2,1,0:T(8,128)(2,1)} %get-tuple-element.46), channel_id=1, source_target_pairs={{0,32},{32,0},{64,96},{96,64},{128,160},{160,128},{192,224},{224,1... | collective-permute-start | bytes 565256 | tf_op jit(solution)/shard_map/ppermute | solution.py:242
  28.6 0.0 collective-permute-done.2
  28.6 2.5 %collective-permute-start = (bf16[23,2,8,256]{3,2,1,0:T(8,128)(2,1)}, bf16[23,2,8,256]{3,2,1,0:T(8,128)(2,1)S(1)}, u32[]{:S(2)}, u32[]{:S(2)}) collective-permute-start(bf16[23,2,8,256]{3,2,1,0:T(8,128)(2,1)} %get-tuple-element.48), channel_id=1, source_target_pairs={{0,384},{32,416},{64,448},{96,480},{128,0},{160,32},{192,64},{224,... | collective-permute-start | bytes 565256 | tf_op jit(solution)/shard_map/ppermute | solution.py:242
  31.1 0.0 collective-permute-done.1
  31.1 1.9 %collective-permute-start.5 = (bf16[23,2,8,256]{3,2,1,0:T(8,128)(2,1)S(1)}, bf16[23,2,8,256]{3,2,1,0:T(8,128)(2,1)S(1)}, u32[]{:S(2)}, u32[]{:S(2)}) collective-permute-start(bf16[23,2,8,256]{3,2,1,0:T(8,128)(2,1)S(1)} %get-tuple-element.52), channel_id=1, source_target_pairs={{0,24},{2,26},{4,28},{6,30},{8,0},{10,2},{12,4},{14,6},{16,8},{18,... | collective-permute-start | bytes 565256 | tf_op jit(solution)/shard_map/ppermute | solution.py:242
  33.0 3.6 %collective-permute-done = bf16[23,2,8,256]{3,2,1,0:T(8,128)(2,1)S(1)} collective-permute-done((bf16[23,2,8,256]{3,2,1,0:T(8,128)(2,1)}, bf16[23,2,8,256]{3,2,1,0:T(8,128)(2,1)S(1)}, u32[]{:S(2)}, u32[]{:S(2)}) %collective-permute-start) | collective-permute-done | bytes 188448 | tf_op jit(solution)/shard_map/ppermute | solution.py:242
  36.6 0.0 copy-done.1
  36.6 1.0 pad_maximum_fusion
  37.6 0.0 collective-permute-done.3
  37.7 0.9 slice.104
  38.6 1.2 collective-permute-start.11
  39.9 8.1 %collective-permute-done.5 = bf16[23,2,8,256]{3,2,1,0:T(8,128)(2,1)S(1)} collective-permute-done((bf16[23,2,8,256]{3,2,1,0:T(8,128)(2,1)S(1)}, bf16[23,2,8,256]{3,2,1,0:T(8,128)(2,1)S(1)}, u32[]{:S(2)}, u32[]{:S(2)}) %collective-permute-start.5) | collective-permute-done | bytes 188448 | tf_op jit(solution)/shard_map/ppermute | solution.py:242
  48.0 0.0 collective-permute-done.4.p
  48.0 0.0 collective-permute-done.6.z
  48.0 14.7 %collective-permute-start.7 = (bf16[4,23,2,8,256]{4,3,2,1,0:T(8,128)(2,1)S(1)}, bf16[4,23,2,8,256]{4,3,2,1,0:T(8,128)(2,1)S(1)}, u32[]{:S(2)}, u32[]{:S(2)}) collective-permute-start(bf16[4,23,2,8,256]{4,3,2,1,0:T(8,128)(2,1)S(1)} %pad_maximum_fusion), channel_id=1, source_target_pairs={{0,448},{32,480},{64,0},{96,32},{128,64},{160,96},{192,128},{224,1... | collective-permute-start | bytes 2261000 | tf_op jit(solution)/shard_map/ppermute | solution.py:242
  62.7 0.2 shard_map.28
  62.8 1.9 %collective-permute-start.9 = (bf16[2,23,2,8,256]{4,3,2,1,0:T(8,128)(2,1)S(1)}, bf16[2,23,2,8,256]{4,3,2,1,0:T(8,128)(2,1)S(1)}, u32[]{:S(2)}, u32[]{:S(2)}) collective-permute-start(bf16[2,23,2,8,256]{4,3,2,1,0:T(8,128)(2,1)S(1)} %get-tuple-element.37), channel_id=1, source_target_pairs={{0,1},{1,2},{2,3},{3,0},{4,5},{5,6},{6,7},{7,4},{8,9},{9,10},{10,1... | collective-permute-start | bytes 1130504 | tf_op jit(solution)/shard_map/ppermute | solution.py:242
  64.7 1.9 %collective-permute-start.10 = (bf16[2,23,2,8,256]{4,3,2,1,0:T(8,128)(2,1)S(1)}, bf16[2,23,2,8,256]{4,3,2,1,0:T(8,128)(2,1)S(1)}, u32[]{:S(2)}, u32[]{:S(2)}) collective-permute-start(bf16[2,23,2,8,256]{4,3,2,1,0:T(8,128)(2,1)S(1)} %get-tuple-element.38), channel_id=1, source_target_pairs={{0,2},{1,3},{2,0},{3,1},{4,6},{5,7},{6,4},{7,5},{8,10},{9,11},{10,... | collective-permute-start | bytes 1130504 | tf_op jit(solution)/shard_map/ppermute | solution.py:242
  66.7 4.6 %collective-permute-start.8 = (bf16[2,23,2,8,256]{4,3,2,1,0:T(8,128)(2,1)S(1)}, bf16[2,23,2,8,256]{4,3,2,1,0:T(8,128)(2,1)S(1)}, u32[]{:S(2)}, u32[]{:S(2)}) collective-permute-start(bf16[2,23,2,8,256]{4,3,2,1,0:T(8,128)(2,1)S(1)} %get-tuple-element.32), channel_id=1, source_target_pairs={{0,3},{1,0},{2,1},{3,2},{4,7},{5,4},{6,5},{7,6},{8,11},{9,8},{10,9... | collective-permute-start | bytes 1130504 | tf_op jit(solution)/shard_map/ppermute | solution.py:242
  71.2 0.0 collective-permute-done.11
  71.3 0.9 slice_bitcast_fusion.4.refs_9_
  72.2 2.5 %collective-permute-done.10 = bf16[2,23,2,8,256]{4,3,2,1,0:T(8,128)(2,1)S(1)} collective-permute-done((bf16[2,23,2,8,256]{4,3,2,1,0:T(8,128)(2,1)S(1)}, bf16[2,23,2,8,256]{4,3,2,1,0:T(8,128)(2,1)S(1)}, u32[]{:S(2)}, u32[]{:S(2)}) %collective-permute-start.10) | collective-permute-done | bytes 376864 | tf_op jit(solution)/shard_map/ppermute | solution.py:242
  74.7 1.7 %collective-permute-done.9 = bf16[2,23,2,8,256]{4,3,2,1,0:T(8,128)(2,1)S(1)} collective-permute-done((bf16[2,23,2,8,256]{4,3,2,1,0:T(8,128)(2,1)S(1)}, bf16[2,23,2,8,256]{4,3,2,1,0:T(8,128)(2,1)S(1)}, u32[]{:S(2)}, u32[]{:S(2)}) %collective-permute-start.9) | collective-permute-done | bytes 376864 | tf_op jit(solution)/shard_map/ppermute | solution.py:242
  76.4 2.5 %collective-permute-done.8 = bf16[2,23,2,8,256]{4,3,2,1,0:T(8,128)(2,1)S(1)} collective-permute-done((bf16[2,23,2,8,256]{4,3,2,1,0:T(8,128)(2,1)S(1)}, bf16[2,23,2,8,256]{4,3,2,1,0:T(8,128)(2,1)S(1)}, u32[]{:S(2)}, u32[]{:S(2)}) %collective-permute-start.8) | collective-permute-done | bytes 376864 | tf_op jit(solution)/shard_map/ppermute | solution.py:242
  78.9 0.1 select_bitcast_fusion
  79.0 3.7 %shard_map.29 = (f32[8,512,256]{2,1,0:T(8,128)S(1)}, bf16[8,512,184]{2,1,0:T(8,128)(2,1)S(1)}) custom-call(bf16[23,2,8,256]{3,2,1,0:T(8,128)(2,1)S(1)} %get-tuple-element.51.refs_0_, bf16[23,2,8,256]{3,2,1,0:T(8,128)(2,1)S(1)} %get-tuple-element.29.refs_1_, bf16[23,2,8,256]{3,2,1,0:T(8,128)(2,1)S(1)} %get-tuple-element.56.refs_2_, ...), custom_call_target="tpu_custom_call" | custom-call | flops 1000000 | bytes 1000000 | tf_op jit(solution)/shard_map/pallas_call | solution.py:95
  82.7 43.8 %collective-permute-done.7.refs_0_ = bf16[4,23,2,8,256]{4,3,2,1,0:T(8,128)(2,1)S(1)} collective-permute-done((bf16[4,23,2,8,256]{4,3,2,1,0:T(8,128)(2,1)S(1)}, bf16[4,23,2,8,256]{4,3,2,1,0:T(8,128)(2,1)S(1)}, u32[]{:S(2)}, u32[]{:S(2)}) %collective-permute-start.7) | collective-permute-done | bytes 753696 | tf_op jit(solution)/shard_map/ppermute | solution.py:242
  126.4 2.4 %shard_map.30 = bf16[2,8,256,256]{3,2,1,0:T(8,128)(2,1)} custom-call(bf16[4,23,2,8,256]{4,3,2,1,0:T(8,128)(2,1)S(1)} %collective-permute-done.7.refs_0_, f32[8,512,256]{2,1,0:T(8,128)S(1)} %get-tuple-element.41.refs_1_, bf16[8,512,184]{2,1,0:T(8,128)(2,1)S(1)} %get-tuple-element.42.refs_2_), custom_call_target="tpu_custom_call" | custom-call | flops 200000000 | bytes 9000000 | tf_op jit(solution)/shard_map/pallas_call | solution.py:117
  (5 shorter events, 0.1 us)
Async XLA Ops:
  1.2 46.8 %collective-permute-start.6 = (bf16[4,23,2,8,256]{4,3,2,1,0:T(8,128)(2,1)S(1)}, bf16[4,23,2,8,256]{4,3,2,1,0:T(8,128)(2,1)S(1)}, u32[]{:S(2)}, u32[]{:S(2)}) collective-permute-start(bf16[4,23,2,8,256]{4,3,2,1,0:T(8,128)(2,1)S(1)} %dynamic-slice_bitcast_fusion), channel_id=1, source_target_pairs={{0,28},{1,29},{2,30},{3,31},{4,0},{5,1},{6,2},{7,3},{8,4},{9,5},{1... | collective-permute-start | bytes 2261000 | tf_op jit(solution)/shard_map/ppermute | solution.py:242
  3.1 10.8 %copy-start = (bf16[1,8,23,2,8,256]{5,4,3,2,1,0:T(8,128)(2,1)S(1)}, bf16[1,8,23,2,8,256]{5,4,3,2,1,0:T(8,128)(2,1)}, u32[]{:S(2)}) copy-start(bf16[1,8,23,2,8,256]{5,4,3,2,1,0:T(8,128)(2,1)} %param.2) | copy-start | bytes 4521988
  5.6 23.0 %collective-permute-start.2 = (bf16[23,2,8,256]{3,2,1,0:T(8,128)(2,1)}, bf16[23,2,8,256]{3,2,1,0:T(8,128)(2,1)}, u32[]{:S(2)}, u32[]{:S(2)}) collective-permute-start(bf16[23,2,8,256]{3,2,1,0:T(8,128)(2,1)} %get-tuple-element.44), channel_id=1, source_target_pairs={{0,416},{32,384},{64,480},{96,448},{128,32},{160,0},{192,96},{224,... | collective-permute-start | bytes 565256 | tf_op jit(solution)/shard_map/ppermute | solution.py:242
  11.4 26.2 %collective-permute-start.3 = (bf16[2,23,2,8,256]{4,3,2,1,0:T(8,128)(2,1)}, bf16[2,23,2,8,256]{4,3,2,1,0:T(8,128)(2,1)}, u32[]{:S(2)}, u32[]{:S(2)}) collective-permute-start(bf16[2,23,2,8,256]{4,3,2,1,0:T(8,128)(2,1)} %pad_maximum_fusion.1), channel_id=1, source_target_pairs={{0,384},{32,416},{64,448},{96,480},{128,0},{160,32},{192,64},{224,... | collective-permute-start | bytes 1130504 | tf_op jit(solution)/shard_map/ppermute | solution.py:242
  13.9 22.7 %copy-start.1 = (bf16[1,23,2,8,256]{4,3,2,1,0:T(8,128)(2,1)S(1)}, bf16[1,23,2,8,256]{4,3,2,1,0:T(8,128)(2,1)}, u32[]{:S(2)}) copy-start(bf16[1,23,2,8,256]{4,3,2,1,0:T(8,128)(2,1)} %get-tuple-element.49) | copy-start | bytes 565252
  13.9 34.0 %collective-permute-start.4 = (bf16[2,23,2,8,256]{4,3,2,1,0:T(8,128)(2,1)S(1)}, bf16[2,23,2,8,256]{4,3,2,1,0:T(8,128)(2,1)S(1)}, u32[]{:S(2)}, u32[]{:S(2)}) collective-permute-start(bf16[2,23,2,8,256]{4,3,2,1,0:T(8,128)(2,1)S(1)} %dynamic-slice_bitcast_fusion.1), channel_id=1, source_target_pairs={{0,24},{1,25},{4,28},{5,29},{8,0},{9,1},{12,4},{13,5},{16,8},{17,9... | collective-permute-start | bytes 1130504 | tf_op jit(solution)/shard_map/ppermute | solution.py:242
  26.5 4.6 %collective-permute-start.1 = (bf16[23,2,8,256]{3,2,1,0:T(8,128)(2,1)}, bf16[23,2,8,256]{3,2,1,0:T(8,128)(2,1)S(1)}, u32[]{:S(2)}, u32[]{:S(2)}) collective-permute-start(bf16[23,2,8,256]{3,2,1,0:T(8,128)(2,1)} %get-tuple-element.46), channel_id=1, source_target_pairs={{0,32},{32,0},{64,96},{96,64},{128,160},{160,128},{192,224},{224,1... | collective-permute-start | bytes 565256 | tf_op jit(solution)/shard_map/ppermute | solution.py:242
  28.6 8.0 %collective-permute-start = (bf16[23,2,8,256]{3,2,1,0:T(8,128)(2,1)}, bf16[23,2,8,256]{3,2,1,0:T(8,128)(2,1)S(1)}, u32[]{:S(2)}, u32[]{:S(2)}) collective-permute-start(bf16[23,2,8,256]{3,2,1,0:T(8,128)(2,1)} %get-tuple-element.48), channel_id=1, source_target_pairs={{0,384},{32,416},{64,448},{96,480},{128,0},{160,32},{192,64},{224,... | collective-permute-start | bytes 565256 | tf_op jit(solution)/shard_map/ppermute | solution.py:242
  31.1 16.9 %collective-permute-start.5 = (bf16[23,2,8,256]{3,2,1,0:T(8,128)(2,1)S(1)}, bf16[23,2,8,256]{3,2,1,0:T(8,128)(2,1)S(1)}, u32[]{:S(2)}, u32[]{:S(2)}) collective-permute-start(bf16[23,2,8,256]{3,2,1,0:T(8,128)(2,1)S(1)} %get-tuple-element.52), channel_id=1, source_target_pairs={{0,24},{2,26},{4,28},{6,30},{8,0},{10,2},{12,4},{14,6},{16,8},{18,... | collective-permute-start | bytes 565256 | tf_op jit(solution)/shard_map/ppermute | solution.py:242
  38.6 32.6 %collective-permute-start.11 = (bf16[2,23,2,8,256]{4,3,2,1,0:T(8,128)(2,1)S(1)}, bf16[2,23,2,8,256]{4,3,2,1,0:T(8,128)(2,1)S(1)}, u32[]{:S(2)}, u32[]{:S(2)}) collective-permute-start(bf16[2,23,2,8,256]{4,3,2,1,0:T(8,128)(2,1)S(1)} %pad_maximum_fusion.2), channel_id=1, source_target_pairs={{0,416},{32,0},{64,480},{96,64},{128,32},{160,128},{192,96},{224,1... | collective-permute-start | bytes 1130504 | tf_op jit(solution)/shard_map/ppermute | solution.py:242
  48.0 78.5 %collective-permute-start.7 = (bf16[4,23,2,8,256]{4,3,2,1,0:T(8,128)(2,1)S(1)}, bf16[4,23,2,8,256]{4,3,2,1,0:T(8,128)(2,1)S(1)}, u32[]{:S(2)}, u32[]{:S(2)}) collective-permute-start(bf16[4,23,2,8,256]{4,3,2,1,0:T(8,128)(2,1)S(1)} %pad_maximum_fusion), channel_id=1, source_target_pairs={{0,448},{32,480},{64,0},{96,32},{128,64},{160,96},{192,128},{224,1... | collective-permute-start | bytes 2261000 | tf_op jit(solution)/shard_map/ppermute | solution.py:242
  62.8 13.6 %collective-permute-start.9 = (bf16[2,23,2,8,256]{4,3,2,1,0:T(8,128)(2,1)S(1)}, bf16[2,23,2,8,256]{4,3,2,1,0:T(8,128)(2,1)S(1)}, u32[]{:S(2)}, u32[]{:S(2)}) collective-permute-start(bf16[2,23,2,8,256]{4,3,2,1,0:T(8,128)(2,1)S(1)} %get-tuple-element.37), channel_id=1, source_target_pairs={{0,1},{1,2},{2,3},{3,0},{4,5},{5,6},{6,7},{7,4},{8,9},{9,10},{10,1... | collective-permute-start | bytes 1130504 | tf_op jit(solution)/shard_map/ppermute | solution.py:242
  64.7 10.0 %collective-permute-start.10 = (bf16[2,23,2,8,256]{4,3,2,1,0:T(8,128)(2,1)S(1)}, bf16[2,23,2,8,256]{4,3,2,1,0:T(8,128)(2,1)S(1)}, u32[]{:S(2)}, u32[]{:S(2)}) collective-permute-start(bf16[2,23,2,8,256]{4,3,2,1,0:T(8,128)(2,1)S(1)} %get-tuple-element.38), channel_id=1, source_target_pairs={{0,2},{1,3},{2,0},{3,1},{4,6},{5,7},{6,4},{7,5},{8,10},{9,11},{10,... | collective-permute-start | bytes 1130504 | tf_op jit(solution)/shard_map/ppermute | solution.py:242
  66.7 12.3 %collective-permute-start.8 = (bf16[2,23,2,8,256]{4,3,2,1,0:T(8,128)(2,1)S(1)}, bf16[2,23,2,8,256]{4,3,2,1,0:T(8,128)(2,1)S(1)}, u32[]{:S(2)}, u32[]{:S(2)}) collective-permute-start(bf16[2,23,2,8,256]{4,3,2,1,0:T(8,128)(2,1)S(1)} %get-tuple-element.32), channel_id=1, source_target_pairs={{0,3},{1,0},{2,1},{3,2},{4,7},{5,4},{6,5},{7,6},{8,11},{9,8},{10,9... | collective-permute-start | bytes 1130504 | tf_op jit(solution)/shard_map/ppermute | solution.py:242

commit v3 on v2

--- a/solution.py
+++ b/solution.py
@@ -129,7 +129,7 @@
     )(*receivers, acc, left)
 
 
-def pack_kernel(place_ref, source, z, p, q, y1, y2, y3, y4):
+def pack_kernel(place_ref, source, z, p, y1, y2, y3, y4):
     place = place_ref[0, 0]
     pairs = (None, y1, y2, y3)
     for t in range(1, 8):
@@ -140,48 +140,41 @@
             def _():
                 out[...] = ref[index]
 
+        aside = {6: place == 0, 7: place == 2}.get(t, False)
         if t <= 3:
             put(place >= t, source, t)
         put((place < t) & (place >= t - 4), z, jnp.clip(t - 1 - place, 0, 3))
-        if t in (5, 6):
-            put(place == 0, p, t - 5)
+        if t in (6, 7):
+            put(aside, source, t)
+        if t in (5, 7):
+            put(place == 0, p, t // 7)
         if t in (6, 7):
             put(place == 1, p, t - 6)
-        if t == 7:
-            put((place == 0) | (place == 2), q, 0)
-
-
-def pack(place, source, z, p, q):
+
+
+def pack(place, source, z, p):
     slot = jax.ShapeDtypeStruct(source.shape[1:], source.dtype)
     two = jax.ShapeDtypeStruct((2,) + source.shape[1:], source.dtype)
     vmem = pl.BlockSpec(memory_space=pltpu.VMEM)
     return pl.pallas_call(
         pack_kernel,
         out_shape=(two, two, two, slot),
-        in_specs=[pl.BlockSpec(memory_space=pltpu.SMEM)] + [vmem] * 4,
+        in_specs=[pl.BlockSpec(memory_space=pltpu.SMEM)] + [vmem] * 3,
         out_specs=(vmem,) * 4,
         compiler_params=pltpu.CompilerParams(vmem_limit_bytes=24 * 2**20),
-        cost_estimate=pl.CostEstimate(flops=60_000_000_000, bytes_accessed=6_000_000, transcendentals=0),
-    )(place.astype(jnp.int32).reshape(1, 1), source, z, p, q)
+        cost_estimate=pl.CostEstimate(flops=1_000, bytes_accessed=1_000, transcendentals=0),
+    )(place.astype(jnp.int32).reshape(1, 1), source, z, p)
 
 
 PLAN = (
-    ("send", "Cl"),
-    ("send", "D"),
-    ("send", "X6"),
-    ("send", "X2"),
+    ("send", "W"),
     ("send", "Q"),
     ("send", "P"),
     ("send", "Z"),
-    ("after", "X2"),
-    ("send", "O"),
+    ("after", "Z"),
     ("after", "P"),
     ("after", "Q"),
-    ("after", "Z"),
     ("send", "F"),
-    ("send", "Y1"),
-    ("send", "Y2"),
-    ("send", "Y3"),
 )
 
 
@@ -190,16 +183,11 @@
     groups, windows = source.shape[:2]
     core = lax.axis_index("src") % 2
     place = lax.axis_index("rcv") % 4
-    got, held = {}, {}
+    got = {}
 
     def of_core(zero, one):
         return jnp.where(core == 0, zero, one)
 
-    def pair(b):
-        if not held:
-            held["y"] = pack(place, source, got["Z"], got["P"], got["Q"][None])
-        return held["y"][b - 1]
-
     def low(far):
         return of_core(receiver[1], receiver[3]) if far else of_core(receiver[3], receiver[1])
 
@@ -215,19 +203,27 @@
     def back_y(steps):
         return [(i, i // 4 * 4 + (i % 4 - steps) % 4) for i in range(32)]
 
+    def nothing_like(*shapes):
+        return lambda *_: tuple(jnp.zeros(s + receiver.shape[1:], receiver.dtype) for s in shapes)
+
+    def one_x_step(receiver):
+        x6 = lax.ppermute(receiver[6], "src", back(lambda i: 4))
+        d = lax.ppermute(high(True), "src", [(i, (i - 4) % 16 ^ 1) for i in range(16)])
+        return x6, d
+
+    def core_step(receiver):
+        return (lax.ppermute(low(True), "src", [(i, i ^ 1) for i in range(16)]),)
+
+    x6, d = lax.cond(core < 2, one_x_step, nothing_like((), ()), receiver)
+    (cl,) = lax.cond(core < 2, core_step, nothing_like(()), receiver)
+    across_y = [(i, i // 4 * 4 + {0: 2, 2: 3}[i % 4]) for i in range(32) if i % 2 == 0]
+
     moves = {
-        "Cl": ("src", [(i, i ^ 1) for i in range(16)], lambda: low(True)),
-        "D": ("src", [(i, (i - 4) % 16 ^ 1) for i in range(16)], lambda: high(True)),
-        "X6": ("src", back(lambda i: 4), lambda: receiver[6]),
-        "X2": ("src", back(lambda i: 4), lambda: jnp.stack([receiver[4], high(False)])),
-        "O": ("src", back(lambda i: 3 - 2 * (i % 2)), lambda: jnp.stack([low(False), got["X2"][1]])),
-        "F": ("src", back(lambda i: 2), lambda: jnp.stack([receiver[2], got["X6"], got["Cl"], got["D"]])),
+        "F": ("src", back(lambda i: 2), lambda: jnp.stack([receiver[2], x6, cl, d])),
         "Z": ("rcv", back_z(1), lambda: lax.dynamic_slice_in_dim(source, 1 + place, 4, 0)),
-        "P": ("rcv", back_z(2, (0, 1)), lambda: lax.dynamic_slice_in_dim(source, jnp.minimum(5 + place, 6), 2, 0)),
-        "Q": ("rcv", back_z(2, (0, 2)), lambda: source[7]),
-        "Y1": ("rcv", back_y(1), lambda: pair(1)),
-        "Y2": ("rcv", back_y(2), lambda: pair(2)),
-        "Y3": ("rcv", back_y(3), lambda: pair(3)),
+        "P": ("rcv", back_z(2, (0, 1)), lambda: jnp.stack([jnp.where(place == 0, source[5], source[6]), source[7]])),
+        "W": ("rcv", across_y, lambda: jnp.where(place == 0, source[6], source[7])),
+        "Q": ("rcv", back_z(2, (2, 3)), lambda: got["W"]),
     }
     tied = []
     for act, name in PLAN:
@@ -240,10 +236,22 @@
             block, *arrived = lax.optimization_barrier((block, *[got[n] for n in tied]))
             got.update(zip(tied, arrived))
         got[name] = lax.ppermute(block, axis, route)
-    y1, y2, y3 = got["Y1"], got["Y2"], got["Y3"]
-    sources = [source[0], held["y"][3], of_core(y1[0], y3[0]), of_core(y1[1], y3[1])]
-    sources += [y2[0], y2[1], of_core(y3[0], y1[0]), of_core(y3[1], y1[1])]
-    acc, left = early(sources, [receiver[0], got["X2"][0], got["O"][0], got["O"][1]])
+
+    def along_y(place, source, receiver, z, p):
+        x2 = lax.ppermute(jnp.stack([receiver[4], high(False)]), "src", back(lambda i: 4))
+        one, two, three, four = pack(place, source, z, p)
+        pairs = [lax.ppermute(x, "rcv", back_y(b)) for b, x in ((1, one), (2, two), (3, three))]
+        near = jnp.stack([low(False), x2[1]])
+        near = lax.ppermute(near, "src", back(lambda i: 3 - 2 * (i % 2)))
+        return (*pairs, four, x2[0], near)
+
+    y1, y2, y3, four, x4, near = lax.cond(
+        core < 2, along_y, nothing_like((2,), (2,), (2,), (), (), (2,)), place, source, receiver, got["Z"], got["P"]
+    )
+    two, three = jnp.where(place == 2, got["Q"], y2[1]), jnp.where(place == 3, got["Q"], y3[1])
+    sources = [source[0], four, of_core(y1[0], y3[0]), of_core(y1[1], three)]
+    sources += [y2[0], two, of_core(y3[0], y1[0]), of_core(three, y1[1])]
+    acc, left = early(sources, [receiver[0], x4, near[0], near[1]])
     return late([got["F"]], acc, left, (groups * windows) ** (-0.5))
 
 

time: 129 us -> 126 us (0.977)
  the two profiles are of different devices: /device:TPU:65 before, /device:TPU:87 now
where the time goes in v3:
time: 126 us; the launch traced here: 125 us
  starting transfers between devices  70.1 us (56%)
  waiting for transfers between devices  20.9 us (17%)
  local copies, waits for them, and re-layouts  19 us (15%)
  Pallas kernels  9.19 us (7%)
  other arithmetic  5.65 us (4%)
    ppermute x5, starting transfers between devices, body(): got[name] = lax.ppermute(block, axis, route)  25.3 us
    ppermute x1, starting transfers between devices, along_y(): near = lax.ppermute(near, 'src', back(lambda i: 3 - 2 * (i % 2)))  23.9 us
    ppermute x5, waiting for transfers between devices, body(): got[name] = lax.ppermute(block, axis, route)  12.1 us
    cond x12, local copies, waits for them, and re-layouts  9.46 us
    ppermute x3, starting transfers between devices, along_y(): lax.ppermute(x, 'rcv', back_y(b))  9.37 us
    ppermute x1, waiting for transfers between devices, one_x_step(): lax.ppermute(high(True), 'src', [(i, (i - 4) % 16 ^ 1) for i in range(16)])  6.42 us
    pallas_call x1, Pallas kernels, early(): pl.pallas_call(functools.partial(early_kernel, len(sources)), out_shape=(...  4.77 us
    ppermute x1, starting transfers between devices, one_x_step(): lax.ppermute(high(True), 'src', [(i, (i - 4) % 16 ^ 1) for i in range(16)])  4.47 us
  transfers between devices with their start and end apart: 13, of which 6 were waited for; matrix products, arithmetic and copies ran while one was open for 17% of the time, Pallas kernels for 5%

profile of v3, /device:TPU:87, one launch (start us, length us, event | category | flops | bytes accessed | tf_op | source)
XLA Modules:
  0.0 125.1 jit_solution(15891642843688407902)
XLA Ops:
  0.0 2.2 %dynamic-slice_bitcast_fusion = bf16[4,23,2,8,256]{4,3,2,1,0:T(8,128)(2,1)} fusion(bf16[1,8,23,2,8,256]{5,4,3,2,1,0:T(8,128)(2,1)} %param.8, s32[]{:T(128)S(6)} %select_n.101), kind=kLoop, calls=%fused_computation.9 | loop fusion | bytes 1507332 | tf_op jit(solution)/shard_map/dynamic_slice | solution.py:223
  2.2 2.0 %collective-permute-start.8 = (bf16[4,23,2,8,256]{4,3,2,1,0:T(8,128)(2,1)}, bf16[4,23,2,8,256]{4,3,2,1,0:T(8,128)(2,1)}, u32[]{:S(2)}, u32[]{:S(2)}) collective-permute-start(bf16[4,23,2,8,256]{4,3,2,1,0:T(8,128)(2,1)} %dynamic-slice_bitcast_fusion), channel_id=1, source_target_pairs={{0,28},{1,29},{2,30},{3,31},{4,0},{5,1},{6,2},{7,3},{8,4},{9,5},{1... | collective-permute-start | bytes 2261000 | tf_op jit(solution)/shard_map/ppermute | solution.py:238
  4.2 0.1 slice_bitcast_fusion.3
  4.3 2.9 %collective-permute-start.10 = (bf16[23,2,8,256]{3,2,1,0:T(8,128)(2,1)S(1)}, bf16[23,2,8,256]{3,2,1,0:T(8,128)(2,1)}, u32[]{:S(2)}, u32[]{:S(2)}) collective-permute-start(bf16[23,2,8,256]{3,2,1,0:T(8,128)(2,1)S(1)} %get-tuple-element.117), channel_id=1, source_target_pairs={{0,2},{2,3},{4,6},{6,7},{8,10},{10,11},{12,14},{14,15},{16,18},{18... | collective-permute-start | bytes 565256 | tf_op jit(solution)/shard_map/ppermute | solution.py:238
  7.2 0.8 pad_maximum_fusion.3
  8.0 1.4 %collective-permute-start.9 = (bf16[2,23,2,8,256]{4,3,2,1,0:T(8,128)(2,1)}, bf16[2,23,2,8,256]{4,3,2,1,0:T(8,128)(2,1)}, u32[]{:S(2)}, u32[]{:S(2)}) collective-permute-start(bf16[2,23,2,8,256]{4,3,2,1,0:T(8,128)(2,1)} %pad_maximum_fusion.3), channel_id=1, source_target_pairs={{0,24},{1,25},{4,28},{5,29},{8,0},{9,1},{12,4},{13,5},{16,8},{17,9... | collective-permute-start | bytes 1130504 | tf_op jit(solution)/shard_map/ppermute | solution.py:238
  9.4 3.9 %collective-permute-done.10 = bf16[23,2,8,256]{3,2,1,0:T(8,128)(2,1)} collective-permute-done((bf16[23,2,8,256]{3,2,1,0:T(8,128)(2,1)S(1)}, bf16[23,2,8,256]{3,2,1,0:T(8,128)(2,1)}, u32[]{:S(2)}, u32[]{:S(2)}) %collective-permute-start.10) | collective-permute-done | bytes 188448 | tf_op jit(solution)/shard_map/ppermute | solution.py:238
  13.3 12.0 %collective-permute-start.11 = (bf16[23,2,8,256]{3,2,1,0:T(8,128)(2,1)}, bf16[23,2,8,256]{3,2,1,0:T(8,128)(2,1)}, u32[]{:S(2)}, u32[]{:S(2)}) collective-permute-start(bf16[23,2,8,256]{3,2,1,0:T(8,128)(2,1)} %collective-permute-done.10), channel_id=1, source_target_pairs={{2,26},{3,27},{6,30},{7,31},{10,2},{11,3},{14,6},{15,7},{18,10},{1... | collective-permute-start | bytes 565256 | tf_op jit(solution)/shard_map/ppermute | solution.py:238
  25.3 0.7 slice_bitcast_fusion.2
  26.0 14.4 %conditional.3 = (bf16[1,23,2,8,256]{4,3,2,1,0:T(8,128)(2,1)}, bf16[1,23,2,8,256]{4,3,2,1,0:T(8,128)(2,1)}) conditional(s32[]{:T(128)} %convert_element_type.2, () %tuple.42, (bf16[8,23,2,8,256]{4,3,2,1,0:T(8,128)(2,1)S(1)}, s32[]{:T(128)}) %tuple.72), branch_computations={%region_0.1_spmd, %region_1.2_spmd} | conditional | flops 94209 | bytes 2449514 | solution.py:217
  26.0 2.5 %collective-permute-start = (bf16[23,2,8,256]{3,2,1,0:T(8,128)(2,1)S(1)}, bf16[23,2,8,256]{3,2,1,0:T(8,128)(2,1)}, u32[]{:S(2)}, u32[]{:S(2)}) collective-permute-start(bf16[23,2,8,256]{3,2,1,0:T(8,128)(2,1)S(1)} %get-tuple-element.99), channel_id=1, source_target_pairs={{0,384},{32,416},{64,448},{96,480},{128,0},{160,32},{192,64},{224,... | collective-permute-start | bytes 565256 | tf_op jit(solution)/shard_map/cond/branch_1_fun/ppermute | solution.py:210
  28.5 4.5 %collective-permute-start.1 = (bf16[23,2,8,256]{3,2,1,0:T(8,128)(2,1)S(1)}, bf16[23,2,8,256]{3,2,1,0:T(8,128)(2,1)}, u32[]{:S(2)}, u32[]{:S(2)}) collective-permute-start(bf16[23,2,8,256]{3,2,1,0:T(8,128)(2,1)S(1)} %get-tuple-element.98), channel_id=1, source_target_pairs={{0,416},{32,384},{64,480},{96,448},{128,32},{160,0},{192,96},{224,... | collective-permute-start | bytes 565256 | tf_op jit(solution)/shard_map/cond/branch_1_fun/ppermute | solution.py:211
  33.0 1.0 collective-permute-done
  34.0 6.4 %collective-permute-done.1 = bf16[23,2,8,256]{3,2,1,0:T(8,128)(2,1)} collective-permute-done((bf16[23,2,8,256]{3,2,1,0:T(8,128)(2,1)S(1)}, bf16[23,2,8,256]{3,2,1,0:T(8,128)(2,1)}, u32[]{:S(2)}, u32[]{:S(2)}) %collective-permute-start.1) | collective-permute-done | bytes 188448 | tf_op jit(solution)/shard_map/cond/branch_1_fun/ppermute | solution.py:211
  40.4 3.7 %conditional.4 = (bf16[1,23,2,8,256]{4,3,2,1,0:T(8,128)(2,1)}) conditional(s32[]{:T(128)} %convert_element_type.2, () %tuple.44, (s32[]{:T(128)}, bf16[8,23,2,8,256]{4,3,2,1,0:T(8,128)(2,1)S(1)}) %tuple.73), branch_computations={%region_2.3_spmd, %region_3.4_spmd} | conditional | flops 94209 | bytes 1318970 | solution.py:218
  40.4 2.5 %collective-permute-start.2 = (bf16[23,2,8,256]{3,2,1,0:T(8,128)(2,1)S(1)}, bf16[23,2,8,256]{3,2,1,0:T(8,128)(2,1)}, u32[]{:S(2)}, u32[]{:S(2)}) collective-permute-start(bf16[23,2,8,256]{3,2,1,0:T(8,128)(2,1)S(1)} %select_bitcast_fusion.1), channel_id=1, source_target_pairs={{0,32},{32,0},{64,96},{96,64},{128,160},{160,128},{192,224},{224,1... | collective-permute-start | bytes 565256 | tf_op jit(solution)/shard_map/cond/branch_1_fun/ppermute | solution.py:215
  43.0 1.2 collective-permute-done.2
  44.1 1.3 %pad_maximum_fusion.2 = bf16[4,23,2,8,256]{4,3,2,1,0:T(8,128)(2,1)S(1)} fusion(bf16[1,23,2,8,256]{4,3,2,1,0:T(8,128)(2,1)} %get-tuple-element.81, bf16[1,23,2,8,256]{4,3,2,1,0:T(8,128)(2,1)} %get-tuple-element.172, bf16[1,23,2,8,256]{4,3,2,1,0:T(8,128)(2,1)} %get-tuple-element.80, bf16[1,23,2,8,256]{4,3,2,1,0:T(8,128)(2,1)} %get-tuple-element.114), kind=kLoop, calls=%fused_computation.8 | loop fusion | flops 1130496 | bytes 1507328 | tf_op jit(solution)/shard_map/stack | solution.py:222
  45.5 6.9 %collective-permute-start.12 = (bf16[4,23,2,8,256]{4,3,2,1,0:T(8,128)(2,1)S(1)}, bf16[4,23,2,8,256]{4,3,2,1,0:T(8,128)(2,1)S(1)}, u32[]{:S(2)}, u32[]{:S(2)}) collective-permute-start(bf16[4,23,2,8,256]{4,3,2,1,0:T(8,128)(2,1)S(1)} %pad_maximum_fusion.2), channel_id=1, source_target_pairs={{0,448},{32,480},{64,0},{96,32},{128,64},{160,96},{192,128},{224,1... | collective-permute-start | bytes 2261000 | tf_op jit(solution)/shard_map/ppermute | solution.py:238
  52.4 54.6 %conditional.5 = (bf16[2,23,2,8,256]{4,3,2,1,0:T(8,128)(2,1)}, bf16[2,23,2,8,256]{4,3,2,1,0:T(8,128)(2,1)}, bf16[2,23,2,8,256]{4,3,2,1,0:T(8,128)(2,1)}, bf16[23...) conditional(s32[]{:T(128)} %convert_element_type.2, () %tuple.47, ...), branch_computations={%region_4.5_spmd, %region_5.6_spmd} | conditional | flops 566249 | bytes 20350370 | solution.py:248
  52.4 1.3 %slice_select_fusion = (bf16[1,23,2,8,256]{4,3,2,1,0:T(8,128)(2,1)S(1)}, bf16[1,23,2,8,256]{4,3,2,1,0:T(8,128)(2,1)S(1)}, bf16[1,23,2,8,256]{4,3,2,1,0:T(8,128)(2,1)S(1)}) fusion(bf16[8,23,2,8,256]{4,3,2,1,0:T(8,128)(2,1)} %get-tuple-element.60, pred[]{:T(512)S(6)} %eq.16), kind=kLoop, calls=%fused_computation.6 | loop fusion | flops 188416 | bytes 1507329 | tf_op jit(solution)/shard_map/cond/branch_1_fun/jit(_where)/select_n | solution.py:189
  53.8 2.2 %collective-permute-start.6 = (bf16[2,23,2,8,256]{4,3,2,1,0:T(8,128)(2,1)S(1)}, bf16[2,23,2,8,256]{4,3,2,1,0:T(8,128)(2,1)S(1)}, u32[]{:S(2)}, u32[]{:S(2)}) collective-permute-start(bf16[2,23,2,8,256]{4,3,2,1,0:T(8,128)(2,1)S(1)} %pad_maximum_fusion), channel_id=1, source_target_pairs={{0,384},{32,416},{64,448},{96,480},{128,0},{160,32},{192,64},{224,... | collective-permute-start | bytes 1130504 | tf_op jit(solution)/shard_map/cond/branch_1_fun/ppermute | solution.py:241
  56.0 2.0 %branch_1_fun.1 = (bf16[2,23,2,8,256]{4,3,2,1,0:T(8,128)(2,1)S(1)}, bf16[2,23,2,8,256]{4,3,2,1,0:T(8,128)(2,1)S(1)}, bf16[2,23,2,8,256]{4,3,2,1,0:T(8,128)(2,1)S(1)}, bf16[23,2,8,256]{3,2,1,0:T(8,128)(2,1)}) custom-call(s32[1,1]{1,0:T(1,128)} %bitcast.6.place_ref, bf16[8,23,2,8,256]{4,3,2,1,0:T(8,128)(2,1)S(1)} %bitcast.36, ...), custom_call_target="tpu_custom_call" | custom-call | flops 1000 | bytes 1000 | tf_op jit(solution)/shard_map/cond/branch_1_fun/pallas_call | solution.py:159
  58.0 3.7 %collective-permute-start.3 = (bf16[2,23,2,8,256]{4,3,2,1,0:T(8,128)(2,1)S(1)}, bf16[2,23,2,8,256]{4,3,2,1,0:T(8,128)(2,1)S(1)}, u32[]{:S(2)}, u32[]{:S(2)}) collective-permute-start(bf16[2,23,2,8,256]{4,3,2,1,0:T(8,128)(2,1)S(1)} %get-tuple-element.56), channel_id=1, source_target_pairs={{0,3},{1,0},{2,1},{3,2},{4,7},{5,4},{6,5},{7,6},{8,11},{9,8},{10,9... | collective-permute-start | bytes 1130504 | tf_op jit(solution)/shard_map/cond/branch_1_fun/ppermute | solution.py:243
  61.7 1.9 %collective-permute-start.4 = (bf16[2,23,2,8,256]{4,3,2,1,0:T(8,128)(2,1)S(1)}, bf16[2,23,2,8,256]{4,3,2,1,0:T(8,128)(2,1)S(1)}, u32[]{:S(2)}, u32[]{:S(2)}) collective-permute-start(bf16[2,23,2,8,256]{4,3,2,1,0:T(8,128)(2,1)S(1)} %get-tuple-element.57), channel_id=1, source_target_pairs={{0,2},{1,3},{2,0},{3,1},{4,6},{5,7},{6,4},{7,5},{8,10},{9,11},{10,... | collective-permute-start | bytes 1130504 | tf_op jit(solution)/shard_map/cond/branch_1_fun/ppermute | solution.py:243
  63.6 3.8 %collective-permute-start.5 = (bf16[2,23,2,8,256]{4,3,2,1,0:T(8,128)(2,1)S(1)}, bf16[2,23,2,8,256]{4,3,2,1,0:T(8,128)(2,1)}, u32[]{:S(2)}, u32[]{:S(2)}) collective-permute-start(bf16[2,23,2,8,256]{4,3,2,1,0:T(8,128)(2,1)S(1)} %get-tuple-element.58), channel_id=1, source_target_pairs={{0,1},{1,2},{2,3},{3,0},{4,5},{5,6},{6,7},{7,4},{8,9},{9,10},{10,1... | collective-permute-start | bytes 1130504 | tf_op jit(solution)/shard_map/cond/branch_1_fun/ppermute | solution.py:243
  67.4 0.2 collective-permute-done.6
  67.6 0.7 fusion.4
  68.4 23.9 %collective-permute-start.7 = (bf16[2,23,2,8,256]{4,3,2,1,0:T(8,128)(2,1)S(1)}, bf16[2,23,2,8,256]{4,3,2,1,0:T(8,128)(2,1)}, u32[]{:S(2)}, u32[]{:S(2)}) collective-permute-start(bf16[2,23,2,8,256]{4,3,2,1,0:T(8,128)(2,1)S(1)} %pad_maximum_fusion.1), channel_id=1, source_target_pairs={{0,416},{32,0},{64,480},{96,64},{128,32},{160,128},{192,96},{224,1... | collective-permute-start | bytes 1130504 | tf_op jit(solution)/shard_map/cond/branch_1_fun/ppermute | solution.py:245
  92.2 0.8 fusion.3
  93.1 1.6 %copy.39 = bf16[23,2,8,256]{3,2,1,0:T(8,128)(2,1)} copy(bf16[23,2,8,256]{3,2,1,0:T(8,128)(2,1)} %bitcast.9) | data formatting | bytes 376832 | tf_op jit(solution)/shard_map/cond
  94.7 0.9 copy.40
  95.6 0.8 fusion.2
  96.5 1.6 %copy.43 = bf16[23,2,8,256]{3,2,1,0:T(8,128)(2,1)} copy(bf16[23,2,8,256]{3,2,1,0:T(8,128)(2,1)} %bitcast.11) | data formatting | bytes 376832 | tf_op jit(solution)/shard_map/cond
  98.1 0.9 copy.44
  99.0 1.8 %fusion.1 = (bf16[1,23,2,8,256]{4,3,2,1,0:T(8,128)(2,1)}, bf16[1,23,2,8,256]{4,3,2,1,0:T(8,128)(2,1)}) fusion(bf16[2,23,2,8,256]{4,3,2,1,0:T(8,128)(2,1)} %collective-permute-done.5), kind=kLoop, calls=%fused_computation.24 | loop fusion | bytes 753664 | tf_op jit(solution)/shard_map/slice | solution.py:251
  100.8 1.6 %copy.47 = bf16[23,2,8,256]{3,2,1,0:T(8,128)(2,1)} copy(bf16[23,2,8,256]{3,2,1,0:T(8,128)(2,1)} %bitcast.13) | data formatting | bytes 376832 | tf_op jit(solution)/shard_map/cond
  102.4 0.9 copy.48
  103.3 1.8 %fusion = (bf16[1,23,2,8,256]{4,3,2,1,0:T(8,128)(2,1)}, bf16[1,23,2,8,256]{4,3,2,1,0:T(8,128)(2,1)}) fusion(bf16[2,23,2,8,256]{4,3,2,1,0:T(8,128)(2,1)} %collective-permute-done.7), kind=kLoop, calls=%fused_computation.23 | loop fusion | bytes 753664 | tf_op jit(solution)/shard_map/slice | solution.py:254
  105.1 0.9 copy.51
  106.1 0.9 copy.52
  107.0 0.7 copy-done.4
  107.7 0.1 copy-done.6
  107.7 1.1 broadcast_select_fusion.3
  108.8 1.0 broadcast_select_fusion.2
  109.8 4.8 %shard_map.28 = (f32[8,512,256]{2,1,0:T(8,128)S(1)}, bf16[8,512,184]{2,1,0:T(8,128)(2,1)S(1)}) custom-call(bf16[23,2,8,256]{3,2,1,0:T(8,128)(2,1)S(1)} %get-tuple-element.115.refs_0_, bf16[23,2,8,256]{3,2,1,0:T(8,128)(2,1)} %get-tuple-element.85.refs_1_, bf16[23,2,8,256]{3,2,1,0:T(8,128)(2,1)S(1)} %get-tuple-element.122.refs_2_, ...), custom_call_target="tpu_custom_call" | custom-call | flops 1000000 | bytes 1000000 | tf_op jit(solution)/shard_map/pallas_call | solution.py:95
  114.6 8.2 %collective-permute-done.12.refs_0_ = bf16[4,23,2,8,256]{4,3,2,1,0:T(8,128)(2,1)S(1)} collective-permute-done((bf16[4,23,2,8,256]{4,3,2,1,0:T(8,128)(2,1)S(1)}, bf16[4,23,2,8,256]{4,3,2,1,0:T(8,128)(2,1)S(1)}, u32[]{:S(2)}, u32[]{:S(2)}) %collective-permute-start.12) | collective-permute-done | bytes 753696 | tf_op jit(solution)/shard_map/ppermute | solution.py:238
  122.8 2.4 %shard_map.29 = bf16[2,8,256,256]{3,2,1,0:T(8,128)(2,1)} custom-call(bf16[4,23,2,8,256]{4,3,2,1,0:T(8,128)(2,1)S(1)} %collective-permute-done.12.refs_0_, f32[8,512,256]{2,1,0:T(8,128)S(1)} %get-tuple-element.96.refs_1_, bf16[8,512,184]{2,1,0:T(8,128)(2,1)S(1)} %get-tuple-element.97.refs_2_), custom_call_target="tpu_custom_call" | custom-call | flops 200000000 | bytes 9000000 | tf_op jit(solution)/shard_map/pallas_call | solution.py:117
  (25 shorter events, 0.2 us)
Async XLA Ops:
  0.0 4.2 %copy-start = (bf16[1,8,23,2,8,256]{5,4,3,2,1,0:T(8,128)(2,1)S(1)}, bf16[1,8,23,2,8,256]{5,4,3,2,1,0:T(8,128)(2,1)}, u32[]{:S(2)}) copy-start(bf16[1,8,23,2,8,256]{5,4,3,2,1,0:T(8,128)(2,1)} %param.8) | copy-start | bytes 4521988
  2.2 23.1 %copy-start.1 = (bf16[1,8,23,2,8,256]{5,4,3,2,1,0:T(8,128)(2,1)S(1)}, bf16[1,8,23,2,8,256]{5,4,3,2,1,0:T(8,128)(2,1)}, u32[]{:S(2)}) copy-start(bf16[1,8,23,2,8,256]{5,4,3,2,1,0:T(8,128)(2,1)} %param.9) | copy-start | bytes 4521988
  2.2 43.3 %collective-permute-start.8 = (bf16[4,23,2,8,256]{4,3,2,1,0:T(8,128)(2,1)}, bf16[4,23,2,8,256]{4,3,2,1,0:T(8,128)(2,1)}, u32[]{:S(2)}, u32[]{:S(2)}) collective-permute-start(bf16[4,23,2,8,256]{4,3,2,1,0:T(8,128)(2,1)} %dynamic-slice_bitcast_fusion), channel_id=1, source_target_pairs={{0,28},{1,29},{2,30},{3,31},{4,0},{5,1},{6,2},{7,3},{8,4},{9,5},{1... | collective-permute-start | bytes 2261000 | tf_op jit(solution)/shard_map/ppermute | solution.py:238
  4.3 9.0 %collective-permute-start.10 = (bf16[23,2,8,256]{3,2,1,0:T(8,128)(2,1)S(1)}, bf16[23,2,8,256]{3,2,1,0:T(8,128)(2,1)}, u32[]{:S(2)}, u32[]{:S(2)}) collective-permute-start(bf16[23,2,8,256]{3,2,1,0:T(8,128)(2,1)S(1)} %get-tuple-element.117), channel_id=1, source_target_pairs={{0,2},{2,3},{4,6},{6,7},{8,10},{10,11},{12,14},{14,15},{16,18},{18... | collective-permute-start | bytes 565256 | tf_op jit(solution)/shard_map/ppermute | solution.py:238
  8.0 37.5 %collective-permute-start.9 = (bf16[2,23,2,8,256]{4,3,2,1,0:T(8,128)(2,1)}, bf16[2,23,2,8,256]{4,3,2,1,0:T(8,128)(2,1)}, u32[]{:S(2)}, u32[]{:S(2)}) collective-permute-start(bf16[2,23,2,8,256]{4,3,2,1,0:T(8,128)(2,1)} %pad_maximum_fusion.3), channel_id=1, source_target_pairs={{0,24},{1,25},{4,28},{5,29},{8,0},{9,1},{12,4},{13,5},{16,8},{17,9... | collective-permute-start | bytes 1130504 | tf_op jit(solution)/shard_map/ppermute | solution.py:238
  13.3 32.2 %collective-permute-start.11 = (bf16[23,2,8,256]{3,2,1,0:T(8,128)(2,1)}, bf16[23,2,8,256]{3,2,1,0:T(8,128)(2,1)}, u32[]{:S(2)}, u32[]{:S(2)}) collective-permute-start(bf16[23,2,8,256]{3,2,1,0:T(8,128)(2,1)} %collective-permute-done.10), channel_id=1, source_target_pairs={{2,26},{3,27},{6,30},{7,31},{10,2},{11,3},{14,6},{15,7},{18,10},{1... | collective-permute-start | bytes 565256 | tf_op jit(solution)/shard_map/ppermute | solution.py:238
  26.0 7.9 %collective-permute-start = (bf16[23,2,8,256]{3,2,1,0:T(8,128)(2,1)S(1)}, bf16[23,2,8,256]{3,2,1,0:T(8,128)(2,1)}, u32[]{:S(2)}, u32[]{:S(2)}) collective-permute-start(bf16[23,2,8,256]{3,2,1,0:T(8,128)(2,1)S(1)} %get-tuple-element.99), channel_id=1, source_target_pairs={{0,384},{32,416},{64,448},{96,480},{128,0},{160,32},{192,64},{224,... | collective-permute-start | bytes 565256 | tf_op jit(solution)/shard_map/cond/branch_1_fun/ppermute | solution.py:210
  28.5 11.9 %collective-permute-start.1 = (bf16[23,2,8,256]{3,2,1,0:T(8,128)(2,1)S(1)}, bf16[23,2,8,256]{3,2,1,0:T(8,128)(2,1)}, u32[]{:S(2)}, u32[]{:S(2)}) collective-permute-start(bf16[23,2,8,256]{3,2,1,0:T(8,128)(2,1)S(1)} %get-tuple-element.98), channel_id=1, source_target_pairs={{0,416},{32,384},{64,480},{96,448},{128,32},{160,0},{192,96},{224,... | collective-permute-start | bytes 565256 | tf_op jit(solution)/shard_map/cond/branch_1_fun/ppermute | solution.py:211
  40.4 3.7 %collective-permute-start.2 = (bf16[23,2,8,256]{3,2,1,0:T(8,128)(2,1)S(1)}, bf16[23,2,8,256]{3,2,1,0:T(8,128)(2,1)}, u32[]{:S(2)}, u32[]{:S(2)}) collective-permute-start(bf16[23,2,8,256]{3,2,1,0:T(8,128)(2,1)S(1)} %select_bitcast_fusion.1), channel_id=1, source_target_pairs={{0,32},{32,0},{64,96},{96,64},{128,160},{160,128},{192,224},{224,1... | collective-permute-start | bytes 565256 | tf_op jit(solution)/shard_map/cond/branch_1_fun/ppermute | solution.py:215
  45.5 77.3 %collective-permute-start.12 = (bf16[4,23,2,8,256]{4,3,2,1,0:T(8,128)(2,1)S(1)}, bf16[4,23,2,8,256]{4,3,2,1,0:T(8,128)(2,1)S(1)}, u32[]{:S(2)}, u32[]{:S(2)}) collective-permute-start(bf16[4,23,2,8,256]{4,3,2,1,0:T(8,128)(2,1)S(1)} %pad_maximum_fusion.2), channel_id=1, source_target_pairs={{0,448},{32,480},{64,0},{96,32},{128,64},{160,96},{192,128},{224,1... | collective-permute-start | bytes 2261000 | tf_op jit(solution)/shard_map/ppermute | solution.py:238
  53.8 13.8 %collective-permute-start.6 = (bf16[2,23,2,8,256]{4,3,2,1,0:T(8,128)(2,1)S(1)}, bf16[2,23,2,8,256]{4,3,2,1,0:T(8,128)(2,1)S(1)}, u32[]{:S(2)}, u32[]{:S(2)}) collective-permute-start(bf16[2,23,2,8,256]{4,3,2,1,0:T(8,128)(2,1)S(1)} %pad_maximum_fusion), channel_id=1, source_target_pairs={{0,384},{32,416},{64,448},{96,480},{128,0},{160,32},{192,64},{224,... | collective-permute-start | bytes 1130504 | tf_op jit(solution)/shard_map/cond/branch_1_fun/ppermute | solution.py:241
  58.0 34.2 %collective-permute-start.3 = (bf16[2,23,2,8,256]{4,3,2,1,0:T(8,128)(2,1)S(1)}, bf16[2,23,2,8,256]{4,3,2,1,0:T(8,128)(2,1)S(1)}, u32[]{:S(2)}, u32[]{:S(2)}) collective-permute-start(bf16[2,23,2,8,256]{4,3,2,1,0:T(8,128)(2,1)S(1)} %get-tuple-element.56), channel_id=1, source_target_pairs={{0,3},{1,0},{2,1},{3,2},{4,7},{5,4},{6,5},{7,6},{8,11},{9,8},{10,9... | collective-permute-start | bytes 1130504 | tf_op jit(solution)/shard_map/cond/branch_1_fun/ppermute | solution.py:243
  61.7 33.9 %collective-permute-start.4 = (bf16[2,23,2,8,256]{4,3,2,1,0:T(8,128)(2,1)S(1)}, bf16[2,23,2,8,256]{4,3,2,1,0:T(8,128)(2,1)S(1)}, u32[]{:S(2)}, u32[]{:S(2)}) collective-permute-start(bf16[2,23,2,8,256]{4,3,2,1,0:T(8,128)(2,1)S(1)} %get-tuple-element.57), channel_id=1, source_target_pairs={{0,2},{1,3},{2,0},{3,1},{4,6},{5,7},{6,4},{7,5},{8,10},{9,11},{10,... | collective-permute-start | bytes 1130504 | tf_op jit(solution)/shard_map/cond/branch_1_fun/ppermute | solution.py:243
  63.6 35.4 %collective-permute-start.5 = (bf16[2,23,2,8,256]{4,3,2,1,0:T(8,128)(2,1)S(1)}, bf16[2,23,2,8,256]{4,3,2,1,0:T(8,128)(2,1)}, u32[]{:S(2)}, u32[]{:S(2)}) collective-permute-start(bf16[2,23,2,8,256]{4,3,2,1,0:T(8,128)(2,1)S(1)} %get-tuple-element.58), channel_id=1, source_target_pairs={{0,1},{1,2},{2,3},{3,0},{4,5},{5,6},{6,7},{7,4},{8,9},{9,10},{10,1... | collective-permute-start | bytes 1130504 | tf_op jit(solution)/shard_map/cond/branch_1_fun/ppermute | solution.py:243
  68.4 35.0 %collective-permute-start.7 = (bf16[2,23,2,8,256]{4,3,2,1,0:T(8,128)(2,1)S(1)}, bf16[2,23,2,8,256]{4,3,2,1,0:T(8,128)(2,1)}, u32[]{:S(2)}, u32[]{:S(2)}) collective-permute-start(bf16[2,23,2,8,256]{4,3,2,1,0:T(8,128)(2,1)S(1)} %pad_maximum_fusion.1), channel_id=1, source_target_pairs={{0,416},{32,0},{64,480},{96,64},{128,32},{160,128},{192,96},{224,1... | collective-permute-start | bytes 1130504 | tf_op jit(solution)/shard_map/cond/branch_1_fun/ppermute | solution.py:245
  92.2 6.8 %copy-start.2 = (bf16[2,23,2,8,256]{4,3,2,1,0:T(8,128)(2,1)}, bf16[2,23,2,8,256]{4,3,2,1,0:T(8,128)(2,1)S(1)}, u32[]{:S(2)}) copy-start(bf16[2,23,2,8,256]{4,3,2,1,0:T(8,128)(2,1)S(1)} %collective-permute-done.3) | copy-start | bytes 1130500 | tf_op jit(solution)/shard_map/cond
  95.6 7.7 %copy-start.3 = (bf16[2,23,2,8,256]{4,3,2,1,0:T(8,128)(2,1)}, bf16[2,23,2,8,256]{4,3,2,1,0:T(8,128)(2,1)S(1)}, u32[]{:S(2)}) copy-start(bf16[2,23,2,8,256]{4,3,2,1,0:T(8,128)(2,1)S(1)} %collective-permute-done.4) | copy-start | bytes 1130500 | tf_op jit(solution)/shard_map/cond
  107.0 0.7 copy-start.4
  107.0 0.7 copy-start.6
  107.7 2.1 %copy-start.5 = (bf16[23,2,8,256]{3,2,1,0:T(8,128)(2,1)S(1)}, bf16[23,2,8,256]{3,2,1,0:T(8,128)(2,1)}, u32[]{:S(2)}) copy-start(bf16[23,2,8,256]{3,2,1,0:T(8,128)(2,1)} %copy-done.4) | copy-start | bytes 565252
  107.7 2.1 %copy-start.7 = (bf16[23,2,8,256]{3,2,1,0:T(8,128)(2,1)S(1)}, bf16[23,2,8,256]{3,2,1,0:T(8,128)(2,1)}, u32[]{:S(2)}) copy-start(bf16[23,2,8,256]{3,2,1,0:T(8,128)(2,1)} %copy-done.6) | copy-start | bytes 565252

commit v4 on v3

--- a/solution.py
+++ b/solution.py
@@ -209,13 +209,11 @@
     def one_x_step(receiver):
         x6 = lax.ppermute(receiver[6], "src", back(lambda i: 4))
         d = lax.ppermute(high(True), "src", [(i, (i - 4) % 16 ^ 1) for i in range(16)])
-        return x6, d
-
-    def core_step(receiver):
-        return (lax.ppermute(low(True), "src", [(i, i ^ 1) for i in range(16)]),)
-
-    x6, d = lax.cond(core < 2, one_x_step, nothing_like((), ()), receiver)
-    (cl,) = lax.cond(core < 2, core_step, nothing_like(()), receiver)
+        first, x6 = lax.optimization_barrier((low(True), x6))
+        cl = lax.ppermute(first, "src", [(i, i ^ 1) for i in range(16)])
+        return x6, d, cl
+
+    x6, d, cl = lax.cond(core < 2, one_x_step, nothing_like((), (), ()), receiver)
     across_y = [(i, i // 4 * 4 + {0: 2, 2: 3}[i % 4]) for i in range(32) if i % 2 == 0]
 
     moves = {

time: 126 us -> 125 us (level)
  waiting for transfers between devices: 20.9 us -> 14 us
  starting transfers between devices: 70.1 us -> 73.3 us
  other arithmetic: 5.65 us -> 7.97 us
    ppermute x1, waiting for transfers between devices: 6.42 us -> 1.52 us  [one_x_step(): lax.ppermute(high(True), 'src', [(i, (i - 4) % 16 ^ 1) for i in range(16)])]
    ppermute x1, starting transfers between devices: 2.52 us -> 5.19 us  [one_x_step(): cl = lax.ppermute(first, 'src', [(i, i ^ 1) for i in range(16)])]
    cond x12 -> x16, local copies, waits for them, and re-layouts: 9.46 us -> 11.1 us
    select_n x5 -> x4, other arithmetic: 3.45 us -> 4.88 us  [of_core(): return jnp.where(core == 0, zero, one)]
  transfers between devices with their start and end apart: 13 -> 13, of which waited for: 6 -> 4; matrix products, arithmetic and copies ran while one was open for 17% -> 21% of each run, Pallas kernels for 5% -> 5%
where the time goes in v4:
time: 125 us; the launch traced here: 124 us
  starting transfers between devices  73.3 us (59%)
  local copies, waits for them, and re-layouts  19.3 us (15%)
  waiting for transfers between devices  14 us (11%)
  Pallas kernels  8.97 us (7%)
  other arithmetic  7.97 us (6%)
    ppermute x5, starting transfers between devices, body(): got[name] = lax.ppermute(block, axis, route)  25.4 us
    ppermute x1, starting transfers between devices, along_y(): near = lax.ppermute(near, 'src', back(lambda i: 3 - 2 * (i % 2)))  24.1 us
    ppermute x5, waiting for transfers between devices, body(): got[name] = lax.ppermute(block, axis, route)  11.8 us
    cond x16, local copies, waits for them, and re-layouts  11.1 us
    ppermute x3, starting transfers between devices, along_y(): lax.ppermute(x, 'rcv', back_y(b))  9.53 us
    ppermute x1, starting transfers between devices, one_x_step(): cl = lax.ppermute(first, 'src', [(i, i ^ 1) for i in range(16)])  5.19 us
    select_n x4, other arithmetic, of_core(): return jnp.where(core == 0, zero, one)  4.88 us
    pallas_call x1, Pallas kernels, early(): pl.pallas_call(functools.partial(early_kernel, len(sources)), out_shape=(...  4.78 us
  transfers between devices with their start and end apart: 13, of which 4 were waited for; matrix products, arithmetic and copies ran while one was open for 21% of the time, Pallas kernels for 5%

profile of v4, /device:TPU:87, one launch (start us, length us, event | category | flops | bytes accessed | tf_op | source)
XLA Modules:
  0.0 123.7 jit_solution(11193744153557166813)
XLA Ops:
  0.0 1.3 %dynamic-slice_bitcast_fusion = bf16[4,23,2,8,256]{4,3,2,1,0:T(8,128)(2,1)S(1)} fusion(bf16[1,8,23,2,8,256]{5,4,3,2,1,0:T(8,128)(2,1)} %param.6, s32[]{:T(128)S(6)} %select_n.99), kind=kLoop, calls=%fused_computation.9 | loop fusion | bytes 1507332 | tf_op jit(solution)/shard_map/dynamic_slice | solution.py:221
  1.3 1.9 %collective-permute-start.8 = (bf16[4,23,2,8,256]{4,3,2,1,0:T(8,128)(2,1)S(1)}, bf16[4,23,2,8,256]{4,3,2,1,0:T(8,128)(2,1)S(1)}, u32[]{:S(2)}, u32[]{:S(2)}) collective-permute-start(bf16[4,23,2,8,256]{4,3,2,1,0:T(8,128)(2,1)S(1)} %dynamic-slice_bitcast_fusion), channel_id=1, source_target_pairs={{0,28},{1,29},{2,30},{3,31},{4,0},{5,1},{6,2},{7,3},{8,4},{9,5},{1... | collective-permute-start | bytes 2261000 | tf_op jit(solution)/shard_map/ppermute | solution.py:236
  3.2 0.1 slice_bitcast_fusion.3
  3.3 2.9 %collective-permute-start.10 = (bf16[23,2,8,256]{3,2,1,0:T(8,128)(2,1)S(1)}, bf16[23,2,8,256]{3,2,1,0:T(8,128)(2,1)}, u32[]{:S(2)}, u32[]{:S(2)}) collective-permute-start(bf16[23,2,8,256]{3,2,1,0:T(8,128)(2,1)S(1)} %get-tuple-element.113), channel_id=1, source_target_pairs={{0,2},{2,3},{4,6},{6,7},{8,10},{10,11},{12,14},{14,15},{16,18},{18... | collective-permute-start | bytes 565256 | tf_op jit(solution)/shard_map/ppermute | solution.py:236
  6.2 0.8 pad_maximum_fusion.3
  7.0 1.4 %collective-permute-start.9 = (bf16[2,23,2,8,256]{4,3,2,1,0:T(8,128)(2,1)}, bf16[2,23,2,8,256]{4,3,2,1,0:T(8,128)(2,1)}, u32[]{:S(2)}, u32[]{:S(2)}) collective-permute-start(bf16[2,23,2,8,256]{4,3,2,1,0:T(8,128)(2,1)} %pad_maximum_fusion.3), channel_id=1, source_target_pairs={{0,24},{1,25},{4,28},{5,29},{8,0},{9,1},{12,4},{13,5},{16,8},{17,9... | collective-permute-start | bytes 1130504 | tf_op jit(solution)/shard_map/ppermute | solution.py:236
  8.4 3.9 %collective-permute-done.10 = bf16[23,2,8,256]{3,2,1,0:T(8,128)(2,1)} collective-permute-done((bf16[23,2,8,256]{3,2,1,0:T(8,128)(2,1)S(1)}, bf16[23,2,8,256]{3,2,1,0:T(8,128)(2,1)}, u32[]{:S(2)}, u32[]{:S(2)}) %collective-permute-start.10) | collective-permute-done | bytes 188448 | tf_op jit(solution)/shard_map/ppermute | solution.py:236
  12.3 12.0 %collective-permute-start.11 = (bf16[23,2,8,256]{3,2,1,0:T(8,128)(2,1)}, bf16[23,2,8,256]{3,2,1,0:T(8,128)(2,1)}, u32[]{:S(2)}, u32[]{:S(2)}) collective-permute-start(bf16[23,2,8,256]{3,2,1,0:T(8,128)(2,1)} %collective-permute-done.10), channel_id=1, source_target_pairs={{2,26},{3,27},{6,30},{7,31},{10,2},{11,3},{14,6},{15,7},{18,10},{1... | collective-permute-start | bytes 565256 | tf_op jit(solution)/shard_map/ppermute | solution.py:236
  24.3 1.7 %slice_bitcast_fusion.2 = (bf16[23,2,8,256]{3,2,1,0:T(8,128)(2,1)S(1)}, bf16[1,23,2,8,256]{4,3,2,1,0:T(8,128)(2,1)}) fusion(bf16[1,8,23,2,8,256]{5,4,3,2,1,0:T(8,128)(2,1)} %param.7), kind=kLoop, calls=%fused_computation.11 | loop fusion | bytes 753664 | tf_op jit(solution)/shard_map/squeeze | solution.py:252
  26.0 15.7 %conditional.2 = (bf16[1,23,2,8,256]{4,3,2,1,0:T(8,128)(2,1)}, bf16[1,23,2,8,256]{4,3,2,1,0:T(8,128)(2,1)}, bf16[1,23,2,8,256]{4,3,2,1,0:T(8,128)(2,1)}) conditional(s32[]{:T(128)} %convert_element_type.4, () %tuple.37, (s32[]{:T(128)}, bf16[8,23,2,8,256]{4,3,2,1,0:T(8,128)(2,1)}) %tuple.63), branch_computations={%region_0.1_spmd, %region_1.2_spmd} | conditional | flops 188417 | bytes 3768474 | solution.py:216
  26.0 1.3 %select_bitcast_fusion = (bf16[23,2,8,256]{3,2,1,0:T(8,128)(2,1)S(1)}, bf16[23,2,8,256]{3,2,1,0:T(8,128)(2,1)S(1)}, bf16[23,2,8,256]{3,2,1,0:T(8,128)(2,1)S(1)}) fusion(bf16[8,23,2,8,256]{4,3,2,1,0:T(8,128)(2,1)} %get-tuple-element.42, pred[]{:T(512)S(6)} %eq.13), kind=kLoop, calls=%fused_computation | loop fusion | flops 188416 | bytes 1507329 | tf_op jit(solution)/shard_map/cond/branch_1_fun/jit(_where)/select_n | solution.py:189
  27.3 2.5 %collective-permute-start = (bf16[23,2,8,256]{3,2,1,0:T(8,128)(2,1)S(1)}, bf16[23,2,8,256]{3,2,1,0:T(8,128)(2,1)}, u32[]{:S(2)}, u32[]{:S(2)}) collective-permute-start(bf16[23,2,8,256]{3,2,1,0:T(8,128)(2,1)S(1)} %get-tuple-element.94), channel_id=1, source_target_pairs={{0,384},{32,416},{64,448},{96,480},{128,0},{160,32},{192,64},{224,... | collective-permute-start | bytes 565256 | tf_op jit(solution)/shard_map/cond/branch_1_fun/ppermute | solution.py:210
  29.8 4.5 %collective-permute-start.1 = (bf16[23,2,8,256]{3,2,1,0:T(8,128)(2,1)S(1)}, bf16[23,2,8,256]{3,2,1,0:T(8,128)(2,1)}, u32[]{:S(2)}, u32[]{:S(2)}) collective-permute-start(bf16[23,2,8,256]{3,2,1,0:T(8,128)(2,1)S(1)} %get-tuple-element.93), channel_id=1, source_target_pairs={{0,416},{32,384},{64,480},{96,448},{128,32},{160,0},{192,96},{224,... | collective-permute-start | bytes 565256 | tf_op jit(solution)/shard_map/cond/branch_1_fun/ppermute | solution.py:211
  34.3 0.7 collective-permute-done
  35.0 5.2 %collective-permute-start.2 = (bf16[23,2,8,256]{3,2,1,0:T(8,128)(2,1)S(1)}, bf16[23,2,8,256]{3,2,1,0:T(8,128)(2,1)}, u32[]{:S(2)}, u32[]{:S(2)}) collective-permute-start(bf16[23,2,8,256]{3,2,1,0:T(8,128)(2,1)S(1)} %get-tuple-element.44), channel_id=1, source_target_pairs={{0,32},{32,0},{64,96},{96,64},{128,160},{160,128},{192,224},{224,1... | collective-permute-start | bytes 565256 | tf_op jit(solution)/shard_map/cond/branch_1_fun/ppermute | solution.py:213
  40.2 1.5 %collective-permute-done.1 = bf16[23,2,8,256]{3,2,1,0:T(8,128)(2,1)} collective-permute-done((bf16[23,2,8,256]{3,2,1,0:T(8,128)(2,1)S(1)}, bf16[23,2,8,256]{3,2,1,0:T(8,128)(2,1)}, u32[]{:S(2)}, u32[]{:S(2)}) %collective-permute-start.1) | collective-permute-done | bytes 188448 | tf_op jit(solution)/shard_map/cond/branch_1_fun/ppermute | solution.py:211
  41.7 2.2 %pad_maximum_fusion.2 = bf16[4,23,2,8,256]{4,3,2,1,0:T(8,128)(2,1)} fusion(bf16[1,23,2,8,256]{4,3,2,1,0:T(8,128)(2,1)} %get-tuple-element.76, bf16[1,23,2,8,256]{4,3,2,1,0:T(8,128)(2,1)} %get-tuple-element.75, bf16[1,23,2,8,256]{4,3,2,1,0:T(8,128)(2,1)} %get-tuple-element.74, bf16[1,23,2,8,256]{4,3,2,1,0:T(8,128)(2,1)} %get-tuple-element.110), kind=kLoop, calls=%fused_computation.8 | loop fusion | flops 1130496 | bytes 1507328 | tf_op jit(solution)/shard_map/stack | solution.py:220
  43.9 0.0 collective-permute-done.8
  43.9 7.1 %collective-permute-start.12 = (bf16[4,23,2,8,256]{4,3,2,1,0:T(8,128)(2,1)}, bf16[4,23,2,8,256]{4,3,2,1,0:T(8,128)(2,1)S(1)}, u32[]{:S(2)}, u32[]{:S(2)}) collective-permute-start(bf16[4,23,2,8,256]{4,3,2,1,0:T(8,128)(2,1)} %pad_maximum_fusion.2), channel_id=1, source_target_pairs={{0,448},{32,480},{64,0},{96,32},{128,64},{160,96},{192,128},{224,1... | collective-permute-start | bytes 2261000 | tf_op jit(solution)/shard_map/ppermute | solution.py:236
  51.0 55.4 %conditional.3 = (bf16[2,23,2,8,256]{4,3,2,1,0:T(8,128)(2,1)}, bf16[2,23,2,8,256]{4,3,2,1,0:T(8,128)(2,1)}, bf16[2,23,2,8,256]{4,3,2,1,0:T(8,128)(2,1)}, bf16[23...) conditional(s32[]{:T(128)} %convert_element_type.4, () %tuple.40, ...), branch_computations={%region_2.3_spmd, %region_3.4_spmd} | conditional | flops 566249 | bytes 21857754 | solution.py:246
  51.1 1.3 %slice_select_fusion = (bf16[1,23,2,8,256]{4,3,2,1,0:T(8,128)(2,1)S(1)}, bf16[1,23,2,8,256]{4,3,2,1,0:T(8,128)(2,1)S(1)}, bf16[1,23,2,8,256]{4,3,2,1,0:T(8,128)(2,1)S(1)}) fusion(bf16[8,23,2,8,256]{4,3,2,1,0:T(8,128)(2,1)} %get-tuple-element.53, pred[]{:T(512)S(6)} %eq.14), kind=kLoop, calls=%fused_computation.6 | loop fusion | flops 188416 | bytes 1507329 | tf_op jit(solution)/shard_map/cond/branch_1_fun/jit(_where)/select_n | solution.py:189
  52.4 2.2 %collective-permute-start.6 = (bf16[2,23,2,8,256]{4,3,2,1,0:T(8,128)(2,1)S(1)}, bf16[2,23,2,8,256]{4,3,2,1,0:T(8,128)(2,1)S(1)}, u32[]{:S(2)}, u32[]{:S(2)}) collective-permute-start(bf16[2,23,2,8,256]{4,3,2,1,0:T(8,128)(2,1)S(1)} %pad_maximum_fusion), channel_id=1, source_target_pairs={{0,384},{32,416},{64,448},{96,480},{128,0},{160,32},{192,64},{224,... | collective-permute-start | bytes 1130504 | tf_op jit(solution)/shard_map/cond/branch_1_fun/ppermute | solution.py:239
  54.6 1.8 %branch_1_fun.1 = (bf16[2,23,2,8,256]{4,3,2,1,0:T(8,128)(2,1)S(1)}, bf16[2,23,2,8,256]{4,3,2,1,0:T(8,128)(2,1)S(1)}, bf16[2,23,2,8,256]{4,3,2,1,0:T(8,128)(2,1)S(1)}, bf16[23,2,8,256]{3,2,1,0:T(8,128)(2,1)}) custom-call(s32[1,1]{1,0:T(1,128)} %bitcast.6.place_ref, bf16[8,23,2,8,256]{4,3,2,1,0:T(8,128)(2,1)S(1)} %bitcast.36, ...), custom_call_target="tpu_custom_call" | custom-call | flops 1000 | bytes 1000 | tf_op jit(solution)/shard_map/cond/branch_1_fun/pallas_call | solution.py:159
  56.4 3.8 %collective-permute-start.3 = (bf16[2,23,2,8,256]{4,3,2,1,0:T(8,128)(2,1)S(1)}, bf16[2,23,2,8,256]{4,3,2,1,0:T(8,128)(2,1)S(1)}, u32[]{:S(2)}, u32[]{:S(2)}) collective-permute-start(bf16[2,23,2,8,256]{4,3,2,1,0:T(8,128)(2,1)S(1)} %get-tuple-element.49), channel_id=1, source_target_pairs={{0,3},{1,0},{2,1},{3,2},{4,7},{5,4},{6,5},{7,6},{8,11},{9,8},{10,9... | collective-permute-start | bytes 1130504 | tf_op jit(solution)/shard_map/cond/branch_1_fun/ppermute | solution.py:241
  60.2 1.9 %collective-permute-start.4 = (bf16[2,23,2,8,256]{4,3,2,1,0:T(8,128)(2,1)S(1)}, bf16[2,23,2,8,256]{4,3,2,1,0:T(8,128)(2,1)S(1)}, u32[]{:S(2)}, u32[]{:S(2)}) collective-permute-start(bf16[2,23,2,8,256]{4,3,2,1,0:T(8,128)(2,1)S(1)} %get-tuple-element.50), channel_id=1, source_target_pairs={{0,2},{1,3},{2,0},{3,1},{4,6},{5,7},{6,4},{7,5},{8,10},{9,11},{10,... | collective-permute-start | bytes 1130504 | tf_op jit(solution)/shard_map/cond/branch_1_fun/ppermute | solution.py:241
  62.2 3.8 %collective-permute-start.5 = (bf16[2,23,2,8,256]{4,3,2,1,0:T(8,128)(2,1)S(1)}, bf16[2,23,2,8,256]{4,3,2,1,0:T(8,128)(2,1)}, u32[]{:S(2)}, u32[]{:S(2)}) collective-permute-start(bf16[2,23,2,8,256]{4,3,2,1,0:T(8,128)(2,1)S(1)} %get-tuple-element.51), channel_id=1, source_target_pairs={{0,1},{1,2},{2,3},{3,0},{4,5},{5,6},{6,7},{7,4},{8,9},{9,10},{10,1... | collective-permute-start | bytes 1130504 | tf_op jit(solution)/shard_map/cond/branch_1_fun/ppermute | solution.py:241
  66.0 0.0 collective-permute-done.6
  66.0 0.7 fusion.4
  66.7 24.1 %collective-permute-start.7 = (bf16[2,23,2,8,256]{4,3,2,1,0:T(8,128)(2,1)S(1)}, bf16[2,23,2,8,256]{4,3,2,1,0:T(8,128)(2,1)}, u32[]{:S(2)}, u32[]{:S(2)}) collective-permute-start(bf16[2,23,2,8,256]{4,3,2,1,0:T(8,128)(2,1)S(1)} %pad_maximum_fusion.1), channel_id=1, source_target_pairs={{0,416},{32,0},{64,480},{96,64},{128,32},{160,128},{192,96},{224,1... | collective-permute-start | bytes 1130504 | tf_op jit(solution)/shard_map/cond/branch_1_fun/ppermute | solution.py:243
  90.8 0.0 collective-permute-done.3
  90.9 0.7 copy.39
  91.6 0.7 copy.40
  92.3 0.0 collective-permute-done.4
  92.3 0.8 fusion.2
  93.1 1.6 %copy.43 = bf16[23,2,8,256]{3,2,1,0:T(8,128)(2,1)} copy(bf16[23,2,8,256]{3,2,1,0:T(8,128)(2,1)} %bitcast.11) | data formatting | bytes 376832 | tf_op jit(solution)/shard_map/cond
  94.7 1.6 %copy.44 = bf16[23,2,8,256]{3,2,1,0:T(8,128)(2,1)} copy(bf16[23,2,8,256]{3,2,1,0:T(8,128)(2,1)} %bitcast.12) | data formatting | bytes 376832 | tf_op jit(solution)/shard_map/cond
  96.3 0.0 collective-permute-done.5
  96.3 1.8 %fusion.1 = (bf16[1,23,2,8,256]{4,3,2,1,0:T(8,128)(2,1)}, bf16[1,23,2,8,256]{4,3,2,1,0:T(8,128)(2,1)}) fusion(bf16[2,23,2,8,256]{4,3,2,1,0:T(8,128)(2,1)} %collective-permute-done.5), kind=kLoop, calls=%fused_computation.24 | loop fusion | bytes 753664 | tf_op jit(solution)/shard_map/slice | solution.py:249
  98.1 1.6 %copy.47 = bf16[23,2,8,256]{3,2,1,0:T(8,128)(2,1)} copy(bf16[23,2,8,256]{3,2,1,0:T(8,128)(2,1)} %bitcast.13) | data formatting | bytes 376832 | tf_op jit(solution)/shard_map/cond
  99.7 1.6 %copy.48 = bf16[23,2,8,256]{3,2,1,0:T(8,128)(2,1)} copy(bf16[23,2,8,256]{3,2,1,0:T(8,128)(2,1)} %bitcast.14) | data formatting | bytes 376832 | tf_op jit(solution)/shard_map/cond
  101.4 1.8 %fusion = (bf16[1,23,2,8,256]{4,3,2,1,0:T(8,128)(2,1)}, bf16[1,23,2,8,256]{4,3,2,1,0:T(8,128)(2,1)}) fusion(bf16[2,23,2,8,256]{4,3,2,1,0:T(8,128)(2,1)} %collective-permute-done.7), kind=kLoop, calls=%fused_computation.23 | loop fusion | bytes 753664 | tf_op jit(solution)/shard_map/slice | solution.py:252
  103.2 1.6 %copy.51 = bf16[23,2,8,256]{3,2,1,0:T(8,128)(2,1)} copy(bf16[23,2,8,256]{3,2,1,0:T(8,128)(2,1)} %bitcast.15) | data formatting | bytes 376832 | tf_op jit(solution)/shard_map/cond
  104.8 1.6 %copy.52 = bf16[23,2,8,256]{3,2,1,0:T(8,128)(2,1)} copy(bf16[23,2,8,256]{3,2,1,0:T(8,128)(2,1)} %bitcast.16) | data formatting | bytes 376832 | tf_op jit(solution)/shard_map/cond
  106.4 1.1 broadcast_select_fusion.3
  107.5 1.2 broadcast_select_fusion.2
  108.7 4.8 %shard_map.28 = (f32[8,512,256]{2,1,0:T(8,128)S(1)}, bf16[8,512,184]{2,1,0:T(8,128)(2,1)S(1)}) custom-call(bf16[23,2,8,256]{3,2,1,0:T(8,128)(2,1)S(1)} %get-tuple-element.111.refs_0_, bf16[23,2,8,256]{3,2,1,0:T(8,128)(2,1)S(1)} %copy-done.3, bf16[23,2,8,256]{3,2,1,0:T(8,128)(2,1)S(1)} %get-tuple-element.118.refs_2_, ...), custom_call_target="tpu_custom_call" | custom-call | flops 1000000 | bytes 1000000 | tf_op jit(solution)/shard_map/pallas_call | solution.py:95
  113.5 7.9 %collective-permute-done.12.refs_0_ = bf16[4,23,2,8,256]{4,3,2,1,0:T(8,128)(2,1)S(1)} collective-permute-done((bf16[4,23,2,8,256]{4,3,2,1,0:T(8,128)(2,1)}, bf16[4,23,2,8,256]{4,3,2,1,0:T(8,128)(2,1)S(1)}, u32[]{:S(2)}, u32[]{:S(2)}) %collective-permute-start.12) | collective-permute-done | bytes 753696 | tf_op jit(solution)/shard_map/ppermute | solution.py:236
  121.4 2.4 %shard_map.29 = bf16[2,8,256,256]{3,2,1,0:T(8,128)(2,1)} custom-call(bf16[4,23,2,8,256]{4,3,2,1,0:T(8,128)(2,1)S(1)} %collective-permute-done.12.refs_0_, f32[8,512,256]{2,1,0:T(8,128)S(1)} %get-tuple-element.91.refs_1_, bf16[8,512,184]{2,1,0:T(8,128)(2,1)S(1)} %get-tuple-element.92.refs_2_), custom_call_target="tpu_custom_call" | custom-call | flops 200000000 | bytes 9000000 | tf_op jit(solution)/shard_map/pallas_call | solution.py:117
  (21 shorter events, 0.1 us)
Async XLA Ops:
  0.0 3.2 %copy-start = (bf16[1,8,23,2,8,256]{5,4,3,2,1,0:T(8,128)(2,1)S(1)}, bf16[1,8,23,2,8,256]{5,4,3,2,1,0:T(8,128)(2,1)}, u32[]{:S(2)}) copy-start(bf16[1,8,23,2,8,256]{5,4,3,2,1,0:T(8,128)(2,1)} %param.6) | copy-start | bytes 4521988
  1.3 42.6 %collective-permute-start.8 = (bf16[4,23,2,8,256]{4,3,2,1,0:T(8,128)(2,1)S(1)}, bf16[4,23,2,8,256]{4,3,2,1,0:T(8,128)(2,1)S(1)}, u32[]{:S(2)}, u32[]{:S(2)}) collective-permute-start(bf16[4,23,2,8,256]{4,3,2,1,0:T(8,128)(2,1)S(1)} %dynamic-slice_bitcast_fusion), channel_id=1, source_target_pairs={{0,28},{1,29},{2,30},{3,31},{4,0},{5,1},{6,2},{7,3},{8,4},{9,5},{1... | collective-permute-start | bytes 2261000 | tf_op jit(solution)/shard_map/ppermute | solution.py:236
  3.3 9.0 %collective-permute-start.10 = (bf16[23,2,8,256]{3,2,1,0:T(8,128)(2,1)S(1)}, bf16[23,2,8,256]{3,2,1,0:T(8,128)(2,1)}, u32[]{:S(2)}, u32[]{:S(2)}) collective-permute-start(bf16[23,2,8,256]{3,2,1,0:T(8,128)(2,1)S(1)} %get-tuple-element.113), channel_id=1, source_target_pairs={{0,2},{2,3},{4,6},{6,7},{8,10},{10,11},{12,14},{14,15},{16,18},{18... | collective-permute-start | bytes 565256 | tf_op jit(solution)/shard_map/ppermute | solution.py:236
  7.0 36.9 %collective-permute-start.9 = (bf16[2,23,2,8,256]{4,3,2,1,0:T(8,128)(2,1)}, bf16[2,23,2,8,256]{4,3,2,1,0:T(8,128)(2,1)}, u32[]{:S(2)}, u32[]{:S(2)}) collective-permute-start(bf16[2,23,2,8,256]{4,3,2,1,0:T(8,128)(2,1)} %pad_maximum_fusion.3), channel_id=1, source_target_pairs={{0,24},{1,25},{4,28},{5,29},{8,0},{9,1},{12,4},{13,5},{16,8},{17,9... | collective-permute-start | bytes 1130504 | tf_op jit(solution)/shard_map/ppermute | solution.py:236
  12.3 31.6 %collective-permute-start.11 = (bf16[23,2,8,256]{3,2,1,0:T(8,128)(2,1)}, bf16[23,2,8,256]{3,2,1,0:T(8,128)(2,1)}, u32[]{:S(2)}, u32[]{:S(2)}) collective-permute-start(bf16[23,2,8,256]{3,2,1,0:T(8,128)(2,1)} %collective-permute-done.10), channel_id=1, source_target_pairs={{2,26},{3,27},{6,30},{7,31},{10,2},{11,3},{14,6},{15,7},{18,10},{1... | collective-permute-start | bytes 565256 | tf_op jit(solution)/shard_map/ppermute | solution.py:236
  27.3 7.6 %collective-permute-start = (bf16[23,2,8,256]{3,2,1,0:T(8,128)(2,1)S(1)}, bf16[23,2,8,256]{3,2,1,0:T(8,128)(2,1)}, u32[]{:S(2)}, u32[]{:S(2)}) collective-permute-start(bf16[23,2,8,256]{3,2,1,0:T(8,128)(2,1)S(1)} %get-tuple-element.94), channel_id=1, source_target_pairs={{0,384},{32,416},{64,448},{96,480},{128,0},{160,32},{192,64},{224,... | collective-permute-start | bytes 565256 | tf_op jit(solution)/shard_map/cond/branch_1_fun/ppermute | solution.py:210
  29.8 11.9 %collective-permute-start.1 = (bf16[23,2,8,256]{3,2,1,0:T(8,128)(2,1)S(1)}, bf16[23,2,8,256]{3,2,1,0:T(8,128)(2,1)}, u32[]{:S(2)}, u32[]{:S(2)}) collective-permute-start(bf16[23,2,8,256]{3,2,1,0:T(8,128)(2,1)S(1)} %get-tuple-element.93), channel_id=1, source_target_pairs={{0,416},{32,384},{64,480},{96,448},{128,32},{160,0},{192,96},{224,... | collective-permute-start | bytes 565256 | tf_op jit(solution)/shard_map/cond/branch_1_fun/ppermute | solution.py:211
  35.0 6.7 %collective-permute-start.2 = (bf16[23,2,8,256]{3,2,1,0:T(8,128)(2,1)S(1)}, bf16[23,2,8,256]{3,2,1,0:T(8,128)(2,1)}, u32[]{:S(2)}, u32[]{:S(2)}) collective-permute-start(bf16[23,2,8,256]{3,2,1,0:T(8,128)(2,1)S(1)} %get-tuple-element.44), channel_id=1, source_target_pairs={{0,32},{32,0},{64,96},{96,64},{128,160},{160,128},{192,224},{224,1... | collective-permute-start | bytes 565256 | tf_op jit(solution)/shard_map/cond/branch_1_fun/ppermute | solution.py:213
  43.9 77.5 %collective-permute-start.12 = (bf16[4,23,2,8,256]{4,3,2,1,0:T(8,128)(2,1)}, bf16[4,23,2,8,256]{4,3,2,1,0:T(8,128)(2,1)S(1)}, u32[]{:S(2)}, u32[]{:S(2)}) collective-permute-start(bf16[4,23,2,8,256]{4,3,2,1,0:T(8,128)(2,1)} %pad_maximum_fusion.2), channel_id=1, source_target_pairs={{0,448},{32,480},{64,0},{96,32},{128,64},{160,96},{192,128},{224,1... | collective-permute-start | bytes 2261000 | tf_op jit(solution)/shard_map/ppermute | solution.py:236
  52.4 13.5 %collective-permute-start.6 = (bf16[2,23,2,8,256]{4,3,2,1,0:T(8,128)(2,1)S(1)}, bf16[2,23,2,8,256]{4,3,2,1,0:T(8,128)(2,1)S(1)}, u32[]{:S(2)}, u32[]{:S(2)}) collective-permute-start(bf16[2,23,2,8,256]{4,3,2,1,0:T(8,128)(2,1)S(1)} %pad_maximum_fusion), channel_id=1, source_target_pairs={{0,384},{32,416},{64,448},{96,480},{128,0},{160,32},{192,64},{224,... | collective-permute-start | bytes 1130504 | tf_op jit(solution)/shard_map/cond/branch_1_fun/ppermute | solution.py:239
  56.4 34.4 %collective-permute-start.3 = (bf16[2,23,2,8,256]{4,3,2,1,0:T(8,128)(2,1)S(1)}, bf16[2,23,2,8,256]{4,3,2,1,0:T(8,128)(2,1)S(1)}, u32[]{:S(2)}, u32[]{:S(2)}) collective-permute-start(bf16[2,23,2,8,256]{4,3,2,1,0:T(8,128)(2,1)S(1)} %get-tuple-element.49), channel_id=1, source_target_pairs={{0,3},{1,0},{2,1},{3,2},{4,7},{5,4},{6,5},{7,6},{8,11},{9,8},{10,9... | collective-permute-start | bytes 1130504 | tf_op jit(solution)/shard_map/cond/branch_1_fun/ppermute | solution.py:241
  60.2 32.0 %collective-permute-start.4 = (bf16[2,23,2,8,256]{4,3,2,1,0:T(8,128)(2,1)S(1)}, bf16[2,23,2,8,256]{4,3,2,1,0:T(8,128)(2,1)S(1)}, u32[]{:S(2)}, u32[]{:S(2)}) collective-permute-start(bf16[2,23,2,8,256]{4,3,2,1,0:T(8,128)(2,1)S(1)} %get-tuple-element.50), channel_id=1, source_target_pairs={{0,2},{1,3},{2,0},{3,1},{4,6},{5,7},{6,4},{7,5},{8,10},{9,11},{10,... | collective-permute-start | bytes 1130504 | tf_op jit(solution)/shard_map/cond/branch_1_fun/ppermute | solution.py:241
  62.2 34.2 %collective-permute-start.5 = (bf16[2,23,2,8,256]{4,3,2,1,0:T(8,128)(2,1)S(1)}, bf16[2,23,2,8,256]{4,3,2,1,0:T(8,128)(2,1)}, u32[]{:S(2)}, u32[]{:S(2)}) collective-permute-start(bf16[2,23,2,8,256]{4,3,2,1,0:T(8,128)(2,1)S(1)} %get-tuple-element.51), channel_id=1, source_target_pairs={{0,1},{1,2},{2,3},{3,0},{4,5},{5,6},{6,7},{7,4},{8,9},{9,10},{10,1... | collective-permute-start | bytes 1130504 | tf_op jit(solution)/shard_map/cond/branch_1_fun/ppermute | solution.py:241
  66.7 34.6 %collective-permute-start.7 = (bf16[2,23,2,8,256]{4,3,2,1,0:T(8,128)(2,1)S(1)}, bf16[2,23,2,8,256]{4,3,2,1,0:T(8,128)(2,1)}, u32[]{:S(2)}, u32[]{:S(2)}) collective-permute-start(bf16[2,23,2,8,256]{4,3,2,1,0:T(8,128)(2,1)S(1)} %pad_maximum_fusion.1), channel_id=1, source_target_pairs={{0,416},{32,0},{64,480},{96,64},{128,32},{160,128},{192,96},{224,1... | collective-permute-start | bytes 1130504 | tf_op jit(solution)/shard_map/cond/branch_1_fun/ppermute | solution.py:243
  90.8 5.5 %copy-start.1 = (bf16[2,23,2,8,256]{4,3,2,1,0:T(8,128)(2,1)}, bf16[2,23,2,8,256]{4,3,2,1,0:T(8,128)(2,1)S(1)}, u32[]{:S(2)}) copy-start(bf16[2,23,2,8,256]{4,3,2,1,0:T(8,128)(2,1)S(1)} %collective-permute-done.3) | copy-start | bytes 1130500 | tf_op jit(solution)/shard_map/cond
  90.8 7.3 %copy-start.5 = (bf16[1,23,2,8,256]{4,3,2,1,0:T(8,128)(2,1)}, bf16[1,23,2,8,256]{4,3,2,1,0:T(8,128)(2,1)S(1)}, u32[]{:S(2)}) copy-start(bf16[1,23,2,8,256]{4,3,2,1,0:T(8,128)(2,1)S(1)} %get-tuple-element.154) | copy-start | bytes 565252 | tf_op jit(solution)/shard_map/cond
  90.8 7.3 %copy-start.6 = (bf16[1,23,2,8,256]{4,3,2,1,0:T(8,128)(2,1)}, bf16[1,23,2,8,256]{4,3,2,1,0:T(8,128)(2,1)S(1)}, u32[]{:S(2)}) copy-start(bf16[1,23,2,8,256]{4,3,2,1,0:T(8,128)(2,1)S(1)} %get-tuple-element.155) | copy-start | bytes 565252 | tf_op jit(solution)/shard_map/cond
  92.3 9.1 %copy-start.2 = (bf16[2,23,2,8,256]{4,3,2,1,0:T(8,128)(2,1)}, bf16[2,23,2,8,256]{4,3,2,1,0:T(8,128)(2,1)S(1)}, u32[]{:S(2)}) copy-start(bf16[2,23,2,8,256]{4,3,2,1,0:T(8,128)(2,1)S(1)} %collective-permute-done.4) | copy-start | bytes 1130500 | tf_op jit(solution)/shard_map/cond
  106.4 2.3 %copy-start.3 = (bf16[23,2,8,256]{3,2,1,0:T(8,128)(2,1)S(1)}, bf16[23,2,8,256]{3,2,1,0:T(8,128)(2,1)}, u32[]{:S(2)}) copy-start(bf16[23,2,8,256]{3,2,1,0:T(8,128)(2,1)} %get-tuple-element.80.refs_1_) | copy-start | bytes 565252
  106.4 2.3 %copy-start.4 = (bf16[23,2,8,256]{3,2,1,0:T(8,128)(2,1)S(1)}, bf16[23,2,8,256]{3,2,1,0:T(8,128)(2,1)}, u32[]{:S(2)}) copy-start(bf16[23,2,8,256]{3,2,1,0:T(8,128)(2,1)} %get-tuple-element.88.refs_9_) | copy-start | bytes 565252

commit v5 on v4

--- a/solution.py
+++ b/solution.py
@@ -166,6 +166,28 @@
     )(place.astype(jnp.int32).reshape(1, 1), source, z, p)
 
 
+def first_kernel(place_ref, source, z, p, w):
+    place = place_ref[0, 0]
+    for k in range(4):
+        z[k] = source[1 + place + k]
+    p[0] = source[jnp.minimum(5 + place, 6)]
+    p[1] = source[7]
+    w[...] = source[jnp.minimum(6 + place, 7)]
+
+
+def first_blocks(place, source):
+    shape = lambda *n: jax.ShapeDtypeStruct(n + source.shape[1:], source.dtype)
+    vmem = pl.BlockSpec(memory_space=pltpu.VMEM)
+    return pl.pallas_call(
+        first_kernel,
+        out_shape=(shape(4), shape(2), shape()),
+        in_specs=[pl.BlockSpec(memory_space=pltpu.SMEM), vmem],
+        out_specs=(vmem,) * 3,
+        compiler_params=pltpu.CompilerParams(vmem_limit_bytes=24 * 2**20),
+        cost_estimate=pl.CostEstimate(flops=0, bytes_accessed=3_000_000, transcendentals=0),
+    )(place.astype(jnp.int32).reshape(1, 1), source)
+
+
 PLAN = (
     ("send", "W"),
     ("send", "Q"),
@@ -216,11 +238,12 @@
     x6, d, cl = lax.cond(core < 2, one_x_step, nothing_like((), (), ()), receiver)
     across_y = [(i, i // 4 * 4 + {0: 2, 2: 3}[i % 4]) for i in range(32) if i % 2 == 0]
 
+    first_z, first_p, first_w = first_blocks(place, source)
     moves = {
         "F": ("src", back(lambda i: 2), lambda: jnp.stack([receiver[2], x6, cl, d])),
-        "Z": ("rcv", back_z(1), lambda: lax.dynamic_slice_in_dim(source, 1 + place, 4, 0)),
-        "P": ("rcv", back_z(2, (0, 1)), lambda: jnp.stack([jnp.where(place == 0, source[5], source[6]), source[7]])),
-        "W": ("rcv", across_y, lambda: jnp.where(place == 0, source[6], source[7])),
+        "Z": ("rcv", back_z(1), lambda: first_z),
+        "P": ("rcv", back_z(2, (0, 1)), lambda: first_p),
+        "W": ("rcv", across_y, lambda: first_w),
         "Q": ("rcv", back_z(2, (2, 3)), lambda: got["W"]),
     }
     tied = []

time: 125 us -> 124 us (level)
  waiting for transfers between devices: 14 us -> 16.7 us
  local copies, waits for them, and re-layouts: 19.3 us -> 17.3 us
    ppermute x5, waiting for transfers between devices: 11.8 us -> 14.5 us  [body(): got[name] = lax.ppermute(block, axis, route)]
    pallas_call x0 -> x1, Pallas kernels: none -> 1.47 us  [first_blocks(): pl.pallas_call(first_kernel, out_shape=(shape(4), shape(2), shape()), in_...]
    dynamic_slice x1 -> x0, local copies, waits for them, and re-layouts: 1.29 us -> none  [body(): lax.dynamic_slice_in_dim(source, 1 + place, 4, 0)]
    cond x16 -> x12, local copies, waits for them, and re-layouts: 11.1 us -> 10.2 us
  transfers between devices with their start and end apart: 13 -> 13, of which waited for: 4 -> 4; matrix products, arithmetic and copies ran while one was open for 21% -> 19% of each run, Pallas kernels for 5% -> 4%
where the time goes in v5:
time: 124 us; the launch traced here: 123 us
  starting transfers between devices  73.2 us (59%)
  local copies, waits for them, and re-layouts  17.3 us (14%)
  waiting for transfers between devices  16.7 us (13%)
  Pallas kernels  8.79 us (7%)
  other arithmetic  7.04 us (6%)
    ppermute x5, starting transfers between devices, body(): got[name] = lax.ppermute(block, axis, route)  24.7 us
    ppermute x1, starting transfers between devices, along_y(): near = lax.ppermute(near, 'src', back(lambda i: 3 - 2 * (i % 2)))  24 us
    ppermute x5, waiting for transfers between devices, body(): got[name] = lax.ppermute(block, axis, route)  14.5 us
    ppermute x3, starting transfers between devices, along_y(): lax.ppermute(x, 'rcv', back_y(b))  10.2 us
    cond x12, local copies, waits for them, and re-layouts  10.2 us
    ppermute x1, starting transfers between devices, one_x_step(): cl = lax.ppermute(first, 'src', [(i, i ^ 1) for i in range(16)])  5.19 us
    select_n x4, other arithmetic, of_core(): return jnp.where(core == 0, zero, one)  4.89 us
    ppermute x1, starting transfers between devices, one_x_step(): lax.ppermute(high(True), 'src', [(i, (i - 4) % 16 ^ 1) for i in range(16)])  4.47 us
  transfers between devices with their start and end apart: 13, of which 4 were waited for; matrix products, arithmetic and copies ran while one was open for 19% of the time, Pallas kernels for 4%

profile of v5, /device:TPU:87, one launch (start us, length us, event | category | flops | bytes accessed | tf_op | source)
XLA Modules:
  0.0 123.2 jit_solution(15952418326878438127)
XLA Ops:
  0.0 1.5 %shard_map.28 = (bf16[4,23,2,8,256]{4,3,2,1,0:T(8,128)(2,1)S(1)}, bf16[2,23,2,8,256]{4,3,2,1,0:T(8,128)(2,1)S(1)}, bf16[23,2,8,256]{3,2,1,0:T(8,128)(2,1)S(1)}) custom-call(s32[1,1]{1,0:T(1,128)} %bitcast.18.place_ref, bf16[8,23,2,8,256]{4,3,2,1,0:T(8,128)(2,1)} %bitcast.29), custom_call_target="tpu_custom_call" | custom-call | bytes 3000000 | tf_op jit(solution)/shard_map/pallas_call | solution.py:181
  1.5 1.9 %collective-permute-start.8 = (bf16[4,23,2,8,256]{4,3,2,1,0:T(8,128)(2,1)S(1)}, bf16[4,23,2,8,256]{4,3,2,1,0:T(8,128)(2,1)}, u32[]{:S(2)}, u32[]{:S(2)}) collective-permute-start(bf16[4,23,2,8,256]{4,3,2,1,0:T(8,128)(2,1)S(1)} %get-tuple-element.79), channel_id=1, source_target_pairs={{0,28},{1,29},{2,30},{3,31},{4,0},{5,1},{6,2},{7,3},{8,4},{9,5},{1... | collective-permute-start | bytes 2261000 | tf_op jit(solution)/shard_map/ppermute | solution.py:259
  3.4 2.9 %collective-permute-start.10 = (bf16[23,2,8,256]{3,2,1,0:T(8,128)(2,1)S(1)}, bf16[23,2,8,256]{3,2,1,0:T(8,128)(2,1)}, u32[]{:S(2)}, u32[]{:S(2)}) collective-permute-start(bf16[23,2,8,256]{3,2,1,0:T(8,128)(2,1)S(1)} %get-tuple-element.81), channel_id=1, source_target_pairs={{0,2},{2,3},{4,6},{6,7},{8,10},{10,11},{12,14},{14,15},{16,18},{18... | collective-permute-start | bytes 565256 | tf_op jit(solution)/shard_map/ppermute | solution.py:259
  6.3 0.7 collective-permute-start.9
  7.0 5.4 %collective-permute-done.10 = bf16[23,2,8,256]{3,2,1,0:T(8,128)(2,1)} collective-permute-done((bf16[23,2,8,256]{3,2,1,0:T(8,128)(2,1)S(1)}, bf16[23,2,8,256]{3,2,1,0:T(8,128)(2,1)}, u32[]{:S(2)}, u32[]{:S(2)}) %collective-permute-start.10) | collective-permute-done | bytes 188448 | tf_op jit(solution)/shard_map/ppermute | solution.py:259
  12.4 12.0 %collective-permute-start.11 = (bf16[23,2,8,256]{3,2,1,0:T(8,128)(2,1)}, bf16[23,2,8,256]{3,2,1,0:T(8,128)(2,1)}, u32[]{:S(2)}, u32[]{:S(2)}) collective-permute-start(bf16[23,2,8,256]{3,2,1,0:T(8,128)(2,1)} %collective-permute-done.10), channel_id=1, source_target_pairs={{2,26},{3,27},{6,30},{7,31},{10,2},{11,3},{14,6},{15,7},{18,10},{1... | collective-permute-start | bytes 565256 | tf_op jit(solution)/shard_map/ppermute | solution.py:259
  24.4 1.0 slice_bitcast_fusion.2
  25.5 0.0 copy-start
  25.5 15.8 %conditional.2 = (bf16[1,23,2,8,256]{4,3,2,1,0:T(8,128)(2,1)}, bf16[1,23,2,8,256]{4,3,2,1,0:T(8,128)(2,1)}, bf16[1,23,2,8,256]{4,3,2,1,0:T(8,128)(2,1)}) conditional(s32[]{:T(128)} %convert_element_type.4, () %tuple.37, (s32[]{:T(128)}, bf16[8,23,2,8,256]{4,3,2,1,0:T(8,128)(2,1)}) %tuple.60), branch_computations={%region_0.1_spmd, %region_1.2_spmd} | conditional | flops 188417 | bytes 3768474 | solution.py:238
  25.5 1.4 %select_bitcast_fusion = (bf16[23,2,8,256]{3,2,1,0:T(8,128)(2,1)S(1)}, bf16[23,2,8,256]{3,2,1,0:T(8,128)(2,1)S(1)}, bf16[23,2,8,256]{3,2,1,0:T(8,128)(2,1)S(1)}) fusion(bf16[8,23,2,8,256]{4,3,2,1,0:T(8,128)(2,1)} %get-tuple-element.41, pred[]{:T(512)S(6)} %eq.12), kind=kLoop, calls=%fused_computation | loop fusion | flops 188416 | bytes 1507329 | tf_op jit(solution)/shard_map/cond/branch_1_fun/jit(_where)/select_n | solution.py:211
  26.9 2.5 %collective-permute-start = (bf16[23,2,8,256]{3,2,1,0:T(8,128)(2,1)S(1)}, bf16[23,2,8,256]{3,2,1,0:T(8,128)(2,1)}, u32[]{:S(2)}, u32[]{:S(2)}) collective-permute-start(bf16[23,2,8,256]{3,2,1,0:T(8,128)(2,1)S(1)} %get-tuple-element.99), channel_id=1, source_target_pairs={{0,384},{32,416},{64,448},{96,480},{128,0},{160,32},{192,64},{224,... | collective-permute-start | bytes 565256 | tf_op jit(solution)/shard_map/cond/branch_1_fun/ppermute | solution.py:232
  29.4 4.5 %collective-permute-start.1 = (bf16[23,2,8,256]{3,2,1,0:T(8,128)(2,1)S(1)}, bf16[23,2,8,256]{3,2,1,0:T(8,128)(2,1)}, u32[]{:S(2)}, u32[]{:S(2)}) collective-permute-start(bf16[23,2,8,256]{3,2,1,0:T(8,128)(2,1)S(1)} %get-tuple-element.98), channel_id=1, source_target_pairs={{0,416},{32,384},{64,480},{96,448},{128,32},{160,0},{192,96},{224,... | collective-permute-start | bytes 565256 | tf_op jit(solution)/shard_map/cond/branch_1_fun/ppermute | solution.py:233
  33.9 0.7 collective-permute-done
  34.6 5.2 %collective-permute-start.2 = (bf16[23,2,8,256]{3,2,1,0:T(8,128)(2,1)S(1)}, bf16[23,2,8,256]{3,2,1,0:T(8,128)(2,1)}, u32[]{:S(2)}, u32[]{:S(2)}) collective-permute-start(bf16[23,2,8,256]{3,2,1,0:T(8,128)(2,1)S(1)} %get-tuple-element.43), channel_id=1, source_target_pairs={{0,32},{32,0},{64,96},{96,64},{128,160},{160,128},{192,224},{224,1... | collective-permute-start | bytes 565256 | tf_op jit(solution)/shard_map/cond/branch_1_fun/ppermute | solution.py:235
  39.8 1.5 %collective-permute-done.1 = bf16[23,2,8,256]{3,2,1,0:T(8,128)(2,1)} collective-permute-done((bf16[23,2,8,256]{3,2,1,0:T(8,128)(2,1)S(1)}, bf16[23,2,8,256]{3,2,1,0:T(8,128)(2,1)}, u32[]{:S(2)}, u32[]{:S(2)}) %collective-permute-start.1) | collective-permute-done | bytes 188448 | tf_op jit(solution)/shard_map/cond/branch_1_fun/ppermute | solution.py:233
  41.3 0.0 collective-permute-done.2
  41.3 2.1 %pad_maximum_fusion.2 = bf16[4,23,2,8,256]{4,3,2,1,0:T(8,128)(2,1)} fusion(bf16[1,23,2,8,256]{4,3,2,1,0:T(8,128)(2,1)} %get-tuple-element.78, bf16[1,23,2,8,256]{4,3,2,1,0:T(8,128)(2,1)} %get-tuple-element.77, bf16[1,23,2,8,256]{4,3,2,1,0:T(8,128)(2,1)} %get-tuple-element.76, bf16[1,23,2,8,256]{4,3,2,1,0:T(8,128)(2,1)S(1)} %get-tuple-element.115), kind=kLoop, calls=%fused_computation.8 | loop fusion | flops 1130496 | bytes 1507328 | tf_op jit(solution)/shard_map/stack | solution.py:243
  43.4 0.0 collective-permute-done.11
  43.4 0.0 collective-permute-done.9
  43.4 0.0 collective-permute-done.8
  43.4 7.1 %collective-permute-start.12 = (bf16[4,23,2,8,256]{4,3,2,1,0:T(8,128)(2,1)}, bf16[4,23,2,8,256]{4,3,2,1,0:T(8,128)(2,1)S(1)}, u32[]{:S(2)}, u32[]{:S(2)}) collective-permute-start(bf16[4,23,2,8,256]{4,3,2,1,0:T(8,128)(2,1)} %pad_maximum_fusion.2), channel_id=1, source_target_pairs={{0,448},{32,480},{64,0},{96,32},{128,64},{160,96},{192,128},{224,1... | collective-permute-start | bytes 2261000 | tf_op jit(solution)/shard_map/ppermute | solution.py:259
  50.6 54.6 %conditional.3 = (bf16[2,23,2,8,256]{4,3,2,1,0:T(8,128)(2,1)}, bf16[2,23,2,8,256]{4,3,2,1,0:T(8,128)(2,1)}, bf16[2,23,2,8,256]{4,3,2,1,0:T(8,128)(2,1)}, bf16[23...) conditional(s32[]{:T(128)} %convert_element_type.4, () %tuple.40, ...), branch_computations={%region_2.3_spmd, %region_3.4_spmd} | conditional | flops 566249 | bytes 20350370 | solution.py:269
  50.6 1.3 %slice_select_fusion = (bf16[1,23,2,8,256]{4,3,2,1,0:T(8,128)(2,1)S(1)}, bf16[1,23,2,8,256]{4,3,2,1,0:T(8,128)(2,1)S(1)}, bf16[1,23,2,8,256]{4,3,2,1,0:T(8,128)(2,1)S(1)}) fusion(bf16[8,23,2,8,256]{4,3,2,1,0:T(8,128)(2,1)} %get-tuple-element.52, pred[]{:T(512)S(6)} %eq.13), kind=kLoop, calls=%fused_computation.6 | loop fusion | flops 188416 | bytes 1507329 | tf_op jit(solution)/shard_map/cond/branch_1_fun/jit(_where)/select_n | solution.py:211
  52.0 2.2 %collective-permute-start.6 = (bf16[2,23,2,8,256]{4,3,2,1,0:T(8,128)(2,1)S(1)}, bf16[2,23,2,8,256]{4,3,2,1,0:T(8,128)(2,1)S(1)}, u32[]{:S(2)}, u32[]{:S(2)}) collective-permute-start(bf16[2,23,2,8,256]{4,3,2,1,0:T(8,128)(2,1)S(1)} %pad_maximum_fusion), channel_id=1, source_target_pairs={{0,384},{32,416},{64,448},{96,480},{128,0},{160,32},{192,64},{224,... | collective-permute-start | bytes 1130504 | tf_op jit(solution)/shard_map/cond/branch_1_fun/ppermute | solution.py:262
  54.1 1.3 %branch_1_fun.1 = (bf16[2,23,2,8,256]{4,3,2,1,0:T(8,128)(2,1)S(1)}, bf16[2,23,2,8,256]{4,3,2,1,0:T(8,128)(2,1)S(1)}, bf16[2,23,2,8,256]{4,3,2,1,0:T(8,128)(2,1)S(1)}, bf16[23,2,8,256]{3,2,1,0:T(8,128)(2,1)S(1)}) custom-call(s32[1,1]{1,0:T(1,128)} %bitcast.6.place_ref, bf16[8,23,2,8,256]{4,3,2,1,0:T(8,128)(2,1)S(1)} %get-tuple-element.45.source, ...), custom_call_target="tpu_custom_call" | custom-call | flops 1000 | bytes 1000 | tf_op jit(solution)/shard_map/cond/branch_1_fun/pallas_call | solution.py:159
  55.4 4.4 %collective-permute-start.3 = (bf16[2,23,2,8,256]{4,3,2,1,0:T(8,128)(2,1)S(1)}, bf16[2,23,2,8,256]{4,3,2,1,0:T(8,128)(2,1)S(1)}, u32[]{:S(2)}, u32[]{:S(2)}) collective-permute-start(bf16[2,23,2,8,256]{4,3,2,1,0:T(8,128)(2,1)S(1)} %get-tuple-element.48), channel_id=1, source_target_pairs={{0,3},{1,0},{2,1},{3,2},{4,7},{5,4},{6,5},{7,6},{8,11},{9,8},{10,9... | collective-permute-start | bytes 1130504 | tf_op jit(solution)/shard_map/cond/branch_1_fun/ppermute | solution.py:264
  59.8 1.9 %collective-permute-start.4 = (bf16[2,23,2,8,256]{4,3,2,1,0:T(8,128)(2,1)S(1)}, bf16[2,23,2,8,256]{4,3,2,1,0:T(8,128)(2,1)S(1)}, u32[]{:S(2)}, u32[]{:S(2)}) collective-permute-start(bf16[2,23,2,8,256]{4,3,2,1,0:T(8,128)(2,1)S(1)} %get-tuple-element.49), channel_id=1, source_target_pairs={{0,2},{1,3},{2,0},{3,1},{4,6},{5,7},{6,4},{7,5},{8,10},{9,11},{10,... | collective-permute-start | bytes 1130504 | tf_op jit(solution)/shard_map/cond/branch_1_fun/ppermute | solution.py:264
  61.8 3.8 %collective-permute-start.5 = (bf16[2,23,2,8,256]{4,3,2,1,0:T(8,128)(2,1)S(1)}, bf16[2,23,2,8,256]{4,3,2,1,0:T(8,128)(2,1)}, u32[]{:S(2)}, u32[]{:S(2)}) collective-permute-start(bf16[2,23,2,8,256]{4,3,2,1,0:T(8,128)(2,1)S(1)} %get-tuple-element.50), channel_id=1, source_target_pairs={{0,1},{1,2},{2,3},{3,0},{4,5},{5,6},{6,7},{7,4},{8,9},{9,10},{10,1... | collective-permute-start | bytes 1130504 | tf_op jit(solution)/shard_map/cond/branch_1_fun/ppermute | solution.py:264
  65.7 24.0 %collective-permute-start.7 = (bf16[2,23,2,8,256]{4,3,2,1,0:T(8,128)(2,1)S(1)}, bf16[2,23,2,8,256]{4,3,2,1,0:T(8,128)(2,1)}, u32[]{:S(2)}, u32[]{:S(2)}) collective-permute-start(bf16[2,23,2,8,256]{4,3,2,1,0:T(8,128)(2,1)S(1)} %pad_maximum_fusion.1), channel_id=1, source_target_pairs={{0,416},{32,0},{64,480},{96,64},{128,32},{160,128},{192,96},{224,1... | collective-permute-start | bytes 1130504 | tf_op jit(solution)/shard_map/cond/branch_1_fun/ppermute | solution.py:266
  89.7 0.8 fusion.3
  90.6 0.9 copy.39
  91.5 1.6 %copy.40 = bf16[23,2,8,256]{3,2,1,0:T(8,128)(2,1)} copy(bf16[23,2,8,256]{3,2,1,0:T(8,128)(2,1)} %bitcast.9) | data formatting | bytes 376832 | tf_op jit(solution)/shard_map/cond
  93.1 0.9 fusion.2
  94.0 0.9 copy.43
  94.9 1.6 %copy.44 = bf16[23,2,8,256]{3,2,1,0:T(8,128)(2,1)} copy(bf16[23,2,8,256]{3,2,1,0:T(8,128)(2,1)} %bitcast.11) | data formatting | bytes 376832 | tf_op jit(solution)/shard_map/cond
  96.5 1.8 %fusion.1 = (bf16[1,23,2,8,256]{4,3,2,1,0:T(8,128)(2,1)}, bf16[1,23,2,8,256]{4,3,2,1,0:T(8,128)(2,1)}) fusion(bf16[2,23,2,8,256]{4,3,2,1,0:T(8,128)(2,1)} %collective-permute-done.5), kind=kLoop, calls=%fused_computation.19 | loop fusion | bytes 753664 | tf_op jit(solution)/shard_map/slice | solution.py:272
  98.3 1.6 %copy.47 = bf16[23,2,8,256]{3,2,1,0:T(8,128)(2,1)} copy(bf16[23,2,8,256]{3,2,1,0:T(8,128)(2,1)} %bitcast.12) | data formatting | bytes 376832 | tf_op jit(solution)/shard_map/cond
  99.9 1.6 %copy.48 = bf16[23,2,8,256]{3,2,1,0:T(8,128)(2,1)} copy(bf16[23,2,8,256]{3,2,1,0:T(8,128)(2,1)} %bitcast.13) | data formatting | bytes 376832 | tf_op jit(solution)/shard_map/cond
  101.5 1.8 %fusion = (bf16[1,23,2,8,256]{4,3,2,1,0:T(8,128)(2,1)}, bf16[1,23,2,8,256]{4,3,2,1,0:T(8,128)(2,1)}) fusion(bf16[2,23,2,8,256]{4,3,2,1,0:T(8,128)(2,1)} %collective-permute-done.7), kind=kLoop, calls=%fused_computation.18 | loop fusion | bytes 753664 | tf_op jit(solution)/shard_map/slice | solution.py:275
  103.3 0.9 copy.51
  104.2 0.9 copy.52
  105.2 0.7 copy-done.3
  105.8 0.1 copy-done.5
  105.9 1.0 broadcast_select_fusion.3
  106.9 1.2 broadcast_select_fusion.2
  108.1 3.7 %shard_map.29 = (f32[8,512,256]{2,1,0:T(8,128)S(1)}, bf16[8,512,184]{2,1,0:T(8,128)(2,1)S(1)}) custom-call(bf16[23,2,8,256]{3,2,1,0:T(8,128)(2,1)S(1)} %slice_bitcast_fusion.3.refs_0_, bf16[23,2,8,256]{3,2,1,0:T(8,128)(2,1)S(1)} %get-tuple-element.85.refs_1_, bf16[23,2,8,256]{3,2,1,0:T(8,128)(2,1)S(1)} %get-tuple-element.119.refs_2_, ...), custom_call_target="tpu_custom_call" | custom-call | flops 1000000 | bytes 1000000 | tf_op jit(solution)/shard_map/pallas_call | solution.py:95
  111.8 9.1 %collective-permute-done.12.refs_0_ = bf16[4,23,2,8,256]{4,3,2,1,0:T(8,128)(2,1)S(1)} collective-permute-done((bf16[4,23,2,8,256]{4,3,2,1,0:T(8,128)(2,1)}, bf16[4,23,2,8,256]{4,3,2,1,0:T(8,128)(2,1)S(1)}, u32[]{:S(2)}, u32[]{:S(2)}) %collective-permute-start.12) | collective-permute-done | bytes 753696 | tf_op jit(solution)/shard_map/ppermute | solution.py:259
  120.9 2.4 %shard_map.30 = bf16[2,8,256,256]{3,2,1,0:T(8,128)(2,1)} custom-call(bf16[4,23,2,8,256]{4,3,2,1,0:T(8,128)(2,1)S(1)} %collective-permute-done.12.refs_0_, f32[8,512,256]{2,1,0:T(8,128)S(1)} %get-tuple-element.96.refs_1_, bf16[8,512,184]{2,1,0:T(8,128)(2,1)S(1)} %get-tuple-element.97.refs_2_), custom_call_target="tpu_custom_call" | custom-call | flops 200000000 | bytes 9000000 | tf_op jit(solution)/shard_map/pallas_call | solution.py:117
  (20 shorter events, 0.1 us)
Async XLA Ops:
  1.5 41.9 %collective-permute-start.8 = (bf16[4,23,2,8,256]{4,3,2,1,0:T(8,128)(2,1)S(1)}, bf16[4,23,2,8,256]{4,3,2,1,0:T(8,128)(2,1)}, u32[]{:S(2)}, u32[]{:S(2)}) collective-permute-start(bf16[4,23,2,8,256]{4,3,2,1,0:T(8,128)(2,1)S(1)} %get-tuple-element.79), channel_id=1, source_target_pairs={{0,28},{1,29},{2,30},{3,31},{4,0},{5,1},{6,2},{7,3},{8,4},{9,5},{1... | collective-permute-start | bytes 2261000 | tf_op jit(solution)/shard_map/ppermute | solution.py:259
  3.4 9.0 %collective-permute-start.10 = (bf16[23,2,8,256]{3,2,1,0:T(8,128)(2,1)S(1)}, bf16[23,2,8,256]{3,2,1,0:T(8,128)(2,1)}, u32[]{:S(2)}, u32[]{:S(2)}) collective-permute-start(bf16[23,2,8,256]{3,2,1,0:T(8,128)(2,1)S(1)} %get-tuple-element.81), channel_id=1, source_target_pairs={{0,2},{2,3},{4,6},{6,7},{8,10},{10,11},{12,14},{14,15},{16,18},{18... | collective-permute-start | bytes 565256 | tf_op jit(solution)/shard_map/ppermute | solution.py:259
  6.3 37.1 %collective-permute-start.9 = (bf16[2,23,2,8,256]{4,3,2,1,0:T(8,128)(2,1)S(1)}, bf16[2,23,2,8,256]{4,3,2,1,0:T(8,128)(2,1)S(1)}, u32[]{:S(2)}, u32[]{:S(2)}) collective-permute-start(bf16[2,23,2,8,256]{4,3,2,1,0:T(8,128)(2,1)S(1)} %get-tuple-element.80), channel_id=1, source_target_pairs={{0,24},{1,25},{4,28},{5,29},{8,0},{9,1},{12,4},{13,5},{16,8},{17,9... | collective-permute-start | bytes 1130504 | tf_op jit(solution)/shard_map/ppermute | solution.py:259
  12.4 31.0 %collective-permute-start.11 = (bf16[23,2,8,256]{3,2,1,0:T(8,128)(2,1)}, bf16[23,2,8,256]{3,2,1,0:T(8,128)(2,1)}, u32[]{:S(2)}, u32[]{:S(2)}) collective-permute-start(bf16[23,2,8,256]{3,2,1,0:T(8,128)(2,1)} %collective-permute-done.10), channel_id=1, source_target_pairs={{2,26},{3,27},{6,30},{7,31},{10,2},{11,3},{14,6},{15,7},{18,10},{1... | collective-permute-start | bytes 565256 | tf_op jit(solution)/shard_map/ppermute | solution.py:259
  25.5 25.1 %copy-start = (bf16[1,8,23,2,8,256]{5,4,3,2,1,0:T(8,128)(2,1)S(1)}, bf16[1,8,23,2,8,256]{5,4,3,2,1,0:T(8,128)(2,1)}, u32[]{:S(2)}) copy-start(bf16[1,8,23,2,8,256]{5,4,3,2,1,0:T(8,128)(2,1)} %param.6) | copy-start | bytes 4521988
  26.9 7.6 %collective-permute-start = (bf16[23,2,8,256]{3,2,1,0:T(8,128)(2,1)S(1)}, bf16[23,2,8,256]{3,2,1,0:T(8,128)(2,1)}, u32[]{:S(2)}, u32[]{:S(2)}) collective-permute-start(bf16[23,2,8,256]{3,2,1,0:T(8,128)(2,1)S(1)} %get-tuple-element.99), channel_id=1, source_target_pairs={{0,384},{32,416},{64,448},{96,480},{128,0},{160,32},{192,64},{224,... | collective-permute-start | bytes 565256 | tf_op jit(solution)/shard_map/cond/branch_1_fun/ppermute | solution.py:232
  29.4 11.9 %collective-permute-start.1 = (bf16[23,2,8,256]{3,2,1,0:T(8,128)(2,1)S(1)}, bf16[23,2,8,256]{3,2,1,0:T(8,128)(2,1)}, u32[]{:S(2)}, u32[]{:S(2)}) collective-permute-start(bf16[23,2,8,256]{3,2,1,0:T(8,128)(2,1)S(1)} %get-tuple-element.98), channel_id=1, source_target_pairs={{0,416},{32,384},{64,480},{96,448},{128,32},{160,0},{192,96},{224,... | collective-permute-start | bytes 565256 | tf_op jit(solution)/shard_map/cond/branch_1_fun/ppermute | solution.py:233
  34.6 6.7 %collective-permute-start.2 = (bf16[23,2,8,256]{3,2,1,0:T(8,128)(2,1)S(1)}, bf16[23,2,8,256]{3,2,1,0:T(8,128)(2,1)}, u32[]{:S(2)}, u32[]{:S(2)}) collective-permute-start(bf16[23,2,8,256]{3,2,1,0:T(8,128)(2,1)S(1)} %get-tuple-element.43), channel_id=1, source_target_pairs={{0,32},{32,0},{64,96},{96,64},{128,160},{160,128},{192,224},{224,1... | collective-permute-start | bytes 565256 | tf_op jit(solution)/shard_map/cond/branch_1_fun/ppermute | solution.py:235
  43.4 77.5 %collective-permute-start.12 = (bf16[4,23,2,8,256]{4,3,2,1,0:T(8,128)(2,1)}, bf16[4,23,2,8,256]{4,3,2,1,0:T(8,128)(2,1)S(1)}, u32[]{:S(2)}, u32[]{:S(2)}) collective-permute-start(bf16[4,23,2,8,256]{4,3,2,1,0:T(8,128)(2,1)} %pad_maximum_fusion.2), channel_id=1, source_target_pairs={{0,448},{32,480},{64,0},{96,32},{128,64},{160,96},{192,128},{224,1... | collective-permute-start | bytes 2261000 | tf_op jit(solution)/shard_map/ppermute | solution.py:259
  52.0 13.7 %collective-permute-start.6 = (bf16[2,23,2,8,256]{4,3,2,1,0:T(8,128)(2,1)S(1)}, bf16[2,23,2,8,256]{4,3,2,1,0:T(8,128)(2,1)S(1)}, u32[]{:S(2)}, u32[]{:S(2)}) collective-permute-start(bf16[2,23,2,8,256]{4,3,2,1,0:T(8,128)(2,1)S(1)} %pad_maximum_fusion), channel_id=1, source_target_pairs={{0,384},{32,416},{64,448},{96,480},{128,0},{160,32},{192,64},{224,... | collective-permute-start | bytes 1130504 | tf_op jit(solution)/shard_map/cond/branch_1_fun/ppermute | solution.py:262
  55.4 34.3 %collective-permute-start.3 = (bf16[2,23,2,8,256]{4,3,2,1,0:T(8,128)(2,1)S(1)}, bf16[2,23,2,8,256]{4,3,2,1,0:T(8,128)(2,1)S(1)}, u32[]{:S(2)}, u32[]{:S(2)}) collective-permute-start(bf16[2,23,2,8,256]{4,3,2,1,0:T(8,128)(2,1)S(1)} %get-tuple-element.48), channel_id=1, source_target_pairs={{0,3},{1,0},{2,1},{3,2},{4,7},{5,4},{6,5},{7,6},{8,11},{9,8},{10,9... | collective-permute-start | bytes 1130504 | tf_op jit(solution)/shard_map/cond/branch_1_fun/ppermute | solution.py:264
  59.8 33.3 %collective-permute-start.4 = (bf16[2,23,2,8,256]{4,3,2,1,0:T(8,128)(2,1)S(1)}, bf16[2,23,2,8,256]{4,3,2,1,0:T(8,128)(2,1)S(1)}, u32[]{:S(2)}, u32[]{:S(2)}) collective-permute-start(bf16[2,23,2,8,256]{4,3,2,1,0:T(8,128)(2,1)S(1)} %get-tuple-element.49), channel_id=1, source_target_pairs={{0,2},{1,3},{2,0},{3,1},{4,6},{5,7},{6,4},{7,5},{8,10},{9,11},{10,... | collective-permute-start | bytes 1130504 | tf_op jit(solution)/shard_map/cond/branch_1_fun/ppermute | solution.py:264
  61.8 34.7 %collective-permute-start.5 = (bf16[2,23,2,8,256]{4,3,2,1,0:T(8,128)(2,1)S(1)}, bf16[2,23,2,8,256]{4,3,2,1,0:T(8,128)(2,1)}, u32[]{:S(2)}, u32[]{:S(2)}) collective-permute-start(bf16[2,23,2,8,256]{4,3,2,1,0:T(8,128)(2,1)S(1)} %get-tuple-element.50), channel_id=1, source_target_pairs={{0,1},{1,2},{2,3},{3,0},{4,5},{5,6},{6,7},{7,4},{8,9},{9,10},{10,1... | collective-permute-start | bytes 1130504 | tf_op jit(solution)/shard_map/cond/branch_1_fun/ppermute | solution.py:264
  65.7 35.8 %collective-permute-start.7 = (bf16[2,23,2,8,256]{4,3,2,1,0:T(8,128)(2,1)S(1)}, bf16[2,23,2,8,256]{4,3,2,1,0:T(8,128)(2,1)}, u32[]{:S(2)}, u32[]{:S(2)}) collective-permute-start(bf16[2,23,2,8,256]{4,3,2,1,0:T(8,128)(2,1)S(1)} %pad_maximum_fusion.1), channel_id=1, source_target_pairs={{0,416},{32,0},{64,480},{96,64},{128,32},{160,128},{192,96},{224,1... | collective-permute-start | bytes 1130504 | tf_op jit(solution)/shard_map/cond/branch_1_fun/ppermute | solution.py:266
  89.7 6.8 %copy-start.1 = (bf16[2,23,2,8,256]{4,3,2,1,0:T(8,128)(2,1)}, bf16[2,23,2,8,256]{4,3,2,1,0:T(8,128)(2,1)S(1)}, u32[]{:S(2)}) copy-start(bf16[2,23,2,8,256]{4,3,2,1,0:T(8,128)(2,1)S(1)} %collective-permute-done.3) | copy-start | bytes 1130500 | tf_op jit(solution)/shard_map/cond
  93.1 8.4 %copy-start.2 = (bf16[2,23,2,8,256]{4,3,2,1,0:T(8,128)(2,1)}, bf16[2,23,2,8,256]{4,3,2,1,0:T(8,128)(2,1)S(1)}, u32[]{:S(2)}) copy-start(bf16[2,23,2,8,256]{4,3,2,1,0:T(8,128)(2,1)S(1)} %collective-permute-done.4) | copy-start | bytes 1130500 | tf_op jit(solution)/shard_map/cond
  105.2 0.7 copy-start.3
  105.2 0.8 copy-start.5
  105.9 2.2 %copy-start.4 = (bf16[23,2,8,256]{3,2,1,0:T(8,128)(2,1)S(1)}, bf16[23,2,8,256]{3,2,1,0:T(8,128)(2,1)}, u32[]{:S(2)}) copy-start(bf16[23,2,8,256]{3,2,1,0:T(8,128)(2,1)} %copy-done.3) | copy-start | bytes 565252
  105.9 2.2 %copy-start.6 = (bf16[23,2,8,256]{3,2,1,0:T(8,128)(2,1)S(1)}, bf16[23,2,8,256]{3,2,1,0:T(8,128)(2,1)}, u32[]{:S(2)}) copy-start(bf16[23,2,8,256]{3,2,1,0:T(8,128)(2,1)} %copy-done.5) | copy-start | bytes 565252
